TPU v7x, 32 devices: a whole 2x2x4 slice. The times are simulated.
32 devices in a mesh: dom: 16 (over z, y, x), sub: 2 (over core).
Axes of the slice: x: 2, y: 2, z: 4, core: 2. Of those that a mesh axis runs over, the one named last changes fastest.
Arguments:
- voltages: float32 [64, 1024], P(None, ('dom', 'sub')), may hold values from -6 to 6
- newton_steps: float32 [2, 64, 1024], P(None, None, ('dom', 'sub')), may hold values from -3 to 3
- cap_diag: float32 [64, 1024], P(None, ('dom', 'sub')), may hold values from 1 to 10
- preconditioner: float32 [64, 64, 1024], P(None, None, ('dom', 'sub')), may hold values from -0.75 to 0.75
- couple_block: int32 [2048], P(('dom', 'sub')), may hold values from 0 to 31
- couple_owner: int32 [2048, 1], P(('dom', 'sub')), may hold values from 0 to 31; in each aligned block of 64 rows (0 to 63, 64 to 127, ...) at most 4 rows name the same one
- couple_offset: int32 [2048], P(('dom', 'sub')), may hold values from 0 to 31
- couple_source: int32 [2048, 768], P(('dom', 'sub')), may hold values from 0 to 63
- couple_target: int32 [2048, 768], P(('dom', 'sub')), may hold values from 0 to 63
- couple_gain: float32 [2048, 768], P(('dom', 'sub')), may hold values from 0.05 to 0.5
- inner_source: int32 [1024, 768], P(('dom', 'sub')), may hold values from 0 to 63
- inner_target: int32 [1024, 768], P(('dom', 'sub')), may hold values from 0 to 63
- inner_gain: float32 [1024, 768], P(('dom', 'sub')), may hold values from 0.05 to 0.5
Outputs:
- preconditioned: float32 [2, 64, 1024], P(None, None, ('dom', 'sub'))
Inputs may be any that keep to these rules, and one draw needn't show every extreme that they name: `couple_owner`: within the 64 stamp blocks of one device no owner is named more than 4 times, a bound that some block reaches.
All inputs are finite; a program needn't handle non-finite values.
Results may differ from a plain program's by a relative error of at most 0.0041.
Values may be sent and summed in bfloat16 or wider, within the bound.
No kernel may reach another device: no remote copies, remote signals or barrier semaphores. Data moves between devices by JAX's collectives and lax.ppermute only.
A program may use at most 64 MiB of HBM per device.

v0:
```python
import math

import jax
import jax.numpy as jnp
from jax import lax
from jax.sharding import PartitionSpec as P

BS = 64
NEWTON = 2


def conductance(gain, first, second):
    drop = first - second
    return (gain / (1.0 + drop * drop)).astype(jnp.bfloat16)


def couple_blocks(source, target, weight):
    row_count = source.shape[0]
    group_size = math.gcd(row_count, 32)
    node_ids = jnp.arange(BS, dtype=jnp.int32)

    def couple_one_group(pieces):
        group_source, group_target, group_weight = pieces
        hot_source = (group_source[..., None] == node_ids).astype(jnp.bfloat16)
        hot_target = (group_target[..., None] == node_ids).astype(jnp.bfloat16) * (-group_weight)[
            ..., None
        ]
        return jnp.einsum(
            "gkj,gki->gji", hot_target, hot_source, preferred_element_type=jnp.float32
        ).astype(jnp.bfloat16)

    shaped = tuple(
        (
            item.reshape(row_count // group_size, group_size, item.shape[1])
            for item in (source, target, weight)
        )
    )
    stacked = lax.map(couple_one_group, shaped)
    return stacked.reshape(row_count, BS, BS)


def inner_images(field, update, capacity, source, target, gain):
    row_count = source.shape[0]
    group_size = math.gcd(row_count, 32)
    node_ids = jnp.arange(BS, dtype=jnp.int32)
    by_block = field.T
    weight = conductance(
        gain,
        jnp.take_along_axis(by_block, source, axis=1),
        jnp.take_along_axis(by_block, target, axis=1),
    )
    identity = jnp.eye(BS, dtype=jnp.float32)

    def inner_one_group(pieces):
        group_source, group_target, group_weight, group_capacity, group_update = pieces
        difference = (group_source[..., None] == node_ids).astype(jnp.bfloat16) - (
            group_target[..., None] == node_ids
        ).astype(jnp.bfloat16)
        weighted = difference * group_weight[..., None]
        matrix = jnp.einsum(
            "gki,gkj->gij", weighted, difference, preferred_element_type=jnp.float32
        )
        matrix = (matrix + group_capacity[:, :, None] * identity[None]).astype(jnp.bfloat16)
        return jnp.einsum("gij,gj->gi", matrix, group_update, preferred_element_type=jnp.float32)

    pieces = (source, target, weight, capacity.T, update.T)
    shaped = tuple(
        (item.reshape((row_count // group_size, group_size) + item.shape[1:]) for item in pieces)
    )
    stacked = lax.map(inner_one_group, shaped)
    return stacked.reshape(row_count, BS).T


def per_device(
    voltages,
    newton_steps,
    cap_diag,
    preconditioner,
    couple_block,
    couple_owner,
    couple_offset,
    couple_source,
    couple_target,
    couple_gain,
    inner_source,
    inner_target,
    inner_gain,
):
    devices_all = lax.axis_size(("dom", "sub"))
    stamp_count = couple_block.shape[0]
    block_count = voltages.shape[1]
    per_owner = max(2, 2 * stamp_count // devices_all)
    slot_total = devices_all * per_owner
    owners = couple_owner[:, 0]
    position = jnp.arange(stamp_count, dtype=jnp.int32)
    earlier = (owners[:, None] == owners[None, :]) & (position[None, :] < position[:, None])
    slot_index = owners * per_owner + jnp.sum(earlier, axis=1, dtype=jnp.int32)
    requests = jnp.full((slot_total,), -1, jnp.int32).at[slot_index].set(couple_offset)
    asked = lax.all_to_all(requests, ("dom", "sub"), split_axis=0, concat_axis=0, tiled=True)
    row_onehot = (asked[:, None] == jnp.arange(block_count, dtype=jnp.int32)[None, :]).astype(
        jnp.float32
    )
    asked_block = jnp.maximum(asked, 0)
    field = voltages
    results = []
    for newton in range(NEWTON):
        update = newton_steps[newton].astype(jnp.bfloat16)
        sent_field = field[:, asked_block]
        remote_field = lax.all_to_all(
            sent_field.astype(jnp.bfloat16), ("dom", "sub"), split_axis=1, concat_axis=1, tiled=True
        ).astype(sent_field.dtype)
        inner_part = inner_images(field, update, cap_diag, inner_source, inner_target, inner_gain)
        by_block = field.T
        local_rows = jnp.take_along_axis(by_block[couple_block], couple_source, axis=1)
        remote_rows = jnp.take_along_axis(remote_field.T[slot_index], couple_target, axis=1)
        couple_weight = conductance(couple_gain, local_rows, remote_rows)
        matrices = couple_blocks(couple_source, couple_target, couple_weight)
        local_update = update.T[couple_block]
        local_images = jnp.einsum(
            "sji,si->sj", matrices, local_update, preferred_element_type=jnp.float32
        )
        image_buffer = jnp.zeros((slot_total, BS), jnp.float32).at[slot_index].set(local_images)
        images = lax.all_to_all(
            image_buffer.astype(jnp.bfloat16),
            ("dom", "sub"),
            split_axis=0,
            concat_axis=0,
            tiled=True,
        ).astype(image_buffer.dtype)
        couple_part = jnp.dot(images.T, row_onehot, precision=lax.Precision.HIGHEST)
        total = inner_part + couple_part
        results.append(
            jnp.einsum("ijr,jr->ir", preconditioner, total, precision=lax.Precision.HIGHEST)
        )
        field = field + newton_steps[newton]
    return jnp.stack(results)


def solution(mesh):
    in_specs = (
        P(None, ("dom", "sub")),
        P(None, None, ("dom", "sub")),
        P(None, ("dom", "sub")),
        P(None, None, ("dom", "sub")),
        P(("dom", "sub")),
        P(("dom", "sub"), None),
        P(("dom", "sub")),
        P(("dom", "sub"), None),
        P(("dom", "sub"), None),
        P(("dom", "sub"), None),
        P(("dom", "sub"), None),
        P(("dom", "sub"), None),
        P(("dom", "sub"), None),
    )
    out_specs = P(None, None, ("dom", "sub"))
    return jax.shard_map(
        per_device, mesh=mesh, in_specs=in_specs, out_specs=out_specs, check_vma=False
    )
```

profile of v0, /device:TPU:0, one launch (start us, length us, event | category | flops | bytes accessed | tf_op | source)
XLA Modules:
  0.0 1964.7 jit_solution(18301053309902909403)
XLA Ops:
  0.0 0.9 convert_reduce_fusion
  0.9 0.7 fusion.119
  1.6 0.9 scatter_custom_fusion
  2.5 0.7 all_to_all.30
  3.2 7.3 all-to-all-start
  10.5 0.9 bitcast_or_fusion.2
  11.5 0.9 bitcast_or_fusion.3
  12.4 157.6 %gather_fusion.9 = f32[24576]{0:T(1024)S(1)} fusion(f32[32,64]{1,0:T(8,128)S(1)} %bitcast.151, s32[24576]{0:T(1024)S(1)} %reshape.341), kind=kCustom, calls=%fused_computation.2.clone | custom fusion | bytes 393216 | tf_op jit(solution)/shard_map/jit(take_along_axis)/gather | solution.py:50
  170.0 157.6 %gather_fusion.8 = f32[24576]{0:T(1024)S(1)} fusion(f32[32,64]{1,0:T(8,128)S(1)} %bitcast.152, s32[24576]{0:T(1024)S(1)} %reshape.336), kind=kCustom, calls=%fused_computation.clone | custom fusion | bytes 393216 | tf_op jit(solution)/shard_map/jit(take_along_axis)/gather | solution.py:49
  327.6 157.6 %gather_fusion.13 = f32[24576]{0:T(1024)S(1)} fusion(f32[32,64]{1,0:T(8,128)S(1)} %bitcast.154, s32[24576]{0:T(1024)S(1)} %reshape.341), kind=kCustom, calls=%fused_computation.4.clone | custom fusion | bytes 393216 | tf_op jit(solution)/shard_map/jit(take_along_axis)/gather | solution.py:50
  485.2 157.6 %gather_fusion.12 = f32[24576]{0:T(1024)S(1)} fusion(f32[32,64]{1,0:T(8,128)S(1)} %bitcast.155, s32[24576]{0:T(1024)S(1)} %reshape.336), kind=kCustom, calls=%fused_computation.3.clone | custom fusion | bytes 393216 | tf_op jit(solution)/shard_map/jit(take_along_axis)/gather | solution.py:49
  643.1 0.4 copy-done.17
  643.4 0.3 copy-done.3
  643.9 0.1 fusion.99
  644.0 2.9 fusion.73
  646.9 2.9 fusion.78
  649.8 0.6 broadcast.352
  650.4 0.8 fusion.122
  651.2 0.1 reshape.211
  651.3 0.6 gather_fusion.1
  652.0 0.7 reshape.411
  652.7 5.8 all-to-all-start.1
  658.5 0.6 gather_fusion
  659.1 0.6 gather_fusion.4
  659.7 314.6 %gather_fusion.10 = f32[49152]{0:T(1024)S(1)} fusion(f32[64,64]{1,0:T(8,128)S(1)} %gather_fusion, s32[49152]{0:T(1024)S(1)} %reshape.346), kind=kCustom, calls=%fused_computation.1.clone | custom fusion | bytes 786432 | tf_op jit(solution)/shard_map/jit(take_along_axis)/gather | solution.py:114
  974.4 0.7 reshape.349
  975.1 314.6 %gather_fusion.14 = f32[49152]{0:T(1024)S(1)} fusion(f32[64,64]{1,0:T(8,128)S(1)} %gather_fusion.4, s32[49152]{0:T(1024)S(1)} %reshape.346), kind=kCustom, calls=%fused_computation.6.clone | custom fusion | bytes 786432 | tf_op jit(solution)/shard_map/jit(take_along_axis)/gather | solution.py:114
  1289.7 0.6 gather_fusion.7
  1290.4 1.6 copy.21
  1292.0 1.2 gather_fusion.3
  1293.2 0.6 gather_fusion.5
  1293.9 0.7 reshape.407
  1294.5 0.7 eq.171
  1295.2 6.0 all-to-all-start.3
  1301.4 0.6 gather_fusion.2
  1301.9 314.6 %gather_fusion.11 = f32[49152]{0:T(1024)S(1)} fusion(f32[64,64]{1,0:T(8,128)S(1)} %gather_fusion.2, s32[49152]{0:T(1024)S(1)} %reshape.351), kind=kCustom, calls=%fused_computation.5.clone | custom fusion | bytes 786432 | tf_op jit(solution)/shard_map/jit(take_along_axis)/gather | solution.py:115
  1616.6 0.1 reshape.408
  1616.7 0.6 gather_fusion.6
  1617.3 314.6 %gather_fusion.15 = f32[49152]{0:T(1024)S(1)} fusion(f32[64,64]{1,0:T(8,128)S(1)} %gather_fusion.6, s32[49152]{0:T(1024)S(1)} %reshape.351), kind=kCustom, calls=%fused_computation.7.clone | custom fusion | bytes 786432 | tf_op jit(solution)/shard_map/jit(take_along_axis)/gather | solution.py:115
  1932.0 0.2 fusion.91
  1932.2 0.1 fusion.92
  1932.3 0.2 broadcast.62.clone
  1932.6 3.3 while.33
  1932.6 1.6 fusion.140
  1934.3 1.6 fusion.140
  1935.9 0.6 fusion.101
  1936.5 0.9 scatter_custom_fusion.2
  1937.4 0.7 reshape.409
  1938.1 5.7 all-to-all-start.4
  1943.8 0.2 broadcast.62.clone.1
  1944.0 3.3 while.32
  1944.1 1.6 fusion.138
  1945.8 1.6 fusion.138
  1947.4 0.6 fusion.103
  1948.0 1.0 scatter_custom_fusion.1
  1949.1 0.7 reshape.413
  1949.8 1.1 all-to-all-done.4
  1950.9 4.7 all-to-all-start.2
  1955.7 0.2 convolution_add_fusion
  1956.0 1.0 fusion.124
  1957.0 5.8 all-to-all-done.2
  1962.9 0.2 convolution_add_fusion.1
  1963.1 1.0 fusion.123
  1964.1 0.6 pad_maximum_fusion
  (77 shorter events, 1.1 us)
Async XLA Ops:
  0.0 12.4 copy-start
  1.6 648.2 %copy-start.14 = (s32[64]{0:T(128)}, s32[64]{0:T(128)S(1)}, u32[]{:S(2)}) copy-start(s32[64]{0:T(128)S(1)} %fusion.119) | copy-start | bytes 772
  3.2 646.6 %all-to-all-start = ((s32[32,4,1]{1,2,0:T(1,128)}), s32[32,4,1]{1,2,0:T(1,128)S(1)}, u32[]{:S(2)}, u32[]{:S(2)}) async-start(s32[32,4,1]{1,2,0:T(1,128)} %bitcast.15), calls=%async_computation | async-start | bytes 32768 | tf_op jit(solution)/shard_map/all_to_all | solution.py:99
  170.0 157.6 %copy-start.12 = (f32[2,64,32]{1,2,0:T(8,128)S(1)}, f32[2,64,32]{1,2,0:T(8,128)}, u32[]{:S(2)}) copy-start(f32[2,64,32]{1,2,0:T(8,128)} %param.22) | copy-start | bytes 49156
  485.2 157.8 %copy-start.1 = (s32[64,768]{1,0:T(8,128)S(1)}, s32[64,768]{1,0:T(8,128)}, u32[]{:S(2)}) copy-start(s32[64,768]{1,0:T(8,128)} %param.29) | copy-start | bytes 589828
  642.8 0.7 copy-start.17
  642.8 0.9 copy-start.3
  642.8 1.0 copy-start.9
  642.8 1.0 copy-start.10
  642.8 1.1 copy-start.11
  642.9 1.1 copy-start.16
  652.7 642.6 %all-to-all-start.1 = ((bf16[32,2,128]{2,1,0:T(2,128)(2,1)}), bf16[32,2,128]{2,1,0:T(2,128)(2,1)S(1)}, u32[]{:S(2)}, u32[]{:S(2)}) async-start(bf16[32,2,128]{2,1,0:T(2,128)(2,1)} %reshape.411), calls=%async_computation.1 | async-start | bytes 32768 | tf_op jit(solution)/shard_map/all_to_all | solution.py:109
  975.1 315.3 %copy-start.6 = (f32[64,64,32]{1,2,0:T(8,128)S(1)}, f32[64,64,32]{1,2,0:T(8,128)}, u32[]{:S(2)}) copy-start(f32[64,64,32]{1,2,0:T(8,128)} %param.24) | copy-start | bytes 1572868
  1295.2 321.4 %all-to-all-start.3 = ((bf16[32,2,128]{2,1,0:T(2,128)(2,1)}), bf16[32,2,128]{2,1,0:T(2,128)(2,1)S(1)}, u32[]{:S(2)}, u32[]{:S(2)}) async-start(bf16[32,2,128]{2,1,0:T(2,128)(2,1)} %reshape.407), calls=%async_computation.3 | async-start | bytes 32768 | tf_op jit(solution)/shard_map/all_to_all | solution.py:109
  1617.3 314.7 %copy-start.2 = (s32[64,768]{1,0:T(8,128)S(1)}, s32[64,768]{1,0:T(8,128)}, u32[]{:S(2)}) copy-start(s32[64,768]{1,0:T(8,128)} %param.29) | copy-start | bytes 589828
  1617.3 314.7 %copy-start.4 = (s32[64,768]{1,0:T(8,128)S(1)}, s32[64,768]{1,0:T(8,128)}, u32[]{:S(2)}) copy-start(s32[64,768]{1,0:T(8,128)} %param.28) | copy-start | bytes 589828
  1617.3 314.7 %copy-start.7 = (f32[64,768]{1,0:T(8,128)S(1)}, f32[64,768]{1,0:T(8,128)}, u32[]{:S(2)}) copy-start(f32[64,768]{1,0:T(8,128)} %reshape.349) | copy-start | bytes 589828
  1617.3 314.7 %copy-start.8 = (f32[64,768]{1,0:T(8,128)S(1)}, f32[64,768]{1,0:T(8,128)}, u32[]{:S(2)}) copy-start(f32[64,768]{1,0:T(8,128)} %param.30) | copy-start | bytes 589828
  1938.1 12.8 all-to-all-start.4
  1944.0 3.4 copy-start.13
  1947.4 8.3 copy-start.15
  1947.4 8.3 copy-start.19
  1947.4 8.6 copy-start.5
  1948.0 14.8 copy-start.18
  1950.9 11.8 all-to-all-start.2
where the time goes:
time: 1970 us; the launch traced here: 1960 us
  local copies, waits for them, and re-layouts  1910 us (97%)
  starting transfers between devices  29.5 us (1%)
    gather x5, local copies, waits for them, and re-layouts, per_device(): jnp.take_along_axis(by_block[couple_block], couple_source, axis=1)  630 us
    gather x5, local copies, waits for them, and re-layouts, per_device(): jnp.take_along_axis(remote_field.T[slot_index], couple_target, axis=1)  629 us
    gather x5, local copies, waits for them, and re-layouts, inner_images(): jnp.take_along_axis(by_block, source, axis=1)  315 us
    gather x5, local copies, waits for them, and re-layouts, inner_images(): jnp.take_along_axis(by_block, target, axis=1)  315 us
  transfers between devices with their start and end apart: 5, of which 2 were waited for; matrix products, arithmetic and copies ran while one was open for 81% of the time, Pallas kernels for 0%

commit v1 on v0

v1 whole, which is shorter than its diff:
```python
import functools

import jax
import jax.numpy as jnp
from jax import lax
from jax.experimental import pallas as pl
from jax.experimental.pallas import tpu as pltpu
from jax.sharding import PartitionSpec as P

BS = 64
NEWTON = 2
LANES = 128
GROUP = 16
DIGIT = 8
AXES = ("dom", "sub")
NT = (((1,), (1,)), ((), ()))
TN = (((0,), (0,)), ((), ()))
NN = (((1,), (0,)), ((), ()))
F32 = jnp.float32
BF16 = jnp.bfloat16


def iota(shape, axis):
    return lax.broadcasted_iota(jnp.int32, shape, axis)


def dot(first, second, numbers):
    return lax.dot_general(first, second, numbers, preferred_element_type=F32)


def pick(table, index):
    return jnp.concatenate(
        [
            jnp.take_along_axis(table[r : r + 8], index[r : r + 8], axis=1)
            for r in range(0, table.shape[0], 8)
        ],
        axis=0,
    )


def conductance(gain, first, second):
    drop = first - second
    return gain / (1.0 + drop * drop)


def digits(index):
    high = lax.shift_right_logical(index, 3)
    return high.astype(F32).astype(BF16), (index - high * DIGIT).astype(F32).astype(BF16)


def hot_rows(digit, values):
    zero = jnp.zeros_like(values[0])
    masks = [digit == jnp.asarray(d, BF16) for d in range(DIGIT)]
    return jnp.concatenate([jnp.where(m, v, zero) for v in values for m in masks], axis=0)


def same_block(rows, columns):
    shape = (rows, columns)
    return (iota(shape, 0) % GROUP) == (iota(shape, 1) % GROUP)


def gather_nodes(spread):
    shape = (NEWTON * DIGIT * GROUP, LANES)
    column, lane = iota(shape, 0), iota(shape, 1)
    low = (column // GROUP) % DIGIT
    step = column // (GROUP * DIGIT)
    keep = low == lane % DIGIT
    if spread:
        keep = keep & (step == lane // BS)
    return keep.astype(F32).astype(BF16)


def fold_rows(wide):
    lane = iota((GROUP, LANES), 1) // DIGIT
    total = jnp.zeros((GROUP, LANES), F32)
    for s in range(NEWTON * DIGIT):
        total = total + jnp.where(lane == s, wide[s * GROUP : (s + 1) * GROUP], 0.0)
    return total


def split(value, parts):
    pieces = []
    for _ in range(parts):
        piece = value.astype(BF16)
        pieces.append(piece)
        value = value - piece.astype(F32)
    return pieces


def prepare_kernel(volt_ref, step_ref, cap_ref, send_ref, volt_out, update_out, cap_out):
    first = volt_ref[...]
    block_count = first.shape[1]
    step = step_ref[0]
    fields = jnp.concatenate([first, first + step], axis=0)
    updates = jnp.concatenate([step, step_ref[1]], axis=0).astype(BF16).astype(F32)
    caps = jnp.concatenate([cap_ref[...], cap_ref[...]], axis=0)
    field_rows = fields.T
    volt_out[...] = field_rows
    update_out[...] = updates.T
    cap_out[...] = caps.T
    packed = field_rows.astype(BF16)
    for d in range(send_ref.shape[0] // block_count):
        send_ref[pl.ds(d * block_count, block_count), :] = packed


def inner_kernel(volt_ref, update_ref, cap_ref, source_ref, target_ref, gain_ref, out_ref):
    block_count, elements = source_ref.shape
    nodes_any, nodes_step = gather_nodes(False), gather_nodes(True)
    images = []
    for start in range(0, block_count, GROUP):
        rows = slice(start, start + GROUP)
        volts, updates = volt_ref[rows, :], update_ref[rows, :]
        acc_ones = jnp.zeros((NEWTON * DIGIT * GROUP, DIGIT * GROUP), F32)
        acc = jnp.zeros((NEWTON * DIGIT * GROUP, NEWTON * DIGIT * GROUP), F32)
        for at in range(0, elements, LANES):
            lanes = slice(at, at + LANES)
            source, target = source_ref[rows, lanes], target_ref[rows, lanes]
            gain = jnp.where(source == target, 0.0, gain_ref[rows, lanes])
            weights, source_updates, target_updates = [], [], []
            for t in range(NEWTON):
                here, there = source + t * BS, target + t * BS
                weights.append(
                    conductance(gain, pick(volts, here), pick(volts, there)).astype(BF16)
                )
                source_updates.append(pick(updates, here).astype(BF16))
                target_updates.append(pick(updates, there).astype(BF16))
            ones = jnp.ones((GROUP, LANES), BF16)
            left, right, right_ones = [], [], []
            for index, others in ((source, target_updates), (target, source_updates)):
                high, low = digits(index)
                left.append(hot_rows(high, weights))
                right_ones.append(hot_rows(low, [ones]))
                right.append(hot_rows(low, others))
            left = jnp.concatenate(left, axis=1)
            acc_ones = acc_ones + dot(left, jnp.concatenate(right_ones, axis=1), NT)
            acc = acc + dot(left, jnp.concatenate(right, axis=1), NT)
        acc = jnp.where(same_block(*acc.shape), acc, 0.0)
        acc_ones = jnp.where(same_block(*acc_ones.shape), acc_ones, 0.0)
        diagonal = fold_rows(
            sum(dot(p, nodes_any[: DIGIT * GROUP], NN) for p in split(acc_ones, 2))
        )
        others = fold_rows(sum(dot(p, nodes_step, NN) for p in split(acc, 2)))
        diagonal = (diagonal + cap_ref[rows, :]).astype(BF16).astype(F32)
        images.append(diagonal * updates - others)
    out_ref[...] = jnp.concatenate(images, axis=0).T


def row_to_column(row):
    count = row.shape[1]
    shape = (count, count)
    return jnp.sum(jnp.where(iota(shape, 0) == iota(shape, 1), row, 0), axis=1, keepdims=True)


def column_to_row(column):
    count = column.shape[0]
    shape = (count, count)
    return jnp.sum(jnp.where(iota(shape, 0) == iota(shape, 1), column, 0), axis=0, keepdims=True)


def couple_kernel(
    per_owner,
    fields_ref,
    volt_ref,
    update_ref,
    block_ref,
    owner_ref,
    offset_ref,
    source_ref,
    target_ref,
    gain_ref,
    send_ref,
):
    stamp_count, elements = source_ref.shape
    block_count = volt_ref.shape[0]
    owner = owner_ref[...].astype(F32)
    offset = row_to_column(offset_ref[...].astype(F32))
    block = row_to_column(block_ref[...].astype(F32))
    owner_row = column_to_row(owner)

    row_hot = (
        iota((stamp_count, fields_ref.shape[0]), 1).astype(F32) == owner * block_count + offset
    )
    remote = dot(row_hot.astype(F32).astype(BF16), fields_ref[...], NN)
    block_hot = (iota((stamp_count, block_count), 1).astype(F32) == block).astype(F32).astype(BF16)
    high, middle, low = (dot(block_hot, p, NN) for p in split(volt_ref[...], 3))
    local = high + middle + low
    update = dot(block_hot, update_ref[...].astype(BF16), NN)

    nodes_step = gather_nodes(True)
    images = []
    for start in range(0, stamp_count, GROUP):
        rows = slice(start, start + GROUP)
        near, far, moved = local[rows], remote[rows], update[rows]
        acc = jnp.zeros((NEWTON * DIGIT * GROUP, NEWTON * DIGIT * GROUP), F32)
        left, right = [], []
        for at in range(0, elements, LANES):
            lanes = slice(at, at + LANES)
            source, target = source_ref[rows, lanes], target_ref[rows, lanes]
            gain = -gain_ref[rows, lanes]
            weights, updates = [], []
            for t in range(NEWTON):
                here, there = source + t * BS, target + t * BS
                weights.append(conductance(gain, pick(near, here), pick(far, there)).astype(BF16))
                updates.append(pick(moved, here).astype(BF16))
            high, low = digits(target)
            left.append(hot_rows(high, weights))
            right.append(hot_rows(low, updates))
            if len(left) == 2 or at + LANES >= elements:
                acc = acc + dot(
                    jnp.concatenate(left, axis=1), jnp.concatenate(right, axis=1), NT
                )
                left, right = [], []
        acc = jnp.where(same_block(*acc.shape), acc, 0.0).astype(BF16)
        images.append(fold_rows(dot(acc, nodes_step, NN)))
    images = jnp.concatenate(images, axis=0)

    shape = (stamp_count, stamp_count)
    earlier = (owner == owner_row) & (iota(shape, 0) < iota(shape, 1))
    rank_row = jnp.sum(jnp.where(earlier, 1.0, 0.0), axis=0, keepdims=True)
    slot_row = (owner_row * per_owner + rank_row) * NEWTON
    slots = jnp.concatenate([slot_row + t for t in range(NEWTON)], axis=1)
    place = iota((send_ref.shape[0], NEWTON * stamp_count), 0).astype(F32) == slots
    lane = iota((stamp_count, LANES), 1)
    offset_hot = jnp.where(lane.astype(F32) == offset, 1.0, 0.0)
    first = jnp.where(lane < BS, offset_hot, pltpu.roll(images, BS, 1))
    second = jnp.where(lane < BS, offset_hot, images)
    messages = jnp.concatenate([first, second], axis=0).astype(BF16)
    send_ref[...] = dot(place.astype(F32).astype(BF16), messages, NN).astype(BF16)


def finish_kernel(images_ref, inner_ref, precond_ref, out_ref):
    received = images_ref[...]
    block_count = inner_ref.shape[1]
    parity = iota(received.shape, 0) % NEWTON
    zero = jnp.zeros_like(received)
    for t in range(NEWTON):
        mine = jnp.where(parity == t, received.astype(F32), 0.0).astype(BF16)
        couple = dot(received, mine, TN)[BS:, :block_count]
        total = inner_ref[t * BS : (t + 1) * BS, :] + couple
        for i in range(0, BS, DIGIT):
            out_ref[t, i : i + DIGIT, :] = jnp.sum(
                precond_ref[i : i + DIGIT] * total[None], axis=1
            )


def call(kernel, out_shape, args, flops, bytes_accessed):
    spec = pl.BlockSpec(memory_space=pltpu.VMEM)
    several = isinstance(out_shape, (list, tuple))
    return pl.pallas_call(
        kernel,
        out_shape=out_shape,
        in_specs=[spec] * len(args),
        out_specs=[spec] * len(out_shape) if several else spec,
        compiler_params=pltpu.CompilerParams(vmem_limit_bytes=24 * 2**20),
        cost_estimate=pl.CostEstimate(
            flops=flops, bytes_accessed=bytes_accessed, transcendentals=0
        ),
    )(*args)


def exchange(rows, devices):
    shaped = rows.reshape((devices, rows.shape[0] // devices, rows.shape[1]))
    out = lax.all_to_all(shaped, AXES, split_axis=0, concat_axis=0, tiled=True)
    return out.reshape(rows.shape)


def per_device(
    voltages,
    newton_steps,
    cap_diag,
    preconditioner,
    couple_block,
    couple_owner,
    couple_offset,
    couple_source,
    couple_target,
    couple_gain,
    inner_source,
    inner_target,
    inner_gain,
):
    devices = lax.axis_size(AXES)
    stamp_count = couple_block.shape[0]
    block_count = voltages.shape[1]
    per_owner = max(2, 2 * stamp_count // devices)
    table = jax.ShapeDtypeStruct((block_count, LANES), F32)
    send, volts, updates, caps = call(
        prepare_kernel,
        [jax.ShapeDtypeStruct((devices * block_count, LANES), BF16), table, table, table],
        (voltages, newton_steps, cap_diag),
        10**5,
        10**5,
    )
    fields = exchange(send, devices)
    inner = call(
        inner_kernel,
        jax.ShapeDtypeStruct((NEWTON * BS, block_count), F32),
        (volts, updates, caps, inner_source, inner_target, inner_gain),
        4 * 10**9,
        10**6,
    )
    images = call(
        functools.partial(couple_kernel, per_owner),
        jax.ShapeDtypeStruct((devices * per_owner * NEWTON, LANES), BF16),
        (
            fields,
            volts,
            updates,
            couple_block.reshape(1, stamp_count),
            couple_owner,
            couple_offset.reshape(1, stamp_count),
            couple_source,
            couple_target,
            couple_gain,
        ),
        4 * 10**9,
        10**6,
    )
    received = exchange(images, devices)
    return call(
        finish_kernel,
        jax.ShapeDtypeStruct((NEWTON, BS, block_count), F32),
        (received, inner, preconditioner),
        10**8,
        2 * 10**6,
    )


def solution(mesh):
    in_specs = (
        P(None, AXES),
        P(None, None, AXES),
        P(None, AXES),
        P(None, None, AXES),
        P(AXES),
        P(AXES, None),
        P(AXES),
        P(AXES, None),
        P(AXES, None),
        P(AXES, None),
        P(AXES, None),
        P(AXES, None),
        P(AXES, None),
    )
    out_specs = P(None, None, AXES)
    return jax.shard_map(
        per_device, mesh=mesh, in_specs=in_specs, out_specs=out_specs, check_vma=False
    )
```

time: 1970 us -> 39.8 us (0.02)
  local copies, waits for them, and re-layouts: 1910 us -> 8.6 us
    gather x28 -> x0, local copies, waits for them, and re-layouts: 1900 us -> none  [the longest x5 630 us: per_device(): jnp.take_along_axis(by_block[couple_block], couple_source, axis=1)]
  transfers between devices with their start and end apart: 5 -> 2, of which waited for: 2 -> 2; matrix products, arithmetic and copies ran while one was open for 81% -> 3% of each run, Pallas kernels for 0% -> 4%
where the time goes in v1:
time: 39.8 us; the launch traced here: 39.4 us
  waiting for transfers between devices  15 us (38%)
  starting transfers between devices  9.84 us (25%)
  local copies, waits for them, and re-layouts  8.6 us (22%)
  Pallas kernels  5.81 us (15%)
    all_to_all x2, waiting for transfers between devices, exchange(): out = lax.all_to_all(shaped, AXES, split_axis=0, concat_axis=0, tiled=True)  15 us
    all_to_all x2, starting transfers between devices, exchange(): out = lax.all_to_all(shaped, AXES, split_axis=0, concat_axis=0, tiled=True)  9.84 us
    unnamed x23, local copies, waits for them, and re-layouts  7.91 us
    pallas_call x4, Pallas kernels, call(): pl.pallas_call(kernel, out_shape=out_shape, in_specs=[spec] * len(args),...  5.81 us
  transfers between devices with their start and end apart: 2, of which 2 were waited for; matrix products, arithmetic and copies ran while one was open for 3% of the time, Pallas kernels for 4%

profile of v1, /device:TPU:0, one launch (start us, length us, event | category | flops | bytes accessed | tf_op | source)
XLA Modules:
  0.0 39.4 jit_solution(10638402449946014439)
XLA Ops:
  0.0 0.8 %copy.14.volt_ref = f32[64,32]{1,0:T(8,128)S(1)} copy(f32[64,32]{0,1:T(8,128)} %param.13) | data formatting | bytes 16384 | tf_op args[0]
  0.8 0.8 %copy.16.cap_ref = f32[64,32]{1,0:T(8,128)S(1)} copy(f32[64,32]{0,1:T(8,128)} %param.15) | data formatting | bytes 16384 | tf_op args[2]
  1.6 0.8 %copy.15.step_ref = f32[2,64,32]{2,1,0:T(8,128)S(1)} copy(f32[2,64,32]{1,2,0:T(8,128)} %param.14) | data formatting | bytes 32768 | tf_op args[1]
  2.4 0.8 %shard_map.127 = (bf16[1024,128]{1,0:T(8,128)(2,1)}, f32[32,128]{1,0:T(8,128)S(1)}, f32[32,128]{1,0:T(8,128)S(1)}, f32[32,128]{1,0:T(8,128)S(1)}) custom-call(f32[64,32]{1,0:T(8,128)S(1)} %copy.14.volt_ref, f32[2,64,32]{2,1,0:T(8,128)S(1)} %copy.15.step_ref, f32[64,32]{1,0:T(8,128)S(1)} %copy.16.cap_ref), custom_call_target="tpu_custom_call" | custom-call | flops 100000 | bytes 100000 | tf_op jit(solution)/shard_map/pallas_call | solution.py:249
  3.2 7.3 %all-to-all-start = ((bf16[32,32,128]{2,1,0:T(8,128)(2,1)}), bf16[32,32,128]{2,1,0:T(8,128)(2,1)S(1)}, u32[]{:S(2)}, u32[]{:S(2)}) async-start(bf16[32,32,128]{2,1,0:T(8,128)(2,1)} %bitcast), calls=%async_computation | async-start | bytes 524288 | tf_op jit(solution)/shard_map/all_to_all | solution.py:263
  10.5 0.7 %copy.17.owner_ref = s32[64,1]{1,0:T(8,128)S(1)} copy(s32[64,1]{0,1:T(1,128)} %param.18) | data formatting | bytes 512 | tf_op args[5]
  11.3 9.9 %all-to-all-done = bf16[32,32,128]{2,1,0:T(8,128)(2,1)S(1)} async-done(((bf16[32,32,128]{2,1,0:T(8,128)(2,1)}), bf16[32,32,128]{2,1,0:T(8,128)(2,1)S(1)}, u32[]{:S(2)}, u32[]{:S(2)}) %all-to-all-start) | async-done | bytes 262176 | tf_op jit(solution)/shard_map/all_to_all | solution.py:263
  21.1 0.0 copy-start
  21.1 0.9 %copy-done = s32[64,768]{1,0:T(8,128)S(1)} copy-done((s32[64,768]{1,0:T(8,128)S(1)}, s32[64,768]{1,0:T(8,128)}, u32[]{:S(2)}) %copy-start) | copy-done | bytes 196632
  22.1 0.0 copy-start.1
  22.1 0.9 %copy-done.1 = s32[64,768]{1,0:T(8,128)S(1)} copy-done((s32[64,768]{1,0:T(8,128)S(1)}, s32[64,768]{1,0:T(8,128)}, u32[]{:S(2)}) %copy-start.1) | copy-done | bytes 196632
  23.0 0.0 copy-start.2
  23.0 0.9 %copy-done.2 = f32[64,768]{1,0:T(8,128)S(1)} copy-done((f32[64,768]{1,0:T(8,128)S(1)}, f32[64,768]{1,0:T(8,128)}, u32[]{:S(2)}) %copy-start.2) | copy-done | bytes 196632
  23.9 0.0 copy-start.6
  23.9 0.7 %copy-done.6 = s32[64]{0:T(128)S(1)} copy-done((s32[64]{0:T(128)S(1)}, s32[64]{0:T(128)}, u32[]{:S(2)}) %copy-start.6) | copy-done | bytes 280
  24.6 0.0 copy-start.7
  24.6 0.7 %copy-done.7 = s32[64]{0:T(128)S(1)} copy-done((s32[64]{0:T(128)S(1)}, s32[64]{0:T(128)}, u32[]{:S(2)}) %copy-start.7) | copy-done | bytes 280
  25.2 0.0 copy-start.3
  25.2 0.0 copy-start.4
  25.2 0.0 copy-start.5
  25.2 2.6 %shard_map.128 = bf16[256,128]{1,0:T(8,128)(2,1)} custom-call(bf16[1024,128]{1,0:T(8,128)(2,1)S(1)} %bitcast.7, f32[32,128]{1,0:T(8,128)S(1)} %get-tuple-element.10.volt_ref, f32[32,128]{1,0:T(8,128)S(1)} %get-tuple-element.11.update_ref, s32[1,64]{1,0:T(1,128)S(1)} %bitcast.8, s32[64,1]{1,0:T(8,128)S(1)} %copy.17.owner_ref, s32[1,64]{1,0:T(1,128)S(1)} %bitcast.9, ...), custom_call_target="tpu_custom_call" | custom-call | flops 4000000000 | bytes 1000000 | tf_op jit(solution)/shard_map/pallas_call | solution.py:249
  27.9 2.5 %all-to-all-start.1 = ((bf16[32,8,128]{2,1,0:T(8,128)(2,1)}), bf16[32,8,128]{2,1,0:T(8,128)(2,1)S(1)}, u32[]{:S(2)}, u32[]{:S(2)}) async-start(bf16[32,8,128]{2,1,0:T(8,128)(2,1)} %bitcast.4), calls=%async_computation.1 | async-start | bytes 131072 | tf_op jit(solution)/shard_map/all_to_all | solution.py:263
  30.4 0.0 copy-done.3
  30.4 0.0 copy-done.4
  30.4 0.0 copy-done.5
  30.5 0.0 copy-start.8
  30.5 1.5 %shard_map.129.inner_ref = f32[128,32]{1,0:T(8,128)S(1)} custom-call(f32[32,128]{1,0:T(8,128)S(1)} %get-tuple-element.10.volt_ref, f32[32,128]{1,0:T(8,128)S(1)} %get-tuple-element.11.update_ref, f32[32,128]{1,0:T(8,128)S(1)} %get-tuple-element.12.cap_ref, s32[32,768]{1,0:T(8,128)S(1)} %copy-done.3, s32[32,768]{1,0:T(8,128)S(1)} %copy-done.4, ...), custom_call_target="tpu_custom_call" | custom-call | flops 4000000000 | bytes 1000000 | tf_op jit(solution)/shard_map/pallas_call | solution.py:249
  32.0 0.0 copy-done.8
  32.0 0.6 %copy.18.precond_ref = f32[64,64,32]{2,1,0:T(8,128)S(1)} copy(f32[64,64,32]{1,2,0:T(8,128)S(1)} %copy-done.8) | data formatting | bytes 1048576 | tf_op args[3]
  32.7 5.2 %all-to-all-done.1 = bf16[32,8,128]{2,1,0:T(8,128)(2,1)S(1)} async-done(((bf16[32,8,128]{2,1,0:T(8,128)(2,1)}), bf16[32,8,128]{2,1,0:T(8,128)(2,1)S(1)}, u32[]{:S(2)}, u32[]{:S(2)}) %all-to-all-start.1) | async-done | bytes 65568 | tf_op jit(solution)/shard_map/all_to_all | solution.py:263
  37.8 0.8 %shard_map.130 = f32[2,64,32]{2,1,0:T(8,128)S(1)} custom-call(bf16[256,128]{1,0:T(8,128)(2,1)S(1)} %bitcast.6, f32[128,32]{1,0:T(8,128)S(1)} %shard_map.129.inner_ref, f32[64,64,32]{2,1,0:T(8,128)S(1)} %copy.18.precond_ref), custom_call_target="tpu_custom_call" | custom-call | flops 100000000 | bytes 2000000 | tf_op jit(solution)/shard_map/pallas_call | solution.py:249
  38.7 0.7 %copy.19 = f32[2,64,32]{1,2,0:T(8,128)} copy(f32[2,64,32]{2,1,0:T(8,128)S(1)} %shard_map.130) | data formatting | bytes 32768 | tf_op jit(solution)/shard_map/pallas_call | solution.py:249
Async XLA Ops:
  3.2 17.9 %all-to-all-start = ((bf16[32,32,128]{2,1,0:T(8,128)(2,1)}), bf16[32,32,128]{2,1,0:T(8,128)(2,1)S(1)}, u32[]{:S(2)}, u32[]{:S(2)}) async-start(bf16[32,32,128]{2,1,0:T(8,128)(2,1)} %bitcast), calls=%async_computation | async-start | bytes 524288 | tf_op jit(solution)/shard_map/all_to_all | solution.py:263
  21.1 0.9 %copy-start = (s32[64,768]{1,0:T(8,128)S(1)}, s32[64,768]{1,0:T(8,128)}, u32[]{:S(2)}) copy-start(s32[64,768]{1,0:T(8,128)} %source_ref.2) | copy-start | bytes 589828
  22.1 0.9 %copy-start.1 = (s32[64,768]{1,0:T(8,128)S(1)}, s32[64,768]{1,0:T(8,128)}, u32[]{:S(2)}) copy-start(s32[64,768]{1,0:T(8,128)} %target_ref.2) | copy-start | bytes 589828
  23.0 0.9 %copy-start.2 = (f32[64,768]{1,0:T(8,128)S(1)}, f32[64,768]{1,0:T(8,128)}, u32[]{:S(2)}) copy-start(f32[64,768]{1,0:T(8,128)} %gain_ref.2) | copy-start | bytes 589828
  23.9 0.7 %copy-start.6 = (s32[64]{0:T(128)S(1)}, s32[64]{0:T(128)}, u32[]{:S(2)}) copy-start(s32[64]{0:T(128)} %param.17) | copy-start | bytes 772
  24.6 0.7 %copy-start.7 = (s32[64]{0:T(128)S(1)}, s32[64]{0:T(128)}, u32[]{:S(2)}) copy-start(s32[64]{0:T(128)} %param.19) | copy-start | bytes 772
  25.2 5.2 %copy-start.3 = (s32[32,768]{1,0:T(8,128)S(1)}, s32[32,768]{1,0:T(8,128)}, u32[]{:S(2)}) copy-start(s32[32,768]{1,0:T(8,128)} %source_ref.3) | copy-start | bytes 294916
  25.2 5.2 %copy-start.4 = (s32[32,768]{1,0:T(8,128)S(1)}, s32[32,768]{1,0:T(8,128)}, u32[]{:S(2)}) copy-start(s32[32,768]{1,0:T(8,128)} %target_ref.3) | copy-start | bytes 294916
  25.2 5.2 %copy-start.5 = (f32[32,768]{1,0:T(8,128)S(1)}, f32[32,768]{1,0:T(8,128)}, u32[]{:S(2)}) copy-start(f32[32,768]{1,0:T(8,128)} %gain_ref.3) | copy-start | bytes 294916
  27.9 10.0 %all-to-all-start.1 = ((bf16[32,8,128]{2,1,0:T(8,128)(2,1)}), bf16[32,8,128]{2,1,0:T(8,128)(2,1)S(1)}, u32[]{:S(2)}, u32[]{:S(2)}) async-start(bf16[32,8,128]{2,1,0:T(8,128)(2,1)} %bitcast.4), calls=%async_computation.1 | async-start | bytes 131072 | tf_op jit(solution)/shard_map/all_to_all | solution.py:263
  30.5 1.6 %copy-start.8 = (f32[64,64,32]{1,2,0:T(8,128)S(1)}, f32[64,64,32]{1,2,0:T(8,128)}, u32[]{:S(2)}) copy-start(f32[64,64,32]{1,2,0:T(8,128)} %param.16) | copy-start | bytes 1572868

commit v2 on v1

v2 whole, which is shorter than its diff:
```python
import functools

import jax
import jax.numpy as jnp
from jax import lax
from jax.experimental import pallas as pl
from jax.experimental.pallas import tpu as pltpu
from jax.sharding import PartitionSpec as P

BS = 64
NEWTON = 2
LANES = 128
GROUP = 16
DIGIT = 8
AXES = ("dom", "sub")
NT = (((1,), (1,)), ((), ()))
TN = (((0,), (0,)), ((), ()))
NN = (((1,), (0,)), ((), ()))
F32 = jnp.float32
BF16 = jnp.bfloat16


def iota(shape, axis):
    return lax.broadcasted_iota(jnp.int32, shape, axis)


def dot(first, second, numbers):
    return lax.dot_general(first, second, numbers, preferred_element_type=F32)


def pick(table, index):
    return jnp.concatenate(
        [
            jnp.take_along_axis(table[r : r + 8], index[r : r + 8], axis=1)
            for r in range(0, table.shape[0], 8)
        ],
        axis=0,
    )


def conductance(gain, first, second):
    drop = first - second
    return gain / (1.0 + drop * drop)


def digits(index):
    high = lax.shift_right_logical(index, 3)
    return high.astype(F32).astype(BF16), (index - high * DIGIT).astype(F32).astype(BF16)


def hot_rows(digit, values):
    zero = jnp.zeros_like(values[0])
    masks = [digit == jnp.asarray(d, BF16) for d in range(DIGIT)]
    return jnp.concatenate([jnp.where(m, v, zero) for v in values for m in masks], axis=0)


def same_block(rows, columns):
    shape = (rows, columns)
    return (iota(shape, 0) % GROUP) == (iota(shape, 1) % GROUP)


def gather_nodes(spread):
    shape = (NEWTON * DIGIT * GROUP, LANES)
    column, lane = iota(shape, 0), iota(shape, 1)
    low = (column // GROUP) % DIGIT
    step = column // (GROUP * DIGIT)
    keep = low == lane % DIGIT
    if spread:
        keep = keep & (step == lane // BS)
    return keep.astype(F32).astype(BF16)


def fold_rows(wide):
    lane = iota((GROUP, LANES), 1) // DIGIT
    total = jnp.zeros((GROUP, LANES), F32)
    for s in range(NEWTON * DIGIT):
        total = total + jnp.where(lane == s, wide[s * GROUP : (s + 1) * GROUP], 0.0)
    return total


def split(value, parts):
    pieces = []
    for _ in range(parts):
        piece = value.astype(BF16)
        pieces.append(piece)
        value = value - piece.astype(F32)
    return pieces


def fields_of(table_ref):
    first = table_ref[0]
    return jnp.concatenate([first, first + table_ref[1]], axis=1)


def prepare_kernel(table_ref, send_ref):
    packed = fields_of(table_ref).astype(BF16)
    block_count = packed.shape[0]
    for d in range(send_ref.shape[0] // block_count):
        send_ref[pl.ds(d * block_count, block_count), :] = packed


def inner_images(volt_rows, update_rows, cap_rows, source_ref, target_ref, gain_ref):
    block_count, elements = source_ref.shape
    nodes_any, nodes_step = gather_nodes(False), gather_nodes(True)
    images = []
    for start in range(0, block_count, GROUP):
        rows = slice(start, start + GROUP)
        volts, updates = volt_rows[rows], update_rows[rows]
        acc_ones = jnp.zeros((NEWTON * DIGIT * GROUP, DIGIT * GROUP), F32)
        acc = jnp.zeros((NEWTON * DIGIT * GROUP, NEWTON * DIGIT * GROUP), F32)
        for at in range(0, elements, LANES):
            lanes = slice(at, at + LANES)
            source, target = source_ref[rows, lanes], target_ref[rows, lanes]
            gain = jnp.where(source == target, 0.0, gain_ref[rows, lanes])
            weights, source_updates, target_updates = [], [], []
            for t in range(NEWTON):
                here, there = source + t * BS, target + t * BS
                weights.append(
                    conductance(gain, pick(volts, here), pick(volts, there)).astype(BF16)
                )
                source_updates.append(pick(updates, here).astype(BF16))
                target_updates.append(pick(updates, there).astype(BF16))
            ones = jnp.ones((GROUP, LANES), BF16)
            left, right, right_ones = [], [], []
            for index, others in ((source, target_updates), (target, source_updates)):
                high, low = digits(index)
                left.append(hot_rows(high, weights))
                right_ones.append(hot_rows(low, [ones]))
                right.append(hot_rows(low, others))
            left = jnp.concatenate(left, axis=1)
            acc_ones = acc_ones + dot(left, jnp.concatenate(right_ones, axis=1), NT)
            acc = acc + dot(left, jnp.concatenate(right, axis=1), NT)
        acc = jnp.where(same_block(*acc.shape), acc, 0.0)
        acc_ones = jnp.where(same_block(*acc_ones.shape), acc_ones, 0.0)
        diagonal = fold_rows(
            sum(dot(p, nodes_any[: DIGIT * GROUP], NN) for p in split(acc_ones, 2))
        )
        others = fold_rows(sum(dot(p, nodes_step, NN) for p in split(acc, 2)))
        diagonal = (diagonal + cap_rows[rows]).astype(BF16).astype(F32)
        images.append(diagonal * updates - others)
    return jnp.concatenate(images, axis=0)


def row_to_column(row):
    count = row.shape[1]
    shape = (count, count)
    return jnp.sum(jnp.where(iota(shape, 0) == iota(shape, 1), row, 0), axis=1, keepdims=True)


def local_kernel(
    per_owner,
    table_ref,
    cap_ref,
    block_ref,
    owner_ref,
    offset_ref,
    inner_source_ref,
    inner_target_ref,
    inner_gain_ref,
    source_ref,
    target_ref,
    gain_ref,
    inner_ref,
    target_out,
    gain_out,
    near_ref,
    moved_ref,
    row_hot_ref,
    place_ref,
    offset_hot_ref,
):
    stamp_count, elements = source_ref.shape
    block_count = table_ref.shape[1]
    target_out[...] = target_ref[...]
    gain_out[...] = gain_ref[...]
    volt_rows = fields_of(table_ref)
    updates = jnp.concatenate([table_ref[1], table_ref[2]], axis=1).astype(BF16)
    caps = jnp.concatenate([cap_ref[...], cap_ref[...]], axis=1)

    owner_row = owner_ref[...].astype(F32)
    owner = row_to_column(owner_row)
    offset = row_to_column(offset_ref[...].astype(F32))
    block = row_to_column(block_ref[...].astype(F32))
    row_hot = iota(row_hot_ref.shape, 1).astype(F32) == owner * block_count + offset
    row_hot_ref[...] = row_hot.astype(F32).astype(BF16)
    shape = (stamp_count, stamp_count)
    earlier = (owner == owner_row) & (iota(shape, 0) < iota(shape, 1))
    rank_row = jnp.sum(jnp.where(earlier, 1.0, 0.0), axis=0, keepdims=True)
    slot_row = (owner_row * per_owner + rank_row) * NEWTON
    slots = jnp.concatenate([slot_row + t for t in range(NEWTON)], axis=1)
    place_ref[...] = (iota(place_ref.shape, 0).astype(F32) == slots).astype(F32).astype(BF16)
    offset_hot_ref[...] = jnp.where(
        iota(offset_hot_ref.shape, 1).astype(F32) == offset, 1.0, 0.0
    )

    block_hot = (iota((stamp_count, block_count), 1).astype(F32) == block).astype(F32).astype(BF16)
    local = sum(dot(block_hot, p, NN) for p in split(volt_rows, 3))
    moved = dot(block_hot, updates, NN)
    for start in range(0, stamp_count, GROUP):
        rows = slice(start, start + GROUP)
        for at in range(0, elements, LANES):
            lanes = slice(at, at + LANES)
            source = source_ref[rows, lanes]
            for t in range(NEWTON):
                here = source + t * BS
                near_ref[t, rows, lanes] = pick(local[rows], here)
                moved_ref[t, rows, lanes] = pick(moved[rows], here).astype(BF16)
    inner_ref[...] = inner_images(
        volt_rows, updates.astype(F32), caps, inner_source_ref, inner_target_ref, inner_gain_ref
    ).T


def couple_kernel(
    fields_ref,
    target_ref,
    gain_ref,
    near_ref,
    moved_ref,
    row_hot_ref,
    place_ref,
    offset_hot_ref,
    send_ref,
):
    stamp_count, elements = target_ref.shape
    remote = dot(row_hot_ref[...], fields_ref[...], NN)
    nodes_step = gather_nodes(True)
    images = []
    for start in range(0, stamp_count, GROUP):
        rows = slice(start, start + GROUP)
        far = remote[rows]
        acc = jnp.zeros((NEWTON * DIGIT * GROUP, NEWTON * DIGIT * GROUP), F32)
        left, right = [], []
        for at in range(0, elements, LANES):
            lanes = slice(at, at + LANES)
            target = target_ref[rows, lanes]
            gain = -gain_ref[rows, lanes]
            weights = [
                conductance(gain, near_ref[t, rows, lanes], pick(far, target + t * BS)).astype(BF16)
                for t in range(NEWTON)
            ]
            high, low = digits(target)
            left.append(hot_rows(high, weights))
            right.append(hot_rows(low, [moved_ref[t, rows, lanes] for t in range(NEWTON)]))
            if len(left) == 2 or at + LANES >= elements:
                acc = acc + dot(
                    jnp.concatenate(left, axis=1), jnp.concatenate(right, axis=1), NT
                )
                left, right = [], []
        acc = jnp.where(same_block(*acc.shape), acc, 0.0).astype(BF16)
        images.append(fold_rows(dot(acc, nodes_step, NN)))
    images = jnp.concatenate(images, axis=0)
    lane = iota(images.shape, 1)
    messages = jnp.concatenate(
        [
            jnp.where(lane < BS, offset_hot_ref[...], pltpu.roll(images, BS, 1)),
            jnp.where(lane < BS, offset_hot_ref[...], images),
        ],
        axis=0,
    ).astype(BF16)
    send_ref[...] = dot(place_ref[...], messages, NN).astype(BF16)


def finish_kernel(images_ref, inner_ref, precond_ref, out_ref):
    received = images_ref[...]
    block_count = inner_ref.shape[1]
    parity = iota(received.shape, 0) % NEWTON
    for t in range(NEWTON):
        mine = jnp.where(parity == t, received.astype(F32), 0.0).astype(BF16)
        couple = dot(received, mine, TN)[BS:, :block_count]
        total = inner_ref[t * BS : (t + 1) * BS, :] + couple
        rows = [
            jnp.sum(precond_ref[i : i + DIGIT] * total[None], axis=1)
            for i in range(0, BS, DIGIT)
        ]
        out_ref[t] = jnp.concatenate(rows, axis=0).T


def call(kernel, out_shape, args, flops):
    spec = pl.BlockSpec(memory_space=pltpu.VMEM)
    several = isinstance(out_shape, (list, tuple))
    return pl.pallas_call(
        kernel,
        out_shape=out_shape,
        in_specs=[spec] * len(args),
        out_specs=[spec] * len(out_shape) if several else spec,
        compiler_params=pltpu.CompilerParams(vmem_limit_bytes=24 * 2**20),
        cost_estimate=pl.CostEstimate(flops=flops, bytes_accessed=10**6, transcendentals=0),
    )(*args)


def exchange(rows, devices):
    shaped = rows.reshape((devices, rows.shape[0] // devices, rows.shape[1]))
    out = lax.all_to_all(shaped, AXES, split_axis=0, concat_axis=0, tiled=True)
    return out.reshape(rows.shape)


def per_device(
    voltages,
    newton_steps,
    cap_diag,
    preconditioner,
    couple_block,
    couple_owner,
    couple_offset,
    couple_source,
    couple_target,
    couple_gain,
    inner_source,
    inner_target,
    inner_gain,
):
    devices = lax.axis_size(AXES)
    stamp_count, elements = couple_source.shape
    block_count = voltages.shape[1]
    per_owner = max(2, 2 * stamp_count // devices)
    row_count = devices * per_owner * NEWTON
    like = jax.ShapeDtypeStruct
    table = jnp.concatenate([voltages.T[None], newton_steps.transpose(0, 2, 1)], axis=0)
    send = call(
        prepare_kernel, like((devices * block_count, LANES), BF16), (table,), 2 * 10**10
    )
    fields = exchange(send, devices)
    inner, *prepared = call(
        functools.partial(local_kernel, per_owner),
        [
            like((NEWTON * BS, block_count), F32),
            like(couple_target.shape, couple_target.dtype),
            like(couple_gain.shape, couple_gain.dtype),
            like((NEWTON, stamp_count, elements), F32),
            like((NEWTON, stamp_count, elements), BF16),
            like((stamp_count, devices * block_count), BF16),
            like((row_count, NEWTON * stamp_count), BF16),
            like((stamp_count, LANES), F32),
        ],
        (
            table,
            cap_diag.T,
            couple_block.reshape(1, stamp_count),
            couple_owner.reshape(1, stamp_count),
            couple_offset.reshape(1, stamp_count),
            inner_source,
            inner_target,
            inner_gain,
            couple_source,
            couple_target,
            couple_gain,
        ),
        2 * 10**10,
    )
    images = call(
        couple_kernel, like((row_count, LANES), BF16), (fields, *prepared), 4 * 10**9
    )
    received = exchange(images, devices)
    out = call(
        finish_kernel,
        like((NEWTON, block_count, BS), F32),
        (received, inner, preconditioner),
        10**8,
    )
    return out.transpose(0, 2, 1)


def solution(mesh):
    in_specs = (
        P(None, AXES),
        P(None, None, AXES),
        P(None, AXES),
        P(None, None, AXES),
        P(AXES),
        P(AXES, None),
        P(AXES),
        P(AXES, None),
        P(AXES, None),
        P(AXES, None),
        P(AXES, None),
        P(AXES, None),
        P(AXES, None),
    )
    out_specs = P(None, None, AXES)
    return jax.shard_map(
        per_device, mesh=mesh, in_specs=in_specs, out_specs=out_specs, check_vma=False
    )
```

time: 39.8 us -> 33.7 us (0.85)
  local copies, waits for them, and re-layouts: 8.6 us -> 1.91 us
  other arithmetic: 0 us -> 0.77 us
  waiting for transfers between devices: 15 us -> 14.3 us
  Pallas kernels: 5.81 us -> 6.33 us
    unnamed x23 -> x21, local copies, waits for them, and re-layouts: 7.91 us -> 1.91 us
    concatenate x0 -> x1, other arithmetic: none -> 0.77 us  [per_device(): jnp.concatenate([voltages.T[None], newton_steps.transpose(0, 2, 1)], axis=0)]
    pallas_call x1 -> x0, local copies, waits for them, and re-layouts: 0.69 us -> none  [call(): pl.pallas_call(kernel, out_shape=out_shape, in_specs=[spec] * len(args),...]
    all_to_all x2, waiting for transfers between devices: 15 us -> 14.3 us  [exchange(): out = lax.all_to_all(shaped, AXES, split_axis=0, concat_axis=0, tiled=True)]
    pallas_call x4, Pallas kernels: 5.81 us -> 6.33 us  [call(): pl.pallas_call(kernel, out_shape=out_shape, in_specs=[spec] * len(args),...]
  transfers between devices with their start and end apart: 2 -> 2, of which waited for: 2 -> 2; matrix products, arithmetic and copies ran while one was open for 3% -> 6% of each run, Pallas kernels for 4% -> 5%
where the time goes in v2:
time: 33.7 us; the launch traced here: 33.4 us
  waiting for transfers between devices  14.3 us (42%)
  starting transfers between devices  9.85 us (29%)
  Pallas kernels  6.33 us (19%)
  local copies, waits for them, and re-layouts  1.91 us (6%)
  other arithmetic  0.77 us (2%)
    all_to_all x2, waiting for transfers between devices, exchange(): out = lax.all_to_all(shaped, AXES, split_axis=0, concat_axis=0, tiled=True)  14.3 us
    all_to_all x2, starting transfers between devices, exchange(): out = lax.all_to_all(shaped, AXES, split_axis=0, concat_axis=0, tiled=True)  9.85 us
    pallas_call x4, Pallas kernels, call(): pl.pallas_call(kernel, out_shape=out_shape, in_specs=[spec] * len(args),...  6.33 us
    unnamed x21, local copies, waits for them, and re-layouts  1.91 us
    concatenate x1, other arithmetic, per_device(): jnp.concatenate([voltages.T[None], newton_steps.transpose(0, 2, 1)], axis=0)  0.77 us
  transfers between devices with their start and end apart: 2, of which 2 were waited for; matrix products, arithmetic and copies ran while one was open for 6% of the time, Pallas kernels for 5%

profile of v2, /device:TPU:0, one launch (start us, length us, event | category | flops | bytes accessed | tf_op | source)
XLA Modules:
  0.0 33.4 jit_solution(6867269057171339422)
XLA Ops:
  0.0 0.8 %pad_maximum_fusion.table_ref = f32[3,32,64]{2,1,0:T(8,128)S(1)} fusion(f32[2,32,64]{2,1,0:T(8,128)} %bitcast.19, f32[1,32,64]{2,1,0:T(8,128)} %bitcast.20), kind=kLoop, calls=%fused_computation | loop fusion | flops 6144 | bytes 49152 | tf_op jit(solution)/shard_map/concatenate | solution.py:318
  0.8 0.0 copy-start
  0.8 0.0 copy-start.1
  0.8 0.0 copy-start.2
  0.8 0.0 copy-start.3
  0.8 0.0 copy-start.4
  0.8 0.0 copy-start.5
  0.8 0.0 copy-start.6
  0.8 0.0 copy-start.7
  0.9 0.0 copy-start.8
  0.9 0.0 copy-start.9
  0.9 0.8 %shard_map.127 = bf16[1024,128]{1,0:T(8,128)(2,1)} custom-call(f32[3,32,64]{2,1,0:T(8,128)S(1)} %pad_maximum_fusion.table_ref), custom_call_target="tpu_custom_call" | custom-call | flops 20000000000 | bytes 1000000 | tf_op jit(solution)/shard_map/pallas_call | solution.py:281
  1.7 7.3 %all-to-all-start = ((bf16[32,32,128]{2,1,0:T(8,128)(2,1)}), bf16[32,32,128]{2,1,0:T(8,128)(2,1)S(1)}, u32[]{:S(2)}, u32[]{:S(2)}) async-start(bf16[32,32,128]{2,1,0:T(8,128)(2,1)} %bitcast.3), calls=%async_computation | async-start | bytes 524288 | tf_op jit(solution)/shard_map/all_to_all | solution.py:293
  9.0 0.0 copy-done
  9.0 0.0 copy-done.1
  9.0 0.0 copy-done.2
  9.0 0.0 copy-done.3
  9.0 0.0 copy-done.4
  9.0 0.0 copy-done.5
  9.0 0.0 copy-done.6
  9.1 0.0 copy-done.7
  9.1 0.0 copy-done.8
  9.1 0.0 copy-done.9
  9.1 1.7 %shard_map.128 = (f32[128,32]{1,0:T(8,128)S(1)}, s32[64,768]{1,0:T(8,128)S(1)}, f32[64,768]{1,0:T(8,128)S(1)}, f32[2,64,768]{2,1,0:T(8,128)S(1)}, bf16[2,64,768]...) custom-call(f32[3,32,64]{2,1,0:T(8,128)S(1)} %pad_maximum_fusion.table_r, ...), custom_call_target="tpu_custom_call" | custom-call | flops 20000000000 | bytes 1000000 | tf_op jit(solution)/shard_map/pallas_call | solution.py:281
  10.8 8.8 %all-to-all-done = bf16[32,32,128]{2,1,0:T(8,128)(2,1)S(1)} async-done(((bf16[32,32,128]{2,1,0:T(8,128)(2,1)}), bf16[32,32,128]{2,1,0:T(8,128)(2,1)S(1)}, u32[]{:S(2)}, u32[]{:S(2)}) %all-to-all-start) | async-done | bytes 262176 | tf_op jit(solution)/shard_map/all_to_all | solution.py:293
  19.6 2.4 %shard_map.129 = bf16[256,128]{1,0:T(8,128)(2,1)} custom-call(bf16[1024,128]{1,0:T(8,128)(2,1)S(1)} %bitcast.14, s32[64,768]{1,0:T(8,128)S(1)} %get-tuple-element.13.target_ref, f32[64,768]{1,0:T(8,128)S(1)} %get-tuple-element.14.gain_ref, f32[2,64,768]{2,1,0:T(8,128)S(1)} %get-tuple-element.15.near_ref, ...), custom_call_target="tpu_custom_call" | custom-call | flops 4000000000 | bytes 1000000 | tf_op jit(solution)/shard_map/pallas_call | solution.py:281
  22.0 2.6 %all-to-all-start.1 = ((bf16[32,8,128]{2,1,0:T(8,128)(2,1)}), bf16[32,8,128]{2,1,0:T(8,128)(2,1)S(1)}, u32[]{:S(2)}, u32[]{:S(2)}) async-start(bf16[32,8,128]{2,1,0:T(8,128)(2,1)} %bitcast.9), calls=%async_computation.1 | async-start | bytes 131072 | tf_op jit(solution)/shard_map/all_to_all | solution.py:293
  24.6 1.8 %copy.14.precond_ref = f32[64,64,32]{2,1,0:T(8,128)S(1)} copy(f32[64,64,32]{1,2,0:T(8,128)} %param.16) | data formatting | bytes 1048576 | tf_op args[3]
  26.4 5.6 %all-to-all-done.1 = bf16[32,8,128]{2,1,0:T(8,128)(2,1)S(1)} async-done(((bf16[32,8,128]{2,1,0:T(8,128)(2,1)}), bf16[32,8,128]{2,1,0:T(8,128)(2,1)S(1)}, u32[]{:S(2)}, u32[]{:S(2)}) %all-to-all-start.1) | async-done | bytes 65568 | tf_op jit(solution)/shard_map/all_to_all | solution.py:293
  32.0 1.4 %shard_map.130 = f32[2,32,64]{2,1,0:T(8,128)} custom-call(bf16[256,128]{1,0:T(8,128)(2,1)S(1)} %bitcast.13, f32[128,32]{1,0:T(8,128)S(1)} %get-tuple-element.20.inner_ref, f32[64,64,32]{2,1,0:T(8,128)S(1)} %copy.14.precond_ref), custom_call_target="tpu_custom_call" | custom-call | flops 100000000 | bytes 1000000 | tf_op jit(solution)/shard_map/pallas_call | solution.py:281
Async XLA Ops:
  0.8 8.2 %copy-start = (s32[64,768]{1,0:T(8,128)S(1)}, s32[64,768]{1,0:T(8,128)}, u32[]{:S(2)}) copy-start(s32[64,768]{1,0:T(8,128)} %source_ref.1) | copy-start | bytes 589828
  0.8 8.2 %copy-start.1 = (s32[64,768]{1,0:T(8,128)S(1)}, s32[64,768]{1,0:T(8,128)}, u32[]{:S(2)}) copy-start(s32[64,768]{1,0:T(8,128)} %target_ref.1) | copy-start | bytes 589828
  0.8 8.2 %copy-start.2 = (f32[64,768]{1,0:T(8,128)S(1)}, f32[64,768]{1,0:T(8,128)}, u32[]{:S(2)}) copy-start(f32[64,768]{1,0:T(8,128)} %gain_ref.1) | copy-start | bytes 589828
  0.8 8.2 %copy-start.3 = (s32[32,768]{1,0:T(8,128)S(1)}, s32[32,768]{1,0:T(8,128)}, u32[]{:S(2)}) copy-start(s32[32,768]{1,0:T(8,128)} %inner_source_ref.1) | copy-start | bytes 294916
  0.8 8.2 %copy-start.4 = (s32[32,768]{1,0:T(8,128)S(1)}, s32[32,768]{1,0:T(8,128)}, u32[]{:S(2)}) copy-start(s32[32,768]{1,0:T(8,128)} %inner_target_ref.1) | copy-start | bytes 294916
  0.8 8.2 %copy-start.5 = (f32[32,768]{1,0:T(8,128)S(1)}, f32[32,768]{1,0:T(8,128)}, u32[]{:S(2)}) copy-start(f32[32,768]{1,0:T(8,128)} %inner_gain_ref.1) | copy-start | bytes 294916
  0.8 8.2 %copy-start.6 = (f32[64,32]{0,1:T(8,128)S(1)}, f32[64,32]{0,1:T(8,128)}, u32[]{:S(2)}) copy-start(f32[64,32]{0,1:T(8,128)} %param.15) | copy-start | bytes 24580
  0.8 8.2 %copy-start.7 = (s32[64]{0:T(128)S(1)}, s32[64]{0:T(128)}, u32[]{:S(2)}) copy-start(s32[64]{0:T(128)} %param.17) | copy-start | bytes 772
  0.9 8.2 %copy-start.8 = (s32[64,1]{0,1:T(1,128)S(1)}, s32[64,1]{0,1:T(1,128)}, u32[]{:S(2)}) copy-start(s32[64,1]{0,1:T(1,128)} %param.18) | copy-start | bytes 772
  0.9 8.2 %copy-start.9 = (s32[64]{0:T(128)S(1)}, s32[64]{0:T(128)}, u32[]{:S(2)}) copy-start(s32[64]{0:T(128)} %param.19) | copy-start | bytes 772
  1.7 17.9 %all-to-all-start = ((bf16[32,32,128]{2,1,0:T(8,128)(2,1)}), bf16[32,32,128]{2,1,0:T(8,128)(2,1)S(1)}, u32[]{:S(2)}, u32[]{:S(2)}) async-start(bf16[32,32,128]{2,1,0:T(8,128)(2,1)} %bitcast.3), calls=%async_computation | async-start | bytes 524288 | tf_op jit(solution)/shard_map/all_to_all | solution.py:293
  22.0 10.0 %all-to-all-start.1 = ((bf16[32,8,128]{2,1,0:T(8,128)(2,1)}), bf16[32,8,128]{2,1,0:T(8,128)(2,1)S(1)}, u32[]{:S(2)}, u32[]{:S(2)}) async-start(bf16[32,8,128]{2,1,0:T(8,128)(2,1)} %bitcast.9), calls=%async_computation.1 | async-start | bytes 131072 | tf_op jit(solution)/shard_map/all_to_all | solution.py:293

commit v3 on v2

--- a/solution.py
+++ b/solution.py
@@ -54,9 +54,8 @@
     return jnp.concatenate([jnp.where(m, v, zero) for v in values for m in masks], axis=0)
 
 
-def same_block(rows, columns):
-    shape = (rows, columns)
-    return (iota(shape, 0) % GROUP) == (iota(shape, 1) % GROUP)
+def same_block(shape, group):
+    return (iota(shape, 0) % group) == (iota(shape, 1) % group)
 
 
 def gather_nodes(spread):
@@ -93,10 +92,15 @@
 
 
 def prepare_kernel(table_ref, send_ref):
-    packed = fields_of(table_ref).astype(BF16)
-    block_count = packed.shape[0]
-    for d in range(send_ref.shape[0] // block_count):
-        send_ref[pl.ds(d * block_count, block_count), :] = packed
+    block_count = table_ref.shape[1]
+    half = block_count // 2
+    first = table_ref[0]
+    packed = [
+        jnp.concatenate([field[:half], field[half:]], axis=1).astype(BF16)
+        for field in (first, first + table_ref[1])
+    ]
+    for d in range(send_ref.shape[0] // half):
+        send_ref[pl.ds(d * half, half), :] = packed[d % NEWTON]
 
 
 def inner_images(volt_rows, update_rows, cap_rows, source_ref, target_ref, gain_ref):
@@ -130,8 +134,8 @@
             left = jnp.concatenate(left, axis=1)
             acc_ones = acc_ones + dot(left, jnp.concatenate(right_ones, axis=1), NT)
             acc = acc + dot(left, jnp.concatenate(right, axis=1), NT)
-        acc = jnp.where(same_block(*acc.shape), acc, 0.0)
-        acc_ones = jnp.where(same_block(*acc_ones.shape), acc_ones, 0.0)
+        acc = jnp.where(same_block(acc.shape, GROUP), acc, 0.0)
+        acc_ones = jnp.where(same_block(acc_ones.shape, GROUP), acc_ones, 0.0)
         diagonal = fold_rows(
             sum(dot(p, nodes_any[: DIGIT * GROUP], NN) for p in split(acc_ones, 2))
         )
@@ -147,20 +151,28 @@
     return jnp.sum(jnp.where(iota(shape, 0) == iota(shape, 1), row, 0), axis=1, keepdims=True)
 
 
-def local_kernel(
+def inner_kernel(
+    table_ref, cap_ref, inner_source_ref, inner_target_ref, inner_gain_ref, inner_ref
+):
+    updates = jnp.concatenate([table_ref[1], table_ref[2]], axis=1).astype(BF16).astype(F32)
+    caps = jnp.concatenate([cap_ref[...], cap_ref[...]], axis=1)
+    inner_ref[...] = inner_images(
+        fields_of(table_ref), updates, caps, inner_source_ref, inner_target_ref, inner_gain_ref
+    ).T
+
+
+def stamp_kernel(
     per_owner,
+    facts_ref,
+    facts_other,
     table_ref,
-    cap_ref,
-    block_ref,
-    owner_ref,
-    offset_ref,
-    inner_source_ref,
-    inner_target_ref,
-    inner_gain_ref,
+    table_other,
     source_ref,
+    source_other,
     target_ref,
+    target_other,
     gain_ref,
-    inner_ref,
+    gain_other,
     target_out,
     gain_out,
     near_ref,
@@ -169,48 +181,58 @@
     place_ref,
     offset_hot_ref,
 ):
-    stamp_count, elements = source_ref.shape
+    own_count, elements = source_ref.shape
+    stamp_count = 2 * own_count
     block_count = table_ref.shape[1]
-    target_out[...] = target_ref[...]
-    gain_out[...] = gain_ref[...]
-    volt_rows = fields_of(table_ref)
-    updates = jnp.concatenate([table_ref[1], table_ref[2]], axis=1).astype(BF16)
-    caps = jnp.concatenate([cap_ref[...], cap_ref[...]], axis=1)
-
-    owner_row = owner_ref[...].astype(F32)
+    half = block_count // 2
+    later = lax.axis_index("sub") == 1
+    tables = []
+    for ref in (table_ref, table_other):
+        field = jnp.where(later, ref[0] + ref[1], ref[0])
+        update = jnp.where(later, ref[2], ref[1]).astype(BF16).astype(F32)
+        tables.append(jnp.concatenate([field, update], axis=1))
+    tables = jnp.concatenate(tables, axis=0)
+
+    facts = jnp.concatenate([facts_ref[...], facts_other[...]], axis=1).astype(F32)
+    block_row, owner_row, offset_row = facts[0:1], facts[1:2], facts[2:3]
+    mine = iota((1, stamp_count), 1) < own_count
+    block = row_to_column(jnp.where(mine, block_row, block_row + block_count))
     owner = row_to_column(owner_row)
-    offset = row_to_column(offset_ref[...].astype(F32))
-    block = row_to_column(block_ref[...].astype(F32))
-    row_hot = iota(row_hot_ref.shape, 1).astype(F32) == owner * block_count + offset
+    offset = row_to_column(offset_row)
+    place_in_half = jnp.where(offset < half, offset, offset - half)
+    row_hot = iota(row_hot_ref.shape, 1).astype(F32) == owner * half + place_in_half
     row_hot_ref[...] = row_hot.astype(F32).astype(BF16)
     shape = (stamp_count, stamp_count)
-    earlier = (owner == owner_row) & (iota(shape, 0) < iota(shape, 1))
+    row, column = iota(shape, 0), iota(shape, 1)
+    earlier = (owner == owner_row) & (row < column) & ((row < own_count) == (column < own_count))
     rank_row = jnp.sum(jnp.where(earlier, 1.0, 0.0), axis=0, keepdims=True)
-    slot_row = (owner_row * per_owner + rank_row) * NEWTON
-    slots = jnp.concatenate([slot_row + t for t in range(NEWTON)], axis=1)
-    place_ref[...] = (iota(place_ref.shape, 0).astype(F32) == slots).astype(F32).astype(BF16)
+    rank_row = jnp.where(mine, rank_row, rank_row + per_owner)
+    slot_row = owner_row * (2 * per_owner) + rank_row
+    place = iota(place_ref.shape, 0).astype(F32) == slot_row
+    place_ref[...] = place.astype(F32).astype(BF16)
     offset_hot_ref[...] = jnp.where(
         iota(offset_hot_ref.shape, 1).astype(F32) == offset, 1.0, 0.0
     )
 
-    block_hot = (iota((stamp_count, block_count), 1).astype(F32) == block).astype(F32).astype(BF16)
-    local = sum(dot(block_hot, p, NN) for p in split(volt_rows, 3))
-    moved = dot(block_hot, updates, NN)
-    for start in range(0, stamp_count, GROUP):
-        rows = slice(start, start + GROUP)
+    block_hot = iota((stamp_count, 2 * block_count), 1).astype(F32) == block
+    block_hot = block_hot.astype(F32).astype(BF16)
+    local = sum(dot(block_hot, p, NN) for p in split(tables, 3))
+    for n, (sources, targets, gains) in enumerate(
+        ((source_ref, target_ref, gain_ref), (source_other, target_other, gain_other))
+    ):
+        held = slice(n * own_count, (n + 1) * own_count)
+        target_out[held, :] = targets[...]
+        gain_out[held, :] = gains[...]
+        near = local[held]
         for at in range(0, elements, LANES):
             lanes = slice(at, at + LANES)
-            source = source_ref[rows, lanes]
-            for t in range(NEWTON):
-                here = source + t * BS
-                near_ref[t, rows, lanes] = pick(local[rows], here)
-                moved_ref[t, rows, lanes] = pick(moved[rows], here).astype(BF16)
-    inner_ref[...] = inner_images(
-        volt_rows, updates.astype(F32), caps, inner_source_ref, inner_target_ref, inner_gain_ref
-    ).T
+            source = sources[:, lanes]
+            near_ref[held, lanes] = pick(near, source)
+            moved_ref[held, lanes] = pick(near, source + BS).astype(BF16)
 
 
 def couple_kernel(
+    half,
     fields_ref,
     target_ref,
     gain_ref,
@@ -222,50 +244,54 @@
     send_ref,
 ):
     stamp_count, elements = target_ref.shape
+    group = NEWTON * GROUP
+    offset_hot = offset_hot_ref[...]
+    lane = iota(offset_hot.shape, 1)
     remote = dot(row_hot_ref[...], fields_ref[...], NN)
-    nodes_step = gather_nodes(True)
+    upper = jnp.sum(
+        jnp.where(lane >= half, offset_hot, 0.0), axis=1, keepdims=True
+    )
+    remote = jnp.where(upper > 0.5, pltpu.roll(remote, BS, 1), remote)
+    shape = (DIGIT * group, LANES)
+    node = iota(shape, 1) - BS
+    nodes = (node >= 0) & (node % DIGIT == iota(shape, 0) // group)
+    nodes = nodes.astype(F32).astype(BF16)
+    high_lane = (iota((group, LANES), 1) - BS) // DIGIT
     images = []
-    for start in range(0, stamp_count, GROUP):
-        rows = slice(start, start + GROUP)
+    for start in range(0, stamp_count, group):
+        rows = slice(start, start + group)
         far = remote[rows]
-        acc = jnp.zeros((NEWTON * DIGIT * GROUP, NEWTON * DIGIT * GROUP), F32)
+        acc = jnp.zeros((DIGIT * group, DIGIT * group), F32)
         left, right = [], []
         for at in range(0, elements, LANES):
             lanes = slice(at, at + LANES)
             target = target_ref[rows, lanes]
-            gain = -gain_ref[rows, lanes]
-            weights = [
-                conductance(gain, near_ref[t, rows, lanes], pick(far, target + t * BS)).astype(BF16)
-                for t in range(NEWTON)
-            ]
+            weight = conductance(-gain_ref[rows, lanes], near_ref[rows, lanes], pick(far, target))
             high, low = digits(target)
-            left.append(hot_rows(high, weights))
-            right.append(hot_rows(low, [moved_ref[t, rows, lanes] for t in range(NEWTON)]))
+            left.append(hot_rows(high, [weight.astype(BF16)]))
+            right.append(hot_rows(low, [moved_ref[rows, lanes]]))
             if len(left) == 2 or at + LANES >= elements:
                 acc = acc + dot(
                     jnp.concatenate(left, axis=1), jnp.concatenate(right, axis=1), NT
                 )
                 left, right = [], []
-        acc = jnp.where(same_block(*acc.shape), acc, 0.0).astype(BF16)
-        images.append(fold_rows(dot(acc, nodes_step, NN)))
+        acc = jnp.where(same_block(acc.shape, group), acc, 0.0).astype(BF16)
+        wide = dot(acc, nodes, NN)
+        total = jnp.zeros((group, LANES), F32)
+        for h in range(DIGIT):
+            total = total + jnp.where(high_lane == h, wide[h * group : (h + 1) * group], 0.0)
+        images.append(total)
     images = jnp.concatenate(images, axis=0)
-    lane = iota(images.shape, 1)
-    messages = jnp.concatenate(
-        [
-            jnp.where(lane < BS, offset_hot_ref[...], pltpu.roll(images, BS, 1)),
-            jnp.where(lane < BS, offset_hot_ref[...], images),
-        ],
-        axis=0,
-    ).astype(BF16)
+    messages = jnp.where(lane < BS, offset_hot, images).astype(BF16)
     send_ref[...] = dot(place_ref[...], messages, NN).astype(BF16)
 
 
-def finish_kernel(images_ref, inner_ref, precond_ref, out_ref):
+def finish_kernel(row_count, images_ref, inner_ref, precond_ref, out_ref):
     received = images_ref[...]
     block_count = inner_ref.shape[1]
-    parity = iota(received.shape, 0) % NEWTON
+    step = iota(received.shape, 0) // row_count % NEWTON
     for t in range(NEWTON):
-        mine = jnp.where(parity == t, received.astype(F32), 0.0).astype(BF16)
+        mine = jnp.where(step == t, received.astype(F32), 0.0).astype(BF16)
         couple = dot(received, mine, TN)[BS:, :block_count]
         total = inner_ref[t * BS : (t + 1) * BS, :] + couple
         rows = [
@@ -315,44 +341,45 @@
     per_owner = max(2, 2 * stamp_count // devices)
     row_count = devices * per_owner * NEWTON
     like = jax.ShapeDtypeStruct
+    swap = lambda array: lax.ppermute(array, "sub", [(0, 1), (1, 0)])
     table = jnp.concatenate([voltages.T[None], newton_steps.transpose(0, 2, 1)], axis=0)
     send = call(
-        prepare_kernel, like((devices * block_count, LANES), BF16), (table,), 2 * 10**10
+        prepare_kernel, like((devices * block_count // 2, LANES), BF16), (table,), 2 * 10**10
     )
     fields = exchange(send, devices)
-    inner, *prepared = call(
-        functools.partial(local_kernel, per_owner),
+    inner = call(
+        inner_kernel,
+        like((NEWTON * BS, block_count), F32),
+        (table, cap_diag.T, inner_source, inner_target, inner_gain),
+        4 * 10**9,
+    )
+    facts = [fact.reshape(1, stamp_count) for fact in (couple_block, couple_owner, couple_offset)]
+    wanted = (jnp.concatenate(facts, axis=0), table, couple_source, couple_target, couple_gain)
+    pairs = [half for array in wanted for half in (array, swap(array))]
+    both = 2 * stamp_count
+    prepared = call(
+        functools.partial(stamp_kernel, per_owner),
         [
-            like((NEWTON * BS, block_count), F32),
-            like(couple_target.shape, couple_target.dtype),
-            like(couple_gain.shape, couple_gain.dtype),
-            like((NEWTON, stamp_count, elements), F32),
-            like((NEWTON, stamp_count, elements), BF16),
-            like((stamp_count, devices * block_count), BF16),
-            like((row_count, NEWTON * stamp_count), BF16),
-            like((stamp_count, LANES), F32),
+            like((both, elements), couple_target.dtype),
+            like((both, elements), couple_gain.dtype),
+            like((both, elements), F32),
+            like((both, elements), BF16),
+            like((both, devices * block_count // 2), BF16),
+            like((row_count, both), BF16),
+            like((both, LANES), F32),
         ],
-        (
-            table,
-            cap_diag.T,
-            couple_block.reshape(1, stamp_count),
-            couple_owner.reshape(1, stamp_count),
-            couple_offset.reshape(1, stamp_count),
-            inner_source,
-            inner_target,
-            inner_gain,
-            couple_source,
-            couple_target,
-            couple_gain,
-        ),
-        2 * 10**10,
+        pairs,
+        10**8,
     )
     images = call(
-        couple_kernel, like((row_count, LANES), BF16), (fields, *prepared), 4 * 10**9
+        functools.partial(couple_kernel, block_count // 2),
+        like((row_count, LANES), BF16),
+        (fields, *prepared),
+        4 * 10**9,
     )
     received = exchange(images, devices)
     out = call(
-        finish_kernel,
+        functools.partial(finish_kernel, 2 * per_owner),
         like((NEWTON, block_count, BS), F32),
         (received, inner, preconditioner),
         10**8,

time: 33.7 us -> 31.2 us (0.926)
  waiting for transfers between devices: 14.3 us -> 10.9 us
  starting transfers between devices: 9.85 us -> 11.3 us
  local copies, waits for them, and re-layouts: 1.91 us -> 0.68 us
  Pallas kernels: 6.33 us -> 7.16 us
    all_to_all x2, waiting for transfers between devices: 14.3 us -> 9.96 us  [exchange(): out = lax.all_to_all(shaped, AXES, split_axis=0, concat_axis=0, tiled=True)]
    ppermute x0 -> x5, starting transfers between devices: none -> 1.4 us  [per_device(): swap = lambda array: lax.ppermute(array, 'sub', [(0, 1), (1, 0)])]
    unnamed x21 -> x23, local copies, waits for them, and re-layouts: 1.91 us -> 0.68 us
    ppermute x0 -> x5, waiting for transfers between devices: none -> 0.92 us  [per_device(): swap = lambda array: lax.ppermute(array, 'sub', [(0, 1), (1, 0)])]
    pallas_call x4 -> x5, Pallas kernels: 6.33 us -> 7.16 us  [call(): pl.pallas_call(kernel, out_shape=out_shape, in_specs=[spec] * len(args),...]
  transfers between devices with their start and end apart: 2 -> 7, of which waited for: 2 -> 3; matrix products, arithmetic and copies ran while one was open for 6% -> 2% of each run, Pallas kernels for 5% -> 8%
where the time goes in v3:
time: 31.2 us; the launch traced here: 30.9 us
  starting transfers between devices  11.3 us (36%)
  waiting for transfers between devices  10.9 us (35%)
  Pallas kernels  7.16 us (23%)
  other arithmetic  0.78 us (2%)
  local copies, waits for them, and re-layouts  0.68 us (2%)
    all_to_all x2, waiting for transfers between devices, exchange(): out = lax.all_to_all(shaped, AXES, split_axis=0, concat_axis=0, tiled=True)  9.96 us
    all_to_all x2, starting transfers between devices, exchange(): out = lax.all_to_all(shaped, AXES, split_axis=0, concat_axis=0, tiled=True)  9.86 us
    pallas_call x5, Pallas kernels, call(): pl.pallas_call(kernel, out_shape=out_shape, in_specs=[spec] * len(args),...  7.16 us
    ppermute x5, starting transfers between devices, per_device(): swap = lambda array: lax.ppermute(array, 'sub', [(0, 1), (1, 0)])  1.4 us
    ppermute x5, waiting for transfers between devices, per_device(): swap = lambda array: lax.ppermute(array, 'sub', [(0, 1), (1, 0)])  0.92 us
    concatenate x1, other arithmetic, per_device(): jnp.concatenate([voltages.T[None], newton_steps.transpose(0, 2, 1)], axis=0)  0.77 us
    unnamed x23, local copies, waits for them, and re-layouts  0.68 us
  transfers between devices with their start and end apart: 7, of which 3 were waited for; matrix products, arithmetic and copies ran while one was open for 2% of the time, Pallas kernels for 8%

profile of v3, /device:TPU:0, one launch (start us, length us, event | category | flops | bytes accessed | tf_op | source)
XLA Modules:
  0.0 30.9 jit_solution(9062887714536636628)
XLA Ops:
  0.0 0.8 %pad_maximum_fusion.table_ref = f32[3,32,64]{2,1,0:T(8,128)S(1)} fusion(f32[2,32,64]{2,1,0:T(8,128)} %bitcast.16, f32[1,32,64]{2,1,0:T(8,128)} %bitcast.17), kind=kLoop, calls=%fused_computation | loop fusion | flops 6144 | bytes 49152 | tf_op jit(solution)/shard_map/concatenate | solution.py:345
  0.8 0.0 copy-start
  0.8 0.0 copy-start.1
  0.8 0.0 copy-start.2
  0.8 0.0 copy-start.8
  0.8 0.0 copy-start.9
  0.8 0.0 copy-start.10
  0.8 0.7 %shard_map.127 = bf16[512,128]{1,0:T(8,128)(2,1)} custom-call(f32[3,32,64]{2,1,0:T(8,128)S(1)} %pad_maximum_fusion.table_ref), custom_call_target="tpu_custom_call" | custom-call | flops 20000000000 | bytes 1000000 | tf_op jit(solution)/shard_map/pallas_call | solution.py:307
  1.6 7.3 %all-to-all-start = ((bf16[32,16,128]{2,1,0:T(8,128)(2,1)}), bf16[32,16,128]{2,1,0:T(8,128)(2,1)S(1)}, u32[]{:S(2)}, u32[]{:S(2)}) async-start(bf16[32,16,128]{2,1,0:T(8,128)(2,1)} %bitcast.3), calls=%async_computation | async-start | bytes 262144 | tf_op jit(solution)/shard_map/all_to_all | solution.py:319
  8.9 0.0 copy-done
  8.9 0.3 %collective-permute-start.2 = (s32[64,768]{1,0:T(8,128)S(1)}, s32[64,768]{1,0:T(8,128)S(1)}, u32[]{:S(2)}, u32[]{:S(2)}) collective-permute-start(s32[64,768]{1,0:T(8,128)S(1)} %copy-done), channel_id=1, source_target_pairs={{0,1},{1,0},{2,3},{3,2},{4,5},{5,4},{6,7},{7,6},{8,9},{9,8},{10,11... | collective-permute-start | bytes 589832 | tf_op jit(solution)/shard_map/ppermute | solution.py:344
  9.2 0.0 copy-done.1
  9.2 0.3 collective-permute-start.3
  9.5 0.0 copy-done.2
  9.5 0.3 collective-permute-start.4
  9.7 0.3 collective-permute-start.1
  10.0 0.0 copy-done.8
  10.0 0.0 copy-done.9
  10.0 0.0 copy-done.10
  10.0 0.3 %collective-permute-start = (s32[3,64]{1,0:T(4,128)S(1)}, s32[3,64]{1,0:T(4,128)S(1)}, u32[]{:S(2)}, u32[]{:S(2)}) collective-permute-start(s32[3,64]{1,0:T(4,128)S(1)} %pad_add_fusion.facts_ref), channel_id=1, source_target_pairs={{0,1},{1,0},{2,3},{3,2},{4,5},{5,4},{6,7},{7,6},{8,9},{9,8},{10,11... | collective-permute-start | bytes 2312 | tf_op jit(solution)/shard_map/ppermute | solution.py:344
  10.3 0.9 %collective-permute-done.facts_other = s32[3,64]{1,0:T(4,128)S(1)} collective-permute-done((s32[3,64]{1,0:T(4,128)S(1)}, s32[3,64]{1,0:T(4,128)S(1)}, u32[]{:S(2)}, u32[]{:S(2)}) %collective-permute-start) | collective-permute-done | bytes 800 | tf_op jit(solution)/shard_map/ppermute | solution.py:344
  11.2 0.0 collective-permute-done.1.table_other
  11.2 0.0 collective-permute-done.2.source_other
  11.2 0.0 collective-permute-done.3.target_other
  11.2 0.0 collective-permute-done.4.gain_other
  11.2 1.0 %shard_map.128 = (s32[128,768]{1,0:T(8,128)S(1)}, f32[128,768]{1,0:T(8,128)S(1)}, f32[128,768]{1,0:T(8,128)S(1)}, bf16[128,768]{1,0:T(8,128)(2,1)S(1)}, bf16[128...) custom-call(s32[3,64]{1,0:T(4,128)S(1)} %pad_add_fusion.facts_ref, ...), custom_call_target="tpu_custom_call" | custom-call | flops 100000000 | bytes 1000000 | tf_op jit(solution)/shard_map/pallas_call | solution.py:307
  12.2 4.9 %all-to-all-done = bf16[32,16,128]{2,1,0:T(8,128)(2,1)S(1)} async-done(((bf16[32,16,128]{2,1,0:T(8,128)(2,1)}), bf16[32,16,128]{2,1,0:T(8,128)(2,1)S(1)}, u32[]{:S(2)}, u32[]{:S(2)}) %all-to-all-start) | async-done | bytes 131104 | tf_op jit(solution)/shard_map/all_to_all | solution.py:319
  17.1 0.0 copy-start.3
  17.1 0.0 copy-start.4
  17.1 0.0 copy-start.5
  17.1 0.0 copy-start.6
  17.1 2.4 %shard_map.129 = bf16[256,128]{1,0:T(8,128)(2,1)} custom-call(bf16[512,128]{1,0:T(8,128)(2,1)S(1)} %bitcast.14, s32[128,768]{1,0:T(8,128)S(1)} %get-tuple-element.12.target_ref, f32[128,768]{1,0:T(8,128)S(1)} %get-tuple-element.13.gain_ref, f32[128,768]{1,0:T(8,128)S(1)} %get-tuple-element.14.near_ref, bf16[128,768]{1,0:T(8,128)(2,1)S(1)} %get-tuple-element.15.moved_ref, ...), custom_call_target="tpu_custom_call" | custom-call | flops 4000000000 | bytes 1000000 | tf_op jit(solution)/shard_map/pallas_call | solution.py:307
  19.5 2.6 %all-to-all-start.1 = ((bf16[32,8,128]{2,1,0:T(8,128)(2,1)}), bf16[32,8,128]{2,1,0:T(8,128)(2,1)S(1)}, u32[]{:S(2)}, u32[]{:S(2)}) async-start(bf16[32,8,128]{2,1,0:T(8,128)(2,1)} %bitcast.8), calls=%async_computation.1 | async-start | bytes 131072 | tf_op jit(solution)/shard_map/all_to_all | solution.py:319
  22.1 0.0 copy-done.3
  22.1 0.0 copy-done.4
  22.1 0.0 copy-done.5
  22.1 0.0 copy-done.6
  22.1 0.0 copy-start.7
  22.1 1.6 %shard_map.130.inner_ref = f32[128,32]{1,0:T(8,128)S(1)} custom-call(f32[3,32,64]{2,1,0:T(8,128)S(1)} %pad_maximum_fusion.table_ref, f32[32,64]{1,0:T(8,128)S(1)} %bitcast.15, s32[32,768]{1,0:T(8,128)S(1)} %copy-done.3, s32[32,768]{1,0:T(8,128)S(1)} %copy-done.4, f32[32,768]{1,0:T(8,128)S(1)} %copy-done.5), custom_call_target="tpu_custom_call" | custom-call | flops 4000000000 | bytes 1000000 | tf_op jit(solution)/shard_map/pallas_call | solution.py:307
  23.8 0.0 copy-done.7
  23.8 0.6 %copy.14.precond_ref = f32[64,64,32]{2,1,0:T(8,128)S(1)} copy(f32[64,64,32]{1,2,0:T(8,128)S(1)} %copy-done.7) | data formatting | bytes 1048576 | tf_op args[3]
  24.4 5.1 %all-to-all-done.1 = bf16[32,8,128]{2,1,0:T(8,128)(2,1)S(1)} async-done(((bf16[32,8,128]{2,1,0:T(8,128)(2,1)}), bf16[32,8,128]{2,1,0:T(8,128)(2,1)S(1)}, u32[]{:S(2)}, u32[]{:S(2)}) %all-to-all-start.1) | async-done | bytes 65568 | tf_op jit(solution)/shard_map/all_to_all | solution.py:319
  29.5 1.4 %shard_map.131 = f32[2,32,64]{2,1,0:T(8,128)} custom-call(bf16[256,128]{1,0:T(8,128)(2,1)S(1)} %bitcast.13, f32[128,32]{1,0:T(8,128)S(1)} %shard_map.130.inner_ref, f32[64,64,32]{2,1,0:T(8,128)S(1)} %copy.14.precond_ref), custom_call_target="tpu_custom_call" | custom-call | flops 100000000 | bytes 1000000 | tf_op jit(solution)/shard_map/pallas_call | solution.py:307
  (1 shorter events, 0.0 us)
Async XLA Ops:
  0.8 8.1 %copy-start = (s32[64,768]{1,0:T(8,128)S(1)}, s32[64,768]{1,0:T(8,128)}, u32[]{:S(2)}) copy-start(s32[64,768]{1,0:T(8,128)} %source_ref.1) | copy-start | bytes 589828
  0.8 8.4 %copy-start.1 = (s32[64,768]{1,0:T(8,128)S(1)}, s32[64,768]{1,0:T(8,128)}, u32[]{:S(2)}) copy-start(s32[64,768]{1,0:T(8,128)} %target_ref.1) | copy-start | bytes 589828
  0.8 8.7 %copy-start.2 = (f32[64,768]{1,0:T(8,128)S(1)}, f32[64,768]{1,0:T(8,128)}, u32[]{:S(2)}) copy-start(f32[64,768]{1,0:T(8,128)} %gain_ref.1) | copy-start | bytes 589828
  0.8 9.2 %copy-start.8 = (s32[64]{0:T(128)S(1)}, s32[64]{0:T(128)}, u32[]{:S(2)}) copy-start(s32[64]{0:T(128)} %param.19) | copy-start | bytes 772
  0.8 9.2 %copy-start.9 = (s32[64,1]{0,1:T(1,128)S(1)}, s32[64,1]{0,1:T(1,128)}, u32[]{:S(2)}) copy-start(s32[64,1]{0,1:T(1,128)} %param.18) | copy-start | bytes 772
  0.8 9.2 %copy-start.10 = (s32[64]{0:T(128)S(1)}, s32[64]{0:T(128)}, u32[]{:S(2)}) copy-start(s32[64]{0:T(128)} %param.17) | copy-start | bytes 772
  1.6 15.5 %all-to-all-start = ((bf16[32,16,128]{2,1,0:T(8,128)(2,1)}), bf16[32,16,128]{2,1,0:T(8,128)(2,1)S(1)}, u32[]{:S(2)}, u32[]{:S(2)}) async-start(bf16[32,16,128]{2,1,0:T(8,128)(2,1)} %bitcast.3), calls=%async_computation | async-start | bytes 262144 | tf_op jit(solution)/shard_map/all_to_all | solution.py:319
  8.9 2.3 %collective-permute-start.2 = (s32[64,768]{1,0:T(8,128)S(1)}, s32[64,768]{1,0:T(8,128)S(1)}, u32[]{:S(2)}, u32[]{:S(2)}) collective-permute-start(s32[64,768]{1,0:T(8,128)S(1)} %copy-done), channel_id=1, source_target_pairs={{0,1},{1,0},{2,3},{3,2},{4,5},{5,4},{6,7},{7,6},{8,9},{9,8},{10,11... | collective-permute-start | bytes 589832 | tf_op jit(solution)/shard_map/ppermute | solution.py:344
  9.2 2.0 %collective-permute-start.3 = (s32[64,768]{1,0:T(8,128)S(1)}, s32[64,768]{1,0:T(8,128)S(1)}, u32[]{:S(2)}, u32[]{:S(2)}) collective-permute-start(s32[64,768]{1,0:T(8,128)S(1)} %copy-done.1), channel_id=1, source_target_pairs={{0,1},{1,0},{2,3},{3,2},{4,5},{5,4},{6,7},{7,6},{8,9},{9,8},{10,11... | collective-permute-start | bytes 589832 | tf_op jit(solution)/shard_map/ppermute | solution.py:344
  9.5 1.8 %collective-permute-start.4 = (f32[64,768]{1,0:T(8,128)S(1)}, f32[64,768]{1,0:T(8,128)S(1)}, u32[]{:S(2)}, u32[]{:S(2)}) collective-permute-start(f32[64,768]{1,0:T(8,128)S(1)} %copy-done.2), channel_id=1, source_target_pairs={{0,1},{1,0},{2,3},{3,2},{4,5},{5,4},{6,7},{7,6},{8,9},{9,8},{10,11... | collective-permute-start | bytes 589832 | tf_op jit(solution)/shard_map/ppermute | solution.py:344
  9.7 1.5 %collective-permute-start.1 = (f32[3,32,64]{2,1,0:T(8,128)S(1)}, f32[3,32,64]{2,1,0:T(8,128)S(1)}, u32[]{:S(2)}, u32[]{:S(2)}) collective-permute-start(f32[3,32,64]{2,1,0:T(8,128)S(1)} %pad_maximum_fusion.table_ref), channel_id=1, source_target_pairs={{0,1},{1,0},{2,3},{3,2},{4,5},{5,4},{6,7},{7,6},{8,9},{9,8},{10,11... | collective-permute-start | bytes 73736 | tf_op jit(solution)/shard_map/ppermute | solution.py:344
  10.0 1.2 %collective-permute-start = (s32[3,64]{1,0:T(4,128)S(1)}, s32[3,64]{1,0:T(4,128)S(1)}, u32[]{:S(2)}, u32[]{:S(2)}) collective-permute-start(s32[3,64]{1,0:T(4,128)S(1)} %pad_add_fusion.facts_ref), channel_id=1, source_target_pairs={{0,1},{1,0},{2,3},{3,2},{4,5},{5,4},{6,7},{7,6},{8,9},{9,8},{10,11... | collective-permute-start | bytes 2312 | tf_op jit(solution)/shard_map/ppermute | solution.py:344
  17.1 5.0 %copy-start.3 = (s32[32,768]{1,0:T(8,128)S(1)}, s32[32,768]{1,0:T(8,128)}, u32[]{:S(2)}) copy-start(s32[32,768]{1,0:T(8,128)} %inner_source_ref.1) | copy-start | bytes 294916
  17.1 5.0 %copy-start.4 = (s32[32,768]{1,0:T(8,128)S(1)}, s32[32,768]{1,0:T(8,128)}, u32[]{:S(2)}) copy-start(s32[32,768]{1,0:T(8,128)} %inner_target_ref.1) | copy-start | bytes 294916
  17.1 5.0 %copy-start.5 = (f32[32,768]{1,0:T(8,128)S(1)}, f32[32,768]{1,0:T(8,128)}, u32[]{:S(2)}) copy-start(f32[32,768]{1,0:T(8,128)} %inner_gain_ref.1) | copy-start | bytes 294916
  17.1 5.0 %copy-start.6 = (f32[64,32]{0,1:T(8,128)S(1)}, f32[64,32]{0,1:T(8,128)}, u32[]{:S(2)}) copy-start(f32[64,32]{0,1:T(8,128)} %param.15) | copy-start | bytes 24580
  19.5 10.0 %all-to-all-start.1 = ((bf16[32,8,128]{2,1,0:T(8,128)(2,1)}), bf16[32,8,128]{2,1,0:T(8,128)(2,1)S(1)}, u32[]{:S(2)}, u32[]{:S(2)}) async-start(bf16[32,8,128]{2,1,0:T(8,128)(2,1)} %bitcast.8), calls=%async_computation.1 | async-start | bytes 131072 | tf_op jit(solution)/shard_map/all_to_all | solution.py:319
  22.1 1.7 %copy-start.7 = (f32[64,64,32]{1,2,0:T(8,128)S(1)}, f32[64,64,32]{1,2,0:T(8,128)}, u32[]{:S(2)}) copy-start(f32[64,64,32]{1,2,0:T(8,128)} %param.16) | copy-start | bytes 1572868

commit v4 on v3

--- a/solution.py
+++ b/solution.py
@@ -152,7 +152,12 @@
 
 
 def inner_kernel(
-    table_ref, cap_ref, inner_source_ref, inner_target_ref, inner_gain_ref, inner_ref
+    table_ref,
+    cap_ref,
+    inner_source_ref,
+    inner_target_ref,
+    inner_gain_ref,
+    inner_ref,
 ):
     updates = jnp.concatenate([table_ref[1], table_ref[2]], axis=1).astype(BF16).astype(F32)
     caps = jnp.concatenate([cap_ref[...], cap_ref[...]], axis=1)
@@ -176,7 +181,7 @@
     target_out,
     gain_out,
     near_ref,
-    moved_ref,
+    right_ref,
     row_hot_ref,
     place_ref,
     offset_hot_ref,
@@ -185,6 +190,7 @@
     stamp_count = 2 * own_count
     block_count = table_ref.shape[1]
     half = block_count // 2
+    group = NEWTON * GROUP
     later = lax.axis_index("sub") == 1
     tables = []
     for ref in (table_ref, table_other):
@@ -199,8 +205,8 @@
     block = row_to_column(jnp.where(mine, block_row, block_row + block_count))
     owner = row_to_column(owner_row)
     offset = row_to_column(offset_row)
-    place_in_half = jnp.where(offset < half, offset, offset - half)
-    row_hot = iota(row_hot_ref.shape, 1).astype(F32) == owner * half + place_in_half
+    upper = jnp.where(offset < half, 0, 1)
+    row_hot = iota(row_hot_ref.shape, 1).astype(F32) == owner * half + offset - half * upper.astype(F32)
     row_hot_ref[...] = row_hot.astype(F32).astype(BF16)
     shape = (stamp_count, stamp_count)
     row, column = iota(shape, 0), iota(shape, 1)
@@ -210,9 +216,8 @@
     slot_row = owner_row * (2 * per_owner) + rank_row
     place = iota(place_ref.shape, 0).astype(F32) == slot_row
     place_ref[...] = place.astype(F32).astype(BF16)
-    offset_hot_ref[...] = jnp.where(
-        iota(offset_hot_ref.shape, 1).astype(F32) == offset, 1.0, 0.0
-    )
+    offset_hot = iota(offset_hot_ref.shape, 1).astype(F32) == offset
+    offset_hot_ref[...] = offset_hot.astype(F32).astype(BF16)
 
     block_hot = iota((stamp_count, 2 * block_count), 1).astype(F32) == block
     block_hot = block_hot.astype(F32).astype(BF16)
@@ -221,87 +226,101 @@
         ((source_ref, target_ref, gain_ref), (source_other, target_other, gain_other))
     ):
         held = slice(n * own_count, (n + 1) * own_count)
-        target_out[held, :] = targets[...]
-        gain_out[held, :] = gains[...]
+        gain_out[held, :] = -gains[...]
         near = local[held]
         for at in range(0, elements, LANES):
             lanes = slice(at, at + LANES)
             source = sources[:, lanes]
             near_ref[held, lanes] = pick(near, source)
-            moved_ref[held, lanes] = pick(near, source + BS).astype(BF16)
+            moved = pick(near, source + BS).astype(BF16)
+            target = targets[:, lanes]
+            target_out[held, lanes] = (target + upper[held] * BS).astype(F32).astype(BF16)
+            low = digits(target)[1]
+            for start in range(0, own_count, group):
+                rows = slice(start, start + group)
+                first = DIGIT * (n * own_count + start)
+                right_ref[first : first + DIGIT * group, lanes] = hot_rows(low[rows], [moved[rows]])
 
 
 def couple_kernel(
-    half,
     fields_ref,
     target_ref,
     gain_ref,
     near_ref,
-    moved_ref,
+    right_ref,
     row_hot_ref,
     place_ref,
     offset_hot_ref,
     send_ref,
+    left_ref,
+    product_ref,
 ):
     stamp_count, elements = target_ref.shape
     group = NEWTON * GROUP
-    offset_hot = offset_hot_ref[...]
-    lane = iota(offset_hot.shape, 1)
+    rows_of = DIGIT * group
     remote = dot(row_hot_ref[...], fields_ref[...], NN)
-    upper = jnp.sum(
-        jnp.where(lane >= half, offset_hot, 0.0), axis=1, keepdims=True
-    )
-    remote = jnp.where(upper > 0.5, pltpu.roll(remote, BS, 1), remote)
-    shape = (DIGIT * group, LANES)
+    for start in range(0, stamp_count, group):
+        rows = slice(start, start + group)
+        held = slice(DIGIT * start, DIGIT * start + rows_of)
+        for at in range(0, elements, LANES):
+            lanes = slice(at, at + LANES)
+            target = target_ref[rows, lanes].astype(F32).astype(jnp.int32)
+            high = digits(target & (BS - 1))[0]
+            far = pick(remote[rows], target)
+            weight = conductance(gain_ref[rows, lanes], near_ref[rows, lanes], far)
+            left_ref[held, lanes] = hot_rows(high, [weight.astype(BF16)])
+    same = same_block((rows_of, rows_of), group)
+    for start in range(0, DIGIT * stamp_count, rows_of):
+        held = slice(start, start + rows_of)
+        product = dot(left_ref[held, :], right_ref[held, :], NT)
+        product_ref[held, :] = jnp.where(same, product, 0.0).astype(BF16)
+    shape = (rows_of, LANES)
     node = iota(shape, 1) - BS
     nodes = (node >= 0) & (node % DIGIT == iota(shape, 0) // group)
-    nodes = nodes.astype(F32).astype(BF16)
+    wide = dot(product_ref[...], nodes.astype(F32).astype(BF16), NN)
     high_lane = (iota((group, LANES), 1) - BS) // DIGIT
     images = []
-    for start in range(0, stamp_count, group):
-        rows = slice(start, start + group)
-        far = remote[rows]
-        acc = jnp.zeros((DIGIT * group, DIGIT * group), F32)
-        left, right = [], []
-        for at in range(0, elements, LANES):
-            lanes = slice(at, at + LANES)
-            target = target_ref[rows, lanes]
-            weight = conductance(-gain_ref[rows, lanes], near_ref[rows, lanes], pick(far, target))
-            high, low = digits(target)
-            left.append(hot_rows(high, [weight.astype(BF16)]))
-            right.append(hot_rows(low, [moved_ref[rows, lanes]]))
-            if len(left) == 2 or at + LANES >= elements:
-                acc = acc + dot(
-                    jnp.concatenate(left, axis=1), jnp.concatenate(right, axis=1), NT
-                )
-                left, right = [], []
-        acc = jnp.where(same_block(acc.shape, group), acc, 0.0).astype(BF16)
-        wide = dot(acc, nodes, NN)
+    for start in range(0, DIGIT * stamp_count, rows_of):
         total = jnp.zeros((group, LANES), F32)
         for h in range(DIGIT):
-            total = total + jnp.where(high_lane == h, wide[h * group : (h + 1) * group], 0.0)
+            slab = wide[start + h * group : start + (h + 1) * group]
+            total = total + jnp.where(high_lane == h, slab, 0.0)
         images.append(total)
     images = jnp.concatenate(images, axis=0)
-    messages = jnp.where(lane < BS, offset_hot, images).astype(BF16)
+    messages = images.astype(BF16) + offset_hot_ref[...]
     send_ref[...] = dot(place_ref[...], messages, NN).astype(BF16)
 
 
-def finish_kernel(row_count, images_ref, inner_ref, precond_ref, out_ref):
+def pack_kernel(precond_ref, packed_ref):
+    for g in range(packed_ref.shape[0]):
+        parts = [precond_ref[i] for i in range(g, BS, packed_ref.shape[0])]
+        packed_ref[g] = jnp.concatenate(parts, axis=0).T
+
+
+def finish_kernel(row_count, images_ref, inner_ref, packed_ref, out_ref):
     received = images_ref[...]
     block_count = inner_ref.shape[1]
+    parts = LANES // block_count
     step = iota(received.shape, 0) // row_count % NEWTON
+    totals = []
     for t in range(NEWTON):
         mine = jnp.where(step == t, received.astype(F32), 0.0).astype(BF16)
         couple = dot(received, mine, TN)[BS:, :block_count]
         total = inner_ref[t * BS : (t + 1) * BS, :] + couple
-        rows = [
-            jnp.sum(precond_ref[i : i + DIGIT] * total[None], axis=1)
-            for i in range(0, BS, DIGIT)
-        ]
-        out_ref[t] = jnp.concatenate(rows, axis=0).T
-
-
-def call(kernel, out_shape, args, flops):
+        totals.append(jnp.concatenate([total] * parts, axis=1))
+    rows = [[] for _ in range(NEWTON)]
+    for g in range(packed_ref.shape[0]):
+        packed = packed_ref[g]
+        for t in range(NEWTON):
+            rows[t].append(jnp.sum(packed * totals[t], axis=0, keepdims=True))
+    for t in range(NEWTON):
+        wide = jnp.concatenate(rows[t], axis=0).T
+        out_ref[t] = jnp.concatenate(
+            [wide[k * block_count : (k + 1) * block_count] for k in range(parts)], axis=1
+        )
+
+
+def call(kernel, out_shape, args, cost, scratch=()):
     spec = pl.BlockSpec(memory_space=pltpu.VMEM)
     several = isinstance(out_shape, (list, tuple))
     return pl.pallas_call(
@@ -309,8 +328,9 @@
         out_shape=out_shape,
         in_specs=[spec] * len(args),
         out_specs=[spec] * len(out_shape) if several else spec,
+        scratch_shapes=list(scratch),
         compiler_params=pltpu.CompilerParams(vmem_limit_bytes=24 * 2**20),
-        cost_estimate=pl.CostEstimate(flops=flops, bytes_accessed=10**6, transcendentals=0),
+        cost_estimate=pl.CostEstimate(flops=cost[0], bytes_accessed=cost[1], transcendentals=0),
     )(*args)
 
 
@@ -344,14 +364,20 @@
     swap = lambda array: lax.ppermute(array, "sub", [(0, 1), (1, 0)])
     table = jnp.concatenate([voltages.T[None], newton_steps.transpose(0, 2, 1)], axis=0)
     send = call(
-        prepare_kernel, like((devices * block_count // 2, LANES), BF16), (table,), 2 * 10**10
+        prepare_kernel, like((devices * block_count // 2, LANES), BF16), (table,), (2 * 10**10, 10**6)
     )
     fields = exchange(send, devices)
     inner = call(
         inner_kernel,
         like((NEWTON * BS, block_count), F32),
         (table, cap_diag.T, inner_source, inner_target, inner_gain),
-        4 * 10**9,
+        (4 * 10**9, 10**6),
+    )
+    packed = call(
+        pack_kernel,
+        like((BS * block_count // LANES, BS, LANES), F32),
+        (preconditioner.transpose(0, 2, 1),),
+        (10**8, 10**6),
     )
     facts = [fact.reshape(1, stamp_count) for fact in (couple_block, couple_owner, couple_offset)]
     wanted = (jnp.concatenate(facts, axis=0), table, couple_source, couple_target, couple_gain)
@@ -360,29 +386,33 @@
     prepared = call(
         functools.partial(stamp_kernel, per_owner),
         [
-            like((both, elements), couple_target.dtype),
+            like((both, elements), BF16),
             like((both, elements), couple_gain.dtype),
             like((both, elements), F32),
-            like((both, elements), BF16),
+            like((DIGIT * both, elements), BF16),
             like((both, devices * block_count // 2), BF16),
             like((row_count, both), BF16),
-            like((both, LANES), F32),
+            like((both, LANES), BF16),
         ],
         pairs,
-        10**8,
+        (4 * 10**8, 10**6),
     )
     images = call(
-        functools.partial(couple_kernel, block_count // 2),
+        couple_kernel,
         like((row_count, LANES), BF16),
         (fields, *prepared),
-        4 * 10**9,
+        (4 * 10**9, 10**6),
+        [
+            pltpu.VMEM((DIGIT * both, elements), BF16),
+            pltpu.VMEM((DIGIT * both, DIGIT * NEWTON * GROUP), BF16),
+        ],
     )
     received = exchange(images, devices)
     out = call(
         functools.partial(finish_kernel, 2 * per_owner),
         like((NEWTON, block_count, BS), F32),
-        (received, inner, preconditioner),
-        10**8,
+        (received, inner, packed),
+        (10**8, 10**6),
     )
     return out.transpose(0, 2, 1)
 

time: 31.2 us -> 30.4 us (0.974)
  local copies, waits for them, and re-layouts: 0.68 us -> 0.06 us
  Pallas kernels: 7.16 us -> 6.69 us
    unnamed x23 -> x22, local copies, waits for them, and re-layouts: 0.68 us -> 0.06 us
    pallas_call x5 -> x6, Pallas kernels: 7.16 us -> 6.69 us  [call(): pl.pallas_call(kernel, out_shape=out_shape, in_specs=[spec] * len(args),...]
  transfers between devices with their start and end apart: 7 -> 7, of which waited for: 3 -> 3; matrix products, arithmetic and copies ran while one was open for 2% -> 0% of each run, Pallas kernels for 8% -> 10%
where the time goes in v4:
time: 30.4 us; the launch traced here: 30 us
  starting transfers between devices  11.3 us (37%)
  waiting for transfers between devices  11.1 us (37%)
  Pallas kernels  6.69 us (22%)
  other arithmetic  0.78 us (3%)
    all_to_all x2, waiting for transfers between devices, exchange(): out = lax.all_to_all(shaped, AXES, split_axis=0, concat_axis=0, tiled=True)  10.2 us
    all_to_all x2, starting transfers between devices, exchange(): out = lax.all_to_all(shaped, AXES, split_axis=0, concat_axis=0, tiled=True)  9.86 us
    pallas_call x6, Pallas kernels, call(): pl.pallas_call(kernel, out_shape=out_shape, in_specs=[spec] * len(args),...  6.69 us
    ppermute x5, starting transfers between devices, per_device(): swap = lambda array: lax.ppermute(array, 'sub', [(0, 1), (1, 0)])  1.4 us
    ppermute x5, waiting for transfers between devices, per_device(): swap = lambda array: lax.ppermute(array, 'sub', [(0, 1), (1, 0)])  0.92 us
    concatenate x1, other arithmetic, per_device(): jnp.concatenate([voltages.T[None], newton_steps.transpose(0, 2, 1)], axis=0)  0.77 us
  transfers between devices with their start and end apart: 7, of which 3 were waited for; matrix products, arithmetic and copies ran while one was open for 0% of the time, Pallas kernels for 10%

profile of v4, /device:TPU:0, one launch (start us, length us, event | category | flops | bytes accessed | tf_op | source)
XLA Modules:
  0.0 30.0 jit_solution(4084774224978473001)
XLA Ops:
  0.0 0.8 %pad_maximum_fusion.table_ref = f32[3,32,64]{2,1,0:T(8,128)S(1)} fusion(f32[2,32,64]{2,1,0:T(8,128)} %bitcast.18, f32[1,32,64]{2,1,0:T(8,128)} %bitcast.19), kind=kLoop, calls=%fused_computation | loop fusion | flops 6144 | bytes 49152 | tf_op jit(solution)/shard_map/concatenate | solution.py:365
  0.8 0.0 copy-start.1
  0.8 0.0 copy-start.2
  0.8 0.0 copy-start.3
  0.8 0.0 copy-start.8
  0.8 0.0 copy-start.9
  0.8 0.0 copy-start.10
  0.8 0.7 %shard_map.127 = bf16[512,128]{1,0:T(8,128)(2,1)} custom-call(f32[3,32,64]{2,1,0:T(8,128)S(1)} %pad_maximum_fusion.table_ref), custom_call_target="tpu_custom_call" | custom-call | flops 20000000000 | bytes 1000000 | tf_op jit(solution)/shard_map/pallas_call | solution.py:326
  1.6 7.3 %all-to-all-start = ((bf16[32,16,128]{2,1,0:T(8,128)(2,1)}), bf16[32,16,128]{2,1,0:T(8,128)(2,1)S(1)}, u32[]{:S(2)}, u32[]{:S(2)}) async-start(bf16[32,16,128]{2,1,0:T(8,128)(2,1)} %bitcast.3), calls=%async_computation | async-start | bytes 262144 | tf_op jit(solution)/shard_map/all_to_all | solution.py:339
  8.9 0.0 copy-done.1
  8.9 0.3 %collective-permute-start.2 = (s32[64,768]{1,0:T(8,128)S(1)}, s32[64,768]{1,0:T(8,128)S(1)}, u32[]{:S(2)}, u32[]{:S(2)}) collective-permute-start(s32[64,768]{1,0:T(8,128)S(1)} %copy-done.1), channel_id=1, source_target_pairs={{0,1},{1,0},{2,3},{3,2},{4,5},{5,4},{6,7},{7,6},{8,9},{9,8},{10,11... | collective-permute-start | bytes 589832 | tf_op jit(solution)/shard_map/ppermute | solution.py:364
  9.2 0.0 copy-done.2
  9.2 0.3 collective-permute-start.3
  9.5 0.0 copy-done.3
  9.5 0.3 collective-permute-start.4
  9.7 0.3 collective-permute-start.1
  10.0 0.0 copy-done.8
  10.0 0.0 copy-done.9
  10.0 0.0 copy-done.10
  10.0 0.3 %collective-permute-start = (s32[3,64]{1,0:T(4,128)S(1)}, s32[3,64]{1,0:T(4,128)S(1)}, u32[]{:S(2)}, u32[]{:S(2)}) collective-permute-start(s32[3,64]{1,0:T(4,128)S(1)} %pad_add_fusion.facts_ref), channel_id=1, source_target_pairs={{0,1},{1,0},{2,3},{3,2},{4,5},{5,4},{6,7},{7,6},{8,9},{9,8},{10,11... | collective-permute-start | bytes 2312 | tf_op jit(solution)/shard_map/ppermute | solution.py:364
  10.3 0.9 %collective-permute-done.facts_other = s32[3,64]{1,0:T(4,128)S(1)} collective-permute-done((s32[3,64]{1,0:T(4,128)S(1)}, s32[3,64]{1,0:T(4,128)S(1)}, u32[]{:S(2)}, u32[]{:S(2)}) %collective-permute-start) | collective-permute-done | bytes 800 | tf_op jit(solution)/shard_map/ppermute | solution.py:364
  11.2 0.0 collective-permute-done.1.table_other
  11.2 0.0 collective-permute-done.2.source_other
  11.2 0.0 collective-permute-done.3.target_other
  11.2 0.0 collective-permute-done.4.gain_other
  11.2 1.0 %shard_map.128 = (bf16[128,768]{1,0:T(8,128)(2,1)S(1)}, f32[128,768]{1,0:T(8,128)S(1)}, f32[128,768]{1,0:T(8,128)S(1)}, bf16[1024,768]{1,0:T(8,128)(2,1)S(1)}, b...) custom-call(s32[3,64]{1,0:T(4,128)S(1)} %pad_add_fusion.facts_ref, ...), custom_call_target="tpu_custom_call" | custom-call | flops 400000000 | bytes 1000000 | tf_op jit(solution)/shard_map/pallas_call | solution.py:326
  12.3 4.8 %all-to-all-done = bf16[32,16,128]{2,1,0:T(8,128)(2,1)S(1)} async-done(((bf16[32,16,128]{2,1,0:T(8,128)(2,1)}), bf16[32,16,128]{2,1,0:T(8,128)(2,1)S(1)}, u32[]{:S(2)}, u32[]{:S(2)}) %all-to-all-start) | async-done | bytes 131104 | tf_op jit(solution)/shard_map/all_to_all | solution.py:339
  17.1 0.0 copy-start.4
  17.1 0.0 copy-start.5
  17.1 0.0 copy-start.6
  17.1 0.0 copy-start.7
  17.1 1.8 %shard_map.129 = bf16[256,128]{1,0:T(8,128)(2,1)} custom-call(bf16[512,128]{1,0:T(8,128)(2,1)S(1)} %bitcast.16, bf16[128,768]{1,0:T(8,128)(2,1)S(1)} %get-tuple-element.12.target_ref, f32[128,768]{1,0:T(8,128)S(1)} %get-tuple-element.13.gain_ref, f32[128,768]{1,0:T(8,128)S(1)} %get-tuple-element.14.near_ref, ...), custom_call_target="tpu_custom_call" | custom-call | flops 4000000000 | bytes 1000000 | tf_op jit(solution)/shard_map/pallas_call | solution.py:326
  18.9 2.6 %all-to-all-start.1 = ((bf16[32,8,128]{2,1,0:T(8,128)(2,1)}), bf16[32,8,128]{2,1,0:T(8,128)(2,1)S(1)}, u32[]{:S(2)}, u32[]{:S(2)}) async-start(bf16[32,8,128]{2,1,0:T(8,128)(2,1)} %bitcast.8), calls=%async_computation.1 | async-start | bytes 131072 | tf_op jit(solution)/shard_map/all_to_all | solution.py:339
  21.5 0.0 copy-done.4
  21.5 0.0 copy-done.5
  21.5 0.0 copy-done.6
  21.5 0.0 copy-done.7
  21.5 0.0 copy-start
  21.5 1.6 %shard_map.130.inner_ref = f32[128,32]{1,0:T(8,128)S(1)} custom-call(f32[3,32,64]{2,1,0:T(8,128)S(1)} %pad_maximum_fusion.table_ref, f32[32,64]{1,0:T(8,128)S(1)} %bitcast.17, s32[32,768]{1,0:T(8,128)S(1)} %copy-done.4, s32[32,768]{1,0:T(8,128)S(1)} %copy-done.5, f32[32,768]{1,0:T(8,128)S(1)} %copy-done.6), custom_call_target="tpu_custom_call" | custom-call | flops 4000000000 | bytes 1000000 | tf_op jit(solution)/shard_map/pallas_call | solution.py:326
  23.2 0.0 copy-done
  23.2 0.3 %shard_map.131.packed_ref = f32[16,64,128]{2,1,0:T(8,128)S(1)} custom-call(f32[64,32,64]{2,1,0:T(8,128)S(1)} %bitcast.14), custom_call_target="tpu_custom_call" | custom-call | flops 100000000 | bytes 1000000 | tf_op jit(solution)/shard_map/pallas_call | solution.py:326
  23.5 5.4 %all-to-all-done.1 = bf16[32,8,128]{2,1,0:T(8,128)(2,1)S(1)} async-done(((bf16[32,8,128]{2,1,0:T(8,128)(2,1)}), bf16[32,8,128]{2,1,0:T(8,128)(2,1)S(1)}, u32[]{:S(2)}, u32[]{:S(2)}) %all-to-all-start.1) | async-done | bytes 65568 | tf_op jit(solution)/shard_map/all_to_all | solution.py:339
  28.9 1.2 %shard_map.132 = f32[2,32,64]{2,1,0:T(8,128)} custom-call(bf16[256,128]{1,0:T(8,128)(2,1)S(1)} %bitcast.15, f32[128,32]{1,0:T(8,128)S(1)} %shard_map.130.inner_ref, f32[16,64,128]{2,1,0:T(8,128)S(1)} %shard_map.131.packed_ref), custom_call_target="tpu_custom_call" | custom-call | flops 100000000 | bytes 1000000 | tf_op jit(solution)/shard_map/pallas_call | solution.py:326
  (1 shorter events, 0.0 us)
Async XLA Ops:
  0.8 8.1 %copy-start.1 = (s32[64,768]{1,0:T(8,128)S(1)}, s32[64,768]{1,0:T(8,128)}, u32[]{:S(2)}) copy-start(s32[64,768]{1,0:T(8,128)} %source_ref.1) | copy-start | bytes 589828
  0.8 8.4 %copy-start.2 = (s32[64,768]{1,0:T(8,128)S(1)}, s32[64,768]{1,0:T(8,128)}, u32[]{:S(2)}) copy-start(s32[64,768]{1,0:T(8,128)} %target_ref.1) | copy-start | bytes 589828
  0.8 8.7 %copy-start.3 = (f32[64,768]{1,0:T(8,128)S(1)}, f32[64,768]{1,0:T(8,128)}, u32[]{:S(2)}) copy-start(f32[64,768]{1,0:T(8,128)} %gain_ref.1) | copy-start | bytes 589828
  0.8 9.2 %copy-start.8 = (s32[64]{0:T(128)S(1)}, s32[64]{0:T(128)}, u32[]{:S(2)}) copy-start(s32[64]{0:T(128)} %param.19) | copy-start | bytes 772
  0.8 9.2 %copy-start.9 = (s32[64,1]{0,1:T(1,128)S(1)}, s32[64,1]{0,1:T(1,128)}, u32[]{:S(2)}) copy-start(s32[64,1]{0,1:T(1,128)} %param.18) | copy-start | bytes 772
  0.8 9.2 %copy-start.10 = (s32[64]{0:T(128)S(1)}, s32[64]{0:T(128)}, u32[]{:S(2)}) copy-start(s32[64]{0:T(128)} %param.17) | copy-start | bytes 772
  1.6 15.5 %all-to-all-start = ((bf16[32,16,128]{2,1,0:T(8,128)(2,1)}), bf16[32,16,128]{2,1,0:T(8,128)(2,1)S(1)}, u32[]{:S(2)}, u32[]{:S(2)}) async-start(bf16[32,16,128]{2,1,0:T(8,128)(2,1)} %bitcast.3), calls=%async_computation | async-start | bytes 262144 | tf_op jit(solution)/shard_map/all_to_all | solution.py:339
  8.9 2.3 %collective-permute-start.2 = (s32[64,768]{1,0:T(8,128)S(1)}, s32[64,768]{1,0:T(8,128)S(1)}, u32[]{:S(2)}, u32[]{:S(2)}) collective-permute-start(s32[64,768]{1,0:T(8,128)S(1)} %copy-done.1), channel_id=1, source_target_pairs={{0,1},{1,0},{2,3},{3,2},{4,5},{5,4},{6,7},{7,6},{8,9},{9,8},{10,11... | collective-permute-start | bytes 589832 | tf_op jit(solution)/shard_map/ppermute | solution.py:364
  9.2 2.0 %collective-permute-start.3 = (s32[64,768]{1,0:T(8,128)S(1)}, s32[64,768]{1,0:T(8,128)S(1)}, u32[]{:S(2)}, u32[]{:S(2)}) collective-permute-start(s32[64,768]{1,0:T(8,128)S(1)} %copy-done.2), channel_id=1, source_target_pairs={{0,1},{1,0},{2,3},{3,2},{4,5},{5,4},{6,7},{7,6},{8,9},{9,8},{10,11... | collective-permute-start | bytes 589832 | tf_op jit(solution)/shard_map/ppermute | solution.py:364
  9.5 1.8 %collective-permute-start.4 = (f32[64,768]{1,0:T(8,128)S(1)}, f32[64,768]{1,0:T(8,128)S(1)}, u32[]{:S(2)}, u32[]{:S(2)}) collective-permute-start(f32[64,768]{1,0:T(8,128)S(1)} %copy-done.3), channel_id=1, source_target_pairs={{0,1},{1,0},{2,3},{3,2},{4,5},{5,4},{6,7},{7,6},{8,9},{9,8},{10,11... | collective-permute-start | bytes 589832 | tf_op jit(solution)/shard_map/ppermute | solution.py:364
  9.7 1.5 %collective-permute-start.1 = (f32[3,32,64]{2,1,0:T(8,128)S(1)}, f32[3,32,64]{2,1,0:T(8,128)S(1)}, u32[]{:S(2)}, u32[]{:S(2)}) collective-permute-start(f32[3,32,64]{2,1,0:T(8,128)S(1)} %pad_maximum_fusion.table_ref), channel_id=1, source_target_pairs={{0,1},{1,0},{2,3},{3,2},{4,5},{5,4},{6,7},{7,6},{8,9},{9,8},{10,11... | collective-permute-start | bytes 73736 | tf_op jit(solution)/shard_map/ppermute | solution.py:364
  10.0 1.2 %collective-permute-start = (s32[3,64]{1,0:T(4,128)S(1)}, s32[3,64]{1,0:T(4,128)S(1)}, u32[]{:S(2)}, u32[]{:S(2)}) collective-permute-start(s32[3,64]{1,0:T(4,128)S(1)} %pad_add_fusion.facts_ref), channel_id=1, source_target_pairs={{0,1},{1,0},{2,3},{3,2},{4,5},{5,4},{6,7},{7,6},{8,9},{9,8},{10,11... | collective-permute-start | bytes 2312 | tf_op jit(solution)/shard_map/ppermute | solution.py:364
  17.1 4.4 %copy-start.4 = (s32[32,768]{1,0:T(8,128)S(1)}, s32[32,768]{1,0:T(8,128)}, u32[]{:S(2)}) copy-start(s32[32,768]{1,0:T(8,128)} %inner_source_ref.1) | copy-start | bytes 294916
  17.1 4.4 %copy-start.5 = (s32[32,768]{1,0:T(8,128)S(1)}, s32[32,768]{1,0:T(8,128)}, u32[]{:S(2)}) copy-start(s32[32,768]{1,0:T(8,128)} %inner_target_ref.1) | copy-start | bytes 294916
  17.1 4.4 %copy-start.6 = (f32[32,768]{1,0:T(8,128)S(1)}, f32[32,768]{1,0:T(8,128)}, u32[]{:S(2)}) copy-start(f32[32,768]{1,0:T(8,128)} %inner_gain_ref.1) | copy-start | bytes 294916
  17.1 4.4 %copy-start.7 = (f32[64,32]{0,1:T(8,128)S(1)}, f32[64,32]{0,1:T(8,128)}, u32[]{:S(2)}) copy-start(f32[64,32]{0,1:T(8,128)} %param.15) | copy-start | bytes 24580
  18.9 10.0 %all-to-all-start.1 = ((bf16[32,8,128]{2,1,0:T(8,128)(2,1)}), bf16[32,8,128]{2,1,0:T(8,128)(2,1)S(1)}, u32[]{:S(2)}, u32[]{:S(2)}) async-start(bf16[32,8,128]{2,1,0:T(8,128)(2,1)} %bitcast.8), calls=%async_computation.1 | async-start | bytes 131072 | tf_op jit(solution)/shard_map/all_to_all | solution.py:339
  21.5 1.7 %copy-start = (f32[64,64,32]{1,2,0:T(8,128)S(1)}, f32[64,64,32]{1,2,0:T(8,128)}, u32[]{:S(2)}) copy-start(f32[64,64,32]{1,2,0:T(8,128)} %param.16) | copy-start | bytes 1572868

commit v5 on v4

--- a/solution.py
+++ b/solution.py
@@ -182,6 +182,7 @@
     gain_out,
     near_ref,
     right_ref,
+    moved_ref,
     row_hot_ref,
     place_ref,
     offset_hot_ref,
@@ -235,11 +236,14 @@
             moved = pick(near, source + BS).astype(BF16)
             target = targets[:, lanes]
             target_out[held, lanes] = (target + upper[held] * BS).astype(F32).astype(BF16)
+            if n > 0:
+                moved_ref[:, lanes] = moved
+                continue
             low = digits(target)[1]
             for start in range(0, own_count, group):
                 rows = slice(start, start + group)
-                first = DIGIT * (n * own_count + start)
-                right_ref[first : first + DIGIT * group, lanes] = hot_rows(low[rows], [moved[rows]])
+                held_rows = slice(DIGIT * start, DIGIT * (start + group))
+                right_ref[held_rows, lanes] = hot_rows(low[rows], [moved[rows]])
 
 
 def couple_kernel(
@@ -248,16 +252,19 @@
     gain_ref,
     near_ref,
     right_ref,
+    moved_ref,
     row_hot_ref,
     place_ref,
     offset_hot_ref,
     send_ref,
     left_ref,
+    late_ref,
     product_ref,
 ):
     stamp_count, elements = target_ref.shape
     group = NEWTON * GROUP
     rows_of = DIGIT * group
+    early = right_ref.shape[0] // DIGIT
     remote = dot(row_hot_ref[...], fields_ref[...], NN)
     for start in range(0, stamp_count, group):
         rows = slice(start, start + group)
@@ -265,14 +272,22 @@
         for at in range(0, elements, LANES):
             lanes = slice(at, at + LANES)
             target = target_ref[rows, lanes].astype(F32).astype(jnp.int32)
-            high = digits(target & (BS - 1))[0]
+            high, low = digits(target & (BS - 1))
+            if start >= early:
+                moved = moved_ref[start - early : start - early + group, lanes]
+                late = slice(held.start - DIGIT * early, held.stop - DIGIT * early)
+                late_ref[late, lanes] = hot_rows(low, [moved])
             far = pick(remote[rows], target)
             weight = conductance(gain_ref[rows, lanes], near_ref[rows, lanes], far)
             left_ref[held, lanes] = hot_rows(high, [weight.astype(BF16)])
     same = same_block((rows_of, rows_of), group)
     for start in range(0, DIGIT * stamp_count, rows_of):
         held = slice(start, start + rows_of)
-        product = dot(left_ref[held, :], right_ref[held, :], NT)
+        if start < DIGIT * early:
+            right = right_ref[held, :]
+        else:
+            right = late_ref[start - DIGIT * early : start - DIGIT * early + rows_of, :]
+        product = dot(left_ref[held, :], right, NT)
         product_ref[held, :] = jnp.where(same, product, 0.0).astype(BF16)
     shape = (rows_of, LANES)
     node = iota(shape, 1) - BS
@@ -366,12 +381,14 @@
     send = call(
         prepare_kernel, like((devices * block_count // 2, LANES), BF16), (table,), (2 * 10**10, 10**6)
     )
+    facts = [fact.reshape(1, stamp_count) for fact in (couple_block, couple_owner, couple_offset)]
+    send, facts = lax.optimization_barrier((send, jnp.concatenate(facts, axis=0)))
     fields = exchange(send, devices)
     inner = call(
         inner_kernel,
         like((NEWTON * BS, block_count), F32),
         (table, cap_diag.T, inner_source, inner_target, inner_gain),
-        (4 * 10**9, 10**6),
+        (10**9, 10**6),
     )
     packed = call(
         pack_kernel,
@@ -379,24 +396,25 @@
         (preconditioner.transpose(0, 2, 1),),
         (10**8, 10**6),
     )
-    facts = [fact.reshape(1, stamp_count) for fact in (couple_block, couple_owner, couple_offset)]
-    wanted = (jnp.concatenate(facts, axis=0), table, couple_source, couple_target, couple_gain)
+    wanted = (facts, table, couple_source, couple_target, couple_gain)
     pairs = [half for array in wanted for half in (array, swap(array))]
     both = 2 * stamp_count
     prepared = call(
         functools.partial(stamp_kernel, per_owner),
         [
             like((both, elements), BF16),
-            like((both, elements), couple_gain.dtype),
             like((both, elements), F32),
-            like((DIGIT * both, elements), BF16),
+            like((both, elements), F32),
+            like((DIGIT * stamp_count, elements), BF16),
+            like((stamp_count, elements), BF16),
             like((both, devices * block_count // 2), BF16),
             like((row_count, both), BF16),
             like((both, LANES), BF16),
         ],
         pairs,
-        (4 * 10**8, 10**6),
-    )
+        (10**8, 10**6),
+    )
+    fields, inner, packed = lax.optimization_barrier((fields, inner, packed))
     images = call(
         couple_kernel,
         like((row_count, LANES), BF16),
@@ -404,6 +422,7 @@
         (4 * 10**9, 10**6),
         [
             pltpu.VMEM((DIGIT * both, elements), BF16),
+            pltpu.VMEM((DIGIT * stamp_count, elements), BF16),
             pltpu.VMEM((DIGIT * both, DIGIT * NEWTON * GROUP), BF16),
         ],
     )

time: 30.4 us -> 29.2 us (0.961)
  blocking collectives: 0 us -> 9.18 us
  waiting for transfers between devices: 11.1 us -> 3.81 us
  starting transfers between devices: 11.3 us -> 8.64 us
  Pallas kernels: 6.69 us -> 6.28 us
    all_to_all x0 -> x1, blocking collectives: none -> 9.18 us  [exchange(): out = lax.all_to_all(shaped, AXES, split_axis=0, concat_axis=0, tiled=True)]
    all_to_all x2 -> x1, waiting for transfers between devices: 10.2 us -> 3.8 us  [exchange(): out = lax.all_to_all(shaped, AXES, split_axis=0, concat_axis=0, tiled=True)]
    all_to_all x2 -> x1, starting transfers between devices: 9.86 us -> 7.3 us  [exchange(): out = lax.all_to_all(shaped, AXES, split_axis=0, concat_axis=0, tiled=True)]
    ppermute x5, waiting for transfers between devices: 0.92 us -> 0.01 us  [per_device(): swap = lambda array: lax.ppermute(array, 'sub', [(0, 1), (1, 0)])]
    pallas_call x6, Pallas kernels: 6.69 us -> 6.28 us  [call(): pl.pallas_call(kernel, out_shape=out_shape, in_specs=[spec] * len(args),...]
  transfers between devices with their start and end apart: 7 -> 6, of which waited for: 3 -> 1; matrix products, arithmetic and copies ran while one was open for 0% -> 0% of each run, Pallas kernels for 10% -> 10%
where the time goes in v5:
time: 29.2 us; the launch traced here: 28.9 us
  blocking collectives  9.18 us (31%)
  starting transfers between devices  8.64 us (30%)
  Pallas kernels  6.28 us (22%)
  waiting for transfers between devices  3.81 us (13%)
  other arithmetic  0.78 us (3%)
    all_to_all x1, blocking collectives, exchange(): out = lax.all_to_all(shaped, AXES, split_axis=0, concat_axis=0, tiled=True)  9.18 us
    all_to_all x1, starting transfers between devices, exchange(): out = lax.all_to_all(shaped, AXES, split_axis=0, concat_axis=0, tiled=True)  7.3 us
    pallas_call x6, Pallas kernels, call(): pl.pallas_call(kernel, out_shape=out_shape, in_specs=[spec] * len(args),...  6.28 us
    all_to_all x1, waiting for transfers between devices, exchange(): out = lax.all_to_all(shaped, AXES, split_axis=0, concat_axis=0, tiled=True)  3.8 us
    ppermute x5, starting transfers between devices, per_device(): swap = lambda array: lax.ppermute(array, 'sub', [(0, 1), (1, 0)])  1.34 us
    concatenate x1, other arithmetic, per_device(): jnp.concatenate([voltages.T[None], newton_steps.transpose(0, 2, 1)], axis=0)  0.77 us
  transfers between devices with their start and end apart: 6, of which 1 were waited for; matrix products, arithmetic and copies ran while one was open for 0% of the time, Pallas kernels for 10%

profile of v5, /device:TPU:0, one launch (start us, length us, event | category | flops | bytes accessed | tf_op | source)
XLA Modules:
  0.0 28.9 jit_solution(15399255227799951548)
XLA Ops:
  0.0 0.8 %pad_maximum_fusion.table_ref = f32[3,32,64]{2,1,0:T(8,128)S(1)} fusion(f32[2,32,64]{2,1,0:T(8,128)} %bitcast.19, f32[1,32,64]{2,1,0:T(8,128)} %bitcast.20), kind=kLoop, calls=%fused_computation | loop fusion | flops 6144 | bytes 49152 | tf_op jit(solution)/shard_map/concatenate | solution.py:380
  0.8 0.0 copy-start.8
  0.8 0.0 copy-start.9
  0.8 0.0 copy-start.10
  0.8 0.0 copy-start.2
  0.8 0.0 copy-start.3
  0.8 0.0 copy-start.4
  0.8 0.0 copy-start.5
  0.8 0.0 copy-start.6
  0.9 0.8 %shard_map.127 = bf16[512,128]{1,0:T(8,128)(2,1)} custom-call(f32[3,32,64]{2,1,0:T(8,128)S(1)} %pad_maximum_fusion.table_ref), custom_call_target="tpu_custom_call" | custom-call | flops 20000000000 | bytes 1000000 | tf_op jit(solution)/shard_map/pallas_call | solution.py:341
  1.6 0.0 copy-start.1
  1.6 0.0 copy-done.8
  1.6 0.0 copy-done.9
  1.6 0.0 copy-done.10
  1.6 0.0 copy-start.7
  1.7 7.3 %all-to-all-start = ((bf16[32,16,128]{2,1,0:T(8,128)(2,1)}), bf16[32,16,128]{2,1,0:T(8,128)(2,1)S(1)}, u32[]{:S(2)}, u32[]{:S(2)}) async-start(bf16[32,16,128]{2,1,0:T(8,128)(2,1)} %bitcast.6), calls=%async_computation | async-start | bytes 262144 | tf_op jit(solution)/shard_map/all_to_all | solution.py:354
  9.0 0.0 copy-done.1
  9.0 0.3 %collective-permute-start.2 = (s32[64,768]{1,0:T(8,128)S(1)}, s32[64,768]{1,0:T(8,128)S(1)}, u32[]{:S(2)}, u32[]{:S(2)}) collective-permute-start(s32[64,768]{1,0:T(8,128)S(1)} %copy-done.1), channel_id=1, source_target_pairs={{0,1},{1,0},{2,3},{3,2},{4,5},{5,4},{6,7},{7,6},{8,9},{9,8},{10,11... | collective-permute-start | bytes 589832 | tf_op jit(solution)/shard_map/ppermute | solution.py:379
  9.3 0.0 copy-done.2
  9.3 0.3 collective-permute-start.3
  9.6 0.0 copy-done.3
  9.6 0.3 collective-permute-start.4
  9.8 0.3 collective-permute-start.1
  10.1 0.3 collective-permute-start
  10.3 0.0 copy-done.4
  10.3 0.0 copy-done.5
  10.3 0.0 copy-done.6
  10.3 0.0 copy-done.7
  10.3 0.0 copy-start
  10.3 1.6 %shard_map.128.inner_ref = f32[128,32]{1,0:T(8,128)S(1)} custom-call(f32[3,32,64]{2,1,0:T(8,128)S(1)} %pad_maximum_fusion.table_ref, f32[32,64]{1,0:T(8,128)S(1)} %bitcast.18, s32[32,768]{1,0:T(8,128)S(1)} %copy-done.4, s32[32,768]{1,0:T(8,128)S(1)} %copy-done.5, f32[32,768]{1,0:T(8,128)S(1)} %copy-done.6), custom_call_target="tpu_custom_call" | custom-call | flops 1000000000 | bytes 1000000 | tf_op jit(solution)/shard_map/pallas_call | solution.py:341
  12.0 0.0 copy-done
  12.0 0.3 %shard_map.129.packed_ref = f32[16,64,128]{2,1,0:T(8,128)S(1)} custom-call(f32[64,32,64]{2,1,0:T(8,128)S(1)} %bitcast.14), custom_call_target="tpu_custom_call" | custom-call | flops 100000000 | bytes 1000000 | tf_op jit(solution)/shard_map/pallas_call | solution.py:341
  12.3 0.0 collective-permute-done.facts_other
  12.3 0.0 collective-permute-done.1.table_other
  12.3 0.0 collective-permute-done.2.source_other
  12.4 0.0 collective-permute-done.3.target_other
  12.4 0.0 collective-permute-done.4.gain_other
  12.4 1.0 %shard_map.130 = (bf16[128,768]{1,0:T(8,128)(2,1)S(1)}, f32[128,768]{1,0:T(8,128)S(1)}, f32[128,768]{1,0:T(8,128)S(1)}, bf16[512,768]{1,0:T(8,128)(2,1)S(1)}, bf...) custom-call(s32[3,64]{1,0:T(4,128)S(1)} %pad_add_fusion.facts_ref, ...), custom_call_target="tpu_custom_call" | custom-call | flops 100000000 | bytes 1000000 | tf_op jit(solution)/shard_map/pallas_call | solution.py:341
  13.4 3.8 %all-to-all-done = bf16[32,16,128]{2,1,0:T(8,128)(2,1)S(1)} async-done(((bf16[32,16,128]{2,1,0:T(8,128)(2,1)}), bf16[32,16,128]{2,1,0:T(8,128)(2,1)S(1)}, u32[]{:S(2)}, u32[]{:S(2)}) %all-to-all-start) | async-done | bytes 131104 | tf_op jit(solution)/shard_map/all_to_all | solution.py:354
  17.2 1.4 %shard_map.131 = bf16[256,128]{1,0:T(8,128)(2,1)S(1)} custom-call(bf16[512,128]{1,0:T(8,128)(2,1)S(1)} %bitcast.16, bf16[128,768]{1,0:T(8,128)(2,1)S(1)} %get-tuple-element.21.target_ref, f32[128,768]{1,0:T(8,128)S(1)} %get-tuple-element.22.gain_ref, f32[128,768]{1,0:T(8,128)S(1)} %get-tuple-element.23.near_ref, ...), custom_call_target="tpu_custom_call" | custom-call | flops 4000000000 | bytes 1000000 | tf_op jit(solution)/shard_map/pallas_call | solution.py:341
  18.6 9.2 %all_to_all.10 = bf16[32,8,128]{2,1,0:T(8,128)(2,1)S(1)} all-to-all(bf16[32,8,128]{2,1,0:T(8,128)(2,1)S(1)} %bitcast.17), channel_id=1, replica_groups=mesh['dom'=16,'sub'=2] {'dom','sub'}, dimensions={0} | all-to-all | bytes 131072 | tf_op jit(solution)/shard_map/all_to_all | solution.py:354
  27.8 1.2 %shard_map.132 = f32[2,32,64]{2,1,0:T(8,128)} custom-call(bf16[256,128]{1,0:T(8,128)(2,1)S(1)} %bitcast.15, f32[128,32]{1,0:T(8,128)S(1)} %shard_map.128.inner_ref, f32[16,64,128]{2,1,0:T(8,128)S(1)} %shard_map.129.packed_ref), custom_call_target="tpu_custom_call" | custom-call | flops 100000000 | bytes 1000000 | tf_op jit(solution)/shard_map/pallas_call | solution.py:341
  (1 shorter events, 0.0 us)
Async XLA Ops:
  0.8 0.8 %copy-start.8 = (s32[64]{0:T(128)S(1)}, s32[64]{0:T(128)}, u32[]{:S(2)}) copy-start(s32[64]{0:T(128)} %param.19) | copy-start | bytes 772
  0.8 0.8 %copy-start.9 = (s32[64,1]{0,1:T(1,128)S(1)}, s32[64,1]{0,1:T(1,128)}, u32[]{:S(2)}) copy-start(s32[64,1]{0,1:T(1,128)} %param.18) | copy-start | bytes 772
  0.8 0.8 %copy-start.10 = (s32[64]{0:T(128)S(1)}, s32[64]{0:T(128)}, u32[]{:S(2)}) copy-start(s32[64]{0:T(128)} %param.17) | copy-start | bytes 772
  0.8 8.5 %copy-start.2 = (s32[64,768]{1,0:T(8,128)S(1)}, s32[64,768]{1,0:T(8,128)}, u32[]{:S(2)}) copy-start(s32[64,768]{1,0:T(8,128)} %target_ref.1) | copy-start | bytes 589828
  0.8 8.7 %copy-start.3 = (f32[64,768]{1,0:T(8,128)S(1)}, f32[64,768]{1,0:T(8,128)}, u32[]{:S(2)}) copy-start(f32[64,768]{1,0:T(8,128)} %gain_ref.1) | copy-start | bytes 589828
  0.8 9.5 %copy-start.4 = (s32[32,768]{1,0:T(8,128)S(1)}, s32[32,768]{1,0:T(8,128)}, u32[]{:S(2)}) copy-start(s32[32,768]{1,0:T(8,128)} %inner_source_ref.1) | copy-start | bytes 294916
  0.8 9.5 %copy-start.5 = (s32[32,768]{1,0:T(8,128)S(1)}, s32[32,768]{1,0:T(8,128)}, u32[]{:S(2)}) copy-start(s32[32,768]{1,0:T(8,128)} %inner_target_ref.1) | copy-start | bytes 294916
  0.8 9.5 %copy-start.6 = (f32[32,768]{1,0:T(8,128)S(1)}, f32[32,768]{1,0:T(8,128)}, u32[]{:S(2)}) copy-start(f32[32,768]{1,0:T(8,128)} %inner_gain_ref.1) | copy-start | bytes 294916
  1.6 7.4 %copy-start.1 = (s32[64,768]{1,0:T(8,128)S(1)}, s32[64,768]{1,0:T(8,128)}, u32[]{:S(2)}) copy-start(s32[64,768]{1,0:T(8,128)} %source_ref.1) | copy-start | bytes 589828
  1.6 8.7 %copy-start.7 = (f32[64,32]{0,1:T(8,128)S(1)}, f32[64,32]{0,1:T(8,128)}, u32[]{:S(2)}) copy-start(f32[64,32]{0,1:T(8,128)} %param.15) | copy-start | bytes 24580
  1.7 15.5 %all-to-all-start = ((bf16[32,16,128]{2,1,0:T(8,128)(2,1)}), bf16[32,16,128]{2,1,0:T(8,128)(2,1)S(1)}, u32[]{:S(2)}, u32[]{:S(2)}) async-start(bf16[32,16,128]{2,1,0:T(8,128)(2,1)} %bitcast.6), calls=%async_computation | async-start | bytes 262144 | tf_op jit(solution)/shard_map/all_to_all | solution.py:354
  9.0 3.4 %collective-permute-start.2 = (s32[64,768]{1,0:T(8,128)S(1)}, s32[64,768]{1,0:T(8,128)S(1)}, u32[]{:S(2)}, u32[]{:S(2)}) collective-permute-start(s32[64,768]{1,0:T(8,128)S(1)} %copy-done.1), channel_id=1, source_target_pairs={{0,1},{1,0},{2,3},{3,2},{4,5},{5,4},{6,7},{7,6},{8,9},{9,8},{10,11... | collective-permute-start | bytes 589832 | tf_op jit(solution)/shard_map/ppermute | solution.py:379
  9.3 3.1 %collective-permute-start.3 = (s32[64,768]{1,0:T(8,128)S(1)}, s32[64,768]{1,0:T(8,128)S(1)}, u32[]{:S(2)}, u32[]{:S(2)}) collective-permute-start(s32[64,768]{1,0:T(8,128)S(1)} %copy-done.2), channel_id=1, source_target_pairs={{0,1},{1,0},{2,3},{3,2},{4,5},{5,4},{6,7},{7,6},{8,9},{9,8},{10,11... | collective-permute-start | bytes 589832 | tf_op jit(solution)/shard_map/ppermute | solution.py:379
  9.6 2.8 %collective-permute-start.4 = (f32[64,768]{1,0:T(8,128)S(1)}, f32[64,768]{1,0:T(8,128)S(1)}, u32[]{:S(2)}, u32[]{:S(2)}) collective-permute-start(f32[64,768]{1,0:T(8,128)S(1)} %copy-done.3), channel_id=1, source_target_pairs={{0,1},{1,0},{2,3},{3,2},{4,5},{5,4},{6,7},{7,6},{8,9},{9,8},{10,11... | collective-permute-start | bytes 589832 | tf_op jit(solution)/shard_map/ppermute | solution.py:379
  9.8 2.5 %collective-permute-start.1 = (f32[3,32,64]{2,1,0:T(8,128)S(1)}, f32[3,32,64]{2,1,0:T(8,128)S(1)}, u32[]{:S(2)}, u32[]{:S(2)}) collective-permute-start(f32[3,32,64]{2,1,0:T(8,128)S(1)} %pad_maximum_fusion.table_ref), channel_id=1, source_target_pairs={{0,1},{1,0},{2,3},{3,2},{4,5},{5,4},{6,7},{7,6},{8,9},{9,8},{10,11... | collective-permute-start | bytes 73736 | tf_op jit(solution)/shard_map/ppermute | solution.py:379
  10.1 2.3 %collective-permute-start = (s32[3,64]{1,0:T(4,128)S(1)}, s32[3,64]{1,0:T(4,128)S(1)}, u32[]{:S(2)}, u32[]{:S(2)}) collective-permute-start(s32[3,64]{1,0:T(4,128)S(1)} %pad_add_fusion.facts_ref), channel_id=1, source_target_pairs={{0,1},{1,0},{2,3},{3,2},{4,5},{5,4},{6,7},{7,6},{8,9},{9,8},{10,11... | collective-permute-start | bytes 2312 | tf_op jit(solution)/shard_map/ppermute | solution.py:379
  10.3 1.7 %copy-start = (f32[64,64,32]{1,2,0:T(8,128)S(1)}, f32[64,64,32]{1,2,0:T(8,128)}, u32[]{:S(2)}) copy-start(f32[64,64,32]{1,2,0:T(8,128)} %param.16) | copy-start | bytes 1572868

commit v6 on v5

--- a/solution.py
+++ b/solution.py
@@ -157,8 +157,13 @@
     inner_source_ref,
     inner_target_ref,
     inner_gain_ref,
+    precond_ref,
     inner_ref,
+    packed_ref,
 ):
+    for g in range(packed_ref.shape[0]):
+        parts = [precond_ref[i] for i in range(g, BS, packed_ref.shape[0])]
+        packed_ref[g] = jnp.concatenate(parts, axis=0).T
     updates = jnp.concatenate([table_ref[1], table_ref[2]], axis=1).astype(BF16).astype(F32)
     caps = jnp.concatenate([cap_ref[...], cap_ref[...]], axis=1)
     inner_ref[...] = inner_images(
@@ -181,7 +186,6 @@
     target_out,
     gain_out,
     near_ref,
-    right_ref,
     moved_ref,
     row_hot_ref,
     place_ref,
@@ -191,7 +195,6 @@
     stamp_count = 2 * own_count
     block_count = table_ref.shape[1]
     half = block_count // 2
-    group = NEWTON * GROUP
     later = lax.axis_index("sub") == 1
     tables = []
     for ref in (table_ref, table_other):
@@ -233,61 +236,40 @@
             lanes = slice(at, at + LANES)
             source = sources[:, lanes]
             near_ref[held, lanes] = pick(near, source)
-            moved = pick(near, source + BS).astype(BF16)
-            target = targets[:, lanes]
-            target_out[held, lanes] = (target + upper[held] * BS).astype(F32).astype(BF16)
-            if n > 0:
-                moved_ref[:, lanes] = moved
-                continue
-            low = digits(target)[1]
-            for start in range(0, own_count, group):
-                rows = slice(start, start + group)
-                held_rows = slice(DIGIT * start, DIGIT * (start + group))
-                right_ref[held_rows, lanes] = hot_rows(low[rows], [moved[rows]])
-
+            moved_ref[held, lanes] = pick(near, source + BS).astype(BF16)
+            target = targets[:, lanes] + upper[held] * BS
+            target_out[held, lanes] = target.astype(F32).astype(BF16)
 
 def couple_kernel(
     fields_ref,
     target_ref,
     gain_ref,
     near_ref,
-    right_ref,
     moved_ref,
     row_hot_ref,
     place_ref,
     offset_hot_ref,
     send_ref,
-    left_ref,
-    late_ref,
     product_ref,
 ):
     stamp_count, elements = target_ref.shape
     group = NEWTON * GROUP
     rows_of = DIGIT * group
-    early = right_ref.shape[0] // DIGIT
+    same = same_block((rows_of, rows_of), group)
     remote = dot(row_hot_ref[...], fields_ref[...], NN)
     for start in range(0, stamp_count, group):
         rows = slice(start, start + group)
         held = slice(DIGIT * start, DIGIT * start + rows_of)
+        left, right = [], []
         for at in range(0, elements, LANES):
             lanes = slice(at, at + LANES)
             target = target_ref[rows, lanes].astype(F32).astype(jnp.int32)
             high, low = digits(target & (BS - 1))
-            if start >= early:
-                moved = moved_ref[start - early : start - early + group, lanes]
-                late = slice(held.start - DIGIT * early, held.stop - DIGIT * early)
-                late_ref[late, lanes] = hot_rows(low, [moved])
             far = pick(remote[rows], target)
             weight = conductance(gain_ref[rows, lanes], near_ref[rows, lanes], far)
-            left_ref[held, lanes] = hot_rows(high, [weight.astype(BF16)])
-    same = same_block((rows_of, rows_of), group)
-    for start in range(0, DIGIT * stamp_count, rows_of):
-        held = slice(start, start + rows_of)
-        if start < DIGIT * early:
-            right = right_ref[held, :]
-        else:
-            right = late_ref[start - DIGIT * early : start - DIGIT * early + rows_of, :]
-        product = dot(left_ref[held, :], right, NT)
+            left.append(hot_rows(high, [weight.astype(BF16)]))
+            right.append(hot_rows(low, [moved_ref[rows, lanes]]))
+        product = dot(jnp.concatenate(left, axis=1), jnp.concatenate(right, axis=1), NT)
         product_ref[held, :] = jnp.where(same, product, 0.0).astype(BF16)
     shape = (rows_of, LANES)
     node = iota(shape, 1) - BS
@@ -304,12 +286,6 @@
     images = jnp.concatenate(images, axis=0)
     messages = images.astype(BF16) + offset_hot_ref[...]
     send_ref[...] = dot(place_ref[...], messages, NN).astype(BF16)
-
-
-def pack_kernel(precond_ref, packed_ref):
-    for g in range(packed_ref.shape[0]):
-        parts = [precond_ref[i] for i in range(g, BS, packed_ref.shape[0])]
-        packed_ref[g] = jnp.concatenate(parts, axis=0).T
 
 
 def finish_kernel(row_count, images_ref, inner_ref, packed_ref, out_ref):
@@ -384,17 +360,21 @@
     facts = [fact.reshape(1, stamp_count) for fact in (couple_block, couple_owner, couple_offset)]
     send, facts = lax.optimization_barrier((send, jnp.concatenate(facts, axis=0)))
     fields = exchange(send, devices)
-    inner = call(
+    inner, packed = call(
         inner_kernel,
-        like((NEWTON * BS, block_count), F32),
-        (table, cap_diag.T, inner_source, inner_target, inner_gain),
+        [
+            like((NEWTON * BS, block_count), F32),
+            like((BS * block_count // LANES, BS, LANES), F32),
+        ],
+        (
+            table,
+            cap_diag.T,
+            inner_source,
+            inner_target,
+            inner_gain,
+            preconditioner.transpose(0, 2, 1),
+        ),
         (10**9, 10**6),
-    )
-    packed = call(
-        pack_kernel,
-        like((BS * block_count // LANES, BS, LANES), F32),
-        (preconditioner.transpose(0, 2, 1),),
-        (10**8, 10**6),
     )
     wanted = (facts, table, couple_source, couple_target, couple_gain)
     pairs = [half for array in wanted for half in (array, swap(array))]
@@ -405,8 +385,7 @@
             like((both, elements), BF16),
             like((both, elements), F32),
             like((both, elements), F32),
-            like((DIGIT * stamp_count, elements), BF16),
-            like((stamp_count, elements), BF16),
+            like((both, elements), BF16),
             like((both, devices * block_count // 2), BF16),
             like((row_count, both), BF16),
             like((both, LANES), BF16),
@@ -421,8 +400,6 @@
         (fields, *prepared),
         (4 * 10**9, 10**6),
         [
-            pltpu.VMEM((DIGIT * both, elements), BF16),
-            pltpu.VMEM((DIGIT * stamp_count, elements), BF16),
             pltpu.VMEM((DIGIT * both, DIGIT * NEWTON * GROUP), BF16),
         ],
     )

time: 29.2 us -> 29 us (level)
  Pallas kernels: 6.28 us -> 5.72 us
  waiting for transfers between devices: 3.81 us -> 4.11 us
    pallas_call x6 -> x5, Pallas kernels: 6.28 us -> 5.72 us  [call(): pl.pallas_call(kernel, out_shape=out_shape, in_specs=[spec] * len(args),...]
    all_to_all x1, waiting for transfers between devices: 3.8 us -> 4.1 us  [exchange(): out = lax.all_to_all(shaped, AXES, split_axis=0, concat_axis=0, tiled=True)]
  transfers between devices with their start and end apart: 6 -> 6, of which waited for: 1 -> 1; matrix products, arithmetic and copies ran while one was open for 0% -> 0% of each run, Pallas kernels for 10% -> 9%
where the time goes in v6:
time: 29 us; the launch traced here: 28.7 us
  blocking collectives  9.18 us (32%)
  starting transfers between devices  8.64 us (30%)
  Pallas kernels  5.72 us (20%)
  waiting for transfers between devices  4.11 us (14%)
  other arithmetic  0.78 us (3%)
    all_to_all x1, blocking collectives, exchange(): out = lax.all_to_all(shaped, AXES, split_axis=0, concat_axis=0, tiled=True)  9.18 us
    all_to_all x1, starting transfers between devices, exchange(): out = lax.all_to_all(shaped, AXES, split_axis=0, concat_axis=0, tiled=True)  7.3 us
    pallas_call x5, Pallas kernels, call(): pl.pallas_call(kernel, out_shape=out_shape, in_specs=[spec] * len(args),...  5.72 us
    all_to_all x1, waiting for transfers between devices, exchange(): out = lax.all_to_all(shaped, AXES, split_axis=0, concat_axis=0, tiled=True)  4.1 us
    ppermute x5, starting transfers between devices, per_device(): swap = lambda array: lax.ppermute(array, 'sub', [(0, 1), (1, 0)])  1.34 us
    concatenate x1, other arithmetic, per_device(): jnp.concatenate([voltages.T[None], newton_steps.transpose(0, 2, 1)], axis=0)  0.77 us
  transfers between devices with their start and end apart: 6, of which 1 were waited for; matrix products, arithmetic and copies ran while one was open for 0% of the time, Pallas kernels for 9%

profile of v6, /device:TPU:0, one launch (start us, length us, event | category | flops | bytes accessed | tf_op | source)
XLA Modules:
  0.0 28.7 jit_solution(16255987231550164158)
XLA Ops:
  0.0 0.8 %pad_maximum_fusion.table_ref = f32[3,32,64]{2,1,0:T(8,128)S(1)} fusion(f32[2,32,64]{2,1,0:T(8,128)} %bitcast.19, f32[1,32,64]{2,1,0:T(8,128)} %bitcast.20), kind=kLoop, calls=%fused_computation | loop fusion | flops 6144 | bytes 49152 | tf_op jit(solution)/shard_map/concatenate | solution.py:356
  0.8 0.0 copy-start.8
  0.8 0.0 copy-start.9
  0.8 0.0 copy-start.10
  0.8 0.0 copy-start.1
  0.8 0.0 copy-start.2
  0.8 0.0 copy-start.3
  0.8 0.0 copy-start.4
  0.8 0.0 copy-start.5
  0.9 0.0 copy-start.6
  0.9 0.7 %shard_map.127 = bf16[512,128]{1,0:T(8,128)(2,1)} custom-call(f32[3,32,64]{2,1,0:T(8,128)S(1)} %pad_maximum_fusion.table_ref), custom_call_target="tpu_custom_call" | custom-call | flops 20000000000 | bytes 1000000 | tf_op jit(solution)/shard_map/pallas_call | solution.py:317
  1.6 0.0 copy-start
  1.6 0.0 copy-done.8
  1.6 0.0 copy-done.9
  1.6 0.0 copy-done.10
  1.6 0.0 copy-start.7
  1.6 7.3 %all-to-all-start = ((bf16[32,16,128]{2,1,0:T(8,128)(2,1)}), bf16[32,16,128]{2,1,0:T(8,128)(2,1)S(1)}, u32[]{:S(2)}, u32[]{:S(2)}) async-start(bf16[32,16,128]{2,1,0:T(8,128)(2,1)} %bitcast.6), calls=%async_computation | async-start | bytes 262144 | tf_op jit(solution)/shard_map/all_to_all | solution.py:330
  9.0 0.0 copy-done
  9.0 0.3 %collective-permute-start.2 = (s32[64,768]{1,0:T(8,128)S(1)}, s32[64,768]{1,0:T(8,128)S(1)}, u32[]{:S(2)}, u32[]{:S(2)}) collective-permute-start(s32[64,768]{1,0:T(8,128)S(1)} %copy-done), channel_id=1, source_target_pairs={{0,1},{1,0},{2,3},{3,2},{4,5},{5,4},{6,7},{7,6},{8,9},{9,8},{10,11... | collective-permute-start | bytes 589832 | tf_op jit(solution)/shard_map/ppermute | solution.py:355
  9.3 0.0 copy-done.1
  9.3 0.3 collective-permute-start.3
  9.5 0.0 copy-done.2
  9.6 0.3 collective-permute-start.4
  9.8 0.3 collective-permute-start.1
  10.1 0.3 collective-permute-start
  10.3 0.0 copy-done.3
  10.3 0.0 copy-done.4
  10.3 0.0 copy-done.5
  10.3 0.0 copy-done.6
  10.3 0.0 copy-done.7
  10.3 1.7 %shard_map.128 = (f32[128,32]{1,0:T(8,128)S(1)}, f32[16,64,128]{2,1,0:T(8,128)S(1)}) custom-call(f32[3,32,64]{2,1,0:T(8,128)S(1)} %pad_maximum_fusion.table_ref, f32[32,64]{1,0:T(8,128)S(1)} %bitcast.18, s32[32,768]{1,0:T(8,128)S(1)} %copy-done.4, s32[32,768]{1,0:T(8,128)S(1)} %copy-done.5, f32[32,768]{1,0:T(8,128)S(1)} %copy-done.6, f32[64,32,64]{2,1,0:T(8,128)S(1)} %bitcast.17), custom_call_target="tpu_custom_call" | custom-call | flops 1000000000 | bytes 1000000 | tf_op jit(solution)/shard_map/pallas_call | solution.py:317
  12.0 0.0 collective-permute-done.facts_other
  12.0 0.0 collective-permute-done.1.table_other
  12.0 0.0 collective-permute-done.2.source_other
  12.1 0.0 collective-permute-done.3.target_other
  12.1 0.0 collective-permute-done.4.gain_other
  12.1 1.0 %shard_map.129 = (bf16[128,768]{1,0:T(8,128)(2,1)S(1)}, f32[128,768]{1,0:T(8,128)S(1)}, f32[128,768]{1,0:T(8,128)S(1)}, bf16[128,768]{1,0:T(8,128)(2,1)S(1)}, bf...) custom-call(s32[3,64]{1,0:T(4,128)S(1)} %pad_add_fusion.facts_ref, ...), custom_call_target="tpu_custom_call" | custom-call | flops 100000000 | bytes 1000000 | tf_op jit(solution)/shard_map/pallas_call | solution.py:317
  13.1 4.1 %all-to-all-done = bf16[32,16,128]{2,1,0:T(8,128)(2,1)S(1)} async-done(((bf16[32,16,128]{2,1,0:T(8,128)(2,1)}), bf16[32,16,128]{2,1,0:T(8,128)(2,1)S(1)}, u32[]{:S(2)}, u32[]{:S(2)}) %all-to-all-start) | async-done | bytes 131104 | tf_op jit(solution)/shard_map/all_to_all | solution.py:330
  17.2 1.1 %shard_map.130 = bf16[256,128]{1,0:T(8,128)(2,1)S(1)} custom-call(bf16[512,128]{1,0:T(8,128)(2,1)S(1)} %bitcast.15, bf16[128,768]{1,0:T(8,128)(2,1)S(1)} %get-tuple-element.24.target_ref, f32[128,768]{1,0:T(8,128)S(1)} %get-tuple-element.25.gain_ref, f32[128,768]{1,0:T(8,128)S(1)} %get-tuple-element.26.near_ref, ...), custom_call_target="tpu_custom_call" | custom-call | flops 4000000000 | bytes 1000000 | tf_op jit(solution)/shard_map/pallas_call | solution.py:317
  18.3 9.2 %all_to_all.10 = bf16[32,8,128]{2,1,0:T(8,128)(2,1)S(1)} all-to-all(bf16[32,8,128]{2,1,0:T(8,128)(2,1)S(1)} %bitcast.16), channel_id=1, replica_groups=mesh['dom'=16,'sub'=2] {'dom','sub'}, dimensions={0} | all-to-all | bytes 131072 | tf_op jit(solution)/shard_map/all_to_all | solution.py:330
  27.5 1.2 %shard_map.131 = f32[2,32,64]{2,1,0:T(8,128)} custom-call(bf16[256,128]{1,0:T(8,128)(2,1)S(1)} %bitcast.14, f32[128,32]{1,0:T(8,128)S(1)} %get-tuple-element.31.inner_ref, f32[16,64,128]{2,1,0:T(8,128)S(1)} %get-tuple-element.32.packed_ref), custom_call_target="tpu_custom_call" | custom-call | flops 100000000 | bytes 1000000 | tf_op jit(solution)/shard_map/pallas_call | solution.py:317
  (1 shorter events, 0.0 us)
Async XLA Ops:
  0.8 0.8 %copy-start.8 = (s32[64]{0:T(128)S(1)}, s32[64]{0:T(128)}, u32[]{:S(2)}) copy-start(s32[64]{0:T(128)} %param.19) | copy-start | bytes 772
  0.8 0.8 %copy-start.9 = (s32[64,1]{0,1:T(1,128)S(1)}, s32[64,1]{0,1:T(1,128)}, u32[]{:S(2)}) copy-start(s32[64,1]{0,1:T(1,128)} %param.18) | copy-start | bytes 772
  0.8 0.8 %copy-start.10 = (s32[64]{0:T(128)S(1)}, s32[64]{0:T(128)}, u32[]{:S(2)}) copy-start(s32[64]{0:T(128)} %param.17) | copy-start | bytes 772
  0.8 8.5 %copy-start.1 = (s32[64,768]{1,0:T(8,128)S(1)}, s32[64,768]{1,0:T(8,128)}, u32[]{:S(2)}) copy-start(s32[64,768]{1,0:T(8,128)} %target_ref.1) | copy-start | bytes 589828
  0.8 8.7 %copy-start.2 = (f32[64,768]{1,0:T(8,128)S(1)}, f32[64,768]{1,0:T(8,128)}, u32[]{:S(2)}) copy-start(f32[64,768]{1,0:T(8,128)} %gain_ref.1) | copy-start | bytes 589828
  0.8 9.5 %copy-start.3 = (f32[64,64,32]{1,2,0:T(8,128)S(1)}, f32[64,64,32]{1,2,0:T(8,128)}, u32[]{:S(2)}) copy-start(f32[64,64,32]{1,2,0:T(8,128)} %param.16) | copy-start | bytes 1572868
  0.8 9.5 %copy-start.4 = (s32[32,768]{1,0:T(8,128)S(1)}, s32[32,768]{1,0:T(8,128)}, u32[]{:S(2)}) copy-start(s32[32,768]{1,0:T(8,128)} %inner_source_ref.1) | copy-start | bytes 294916
  0.8 9.5 %copy-start.5 = (s32[32,768]{1,0:T(8,128)S(1)}, s32[32,768]{1,0:T(8,128)}, u32[]{:S(2)}) copy-start(s32[32,768]{1,0:T(8,128)} %inner_target_ref.1) | copy-start | bytes 294916
  0.9 9.5 %copy-start.6 = (f32[32,768]{1,0:T(8,128)S(1)}, f32[32,768]{1,0:T(8,128)}, u32[]{:S(2)}) copy-start(f32[32,768]{1,0:T(8,128)} %inner_gain_ref.1) | copy-start | bytes 294916
  1.6 7.4 %copy-start = (s32[64,768]{1,0:T(8,128)S(1)}, s32[64,768]{1,0:T(8,128)}, u32[]{:S(2)}) copy-start(s32[64,768]{1,0:T(8,128)} %source_ref.1) | copy-start | bytes 589828
  1.6 8.7 %copy-start.7 = (f32[64,32]{0,1:T(8,128)S(1)}, f32[64,32]{0,1:T(8,128)}, u32[]{:S(2)}) copy-start(f32[64,32]{0,1:T(8,128)} %param.15) | copy-start | bytes 24580
  1.6 15.5 %all-to-all-start = ((bf16[32,16,128]{2,1,0:T(8,128)(2,1)}), bf16[32,16,128]{2,1,0:T(8,128)(2,1)S(1)}, u32[]{:S(2)}, u32[]{:S(2)}) async-start(bf16[32,16,128]{2,1,0:T(8,128)(2,1)} %bitcast.6), calls=%async_computation | async-start | bytes 262144 | tf_op jit(solution)/shard_map/all_to_all | solution.py:330
  9.0 3.1 %collective-permute-start.2 = (s32[64,768]{1,0:T(8,128)S(1)}, s32[64,768]{1,0:T(8,128)S(1)}, u32[]{:S(2)}, u32[]{:S(2)}) collective-permute-start(s32[64,768]{1,0:T(8,128)S(1)} %copy-done), channel_id=1, source_target_pairs={{0,1},{1,0},{2,3},{3,2},{4,5},{5,4},{6,7},{7,6},{8,9},{9,8},{10,11... | collective-permute-start | bytes 589832 | tf_op jit(solution)/shard_map/ppermute | solution.py:355
  9.3 2.8 %collective-permute-start.3 = (s32[64,768]{1,0:T(8,128)S(1)}, s32[64,768]{1,0:T(8,128)S(1)}, u32[]{:S(2)}, u32[]{:S(2)}) collective-permute-start(s32[64,768]{1,0:T(8,128)S(1)} %copy-done.1), channel_id=1, source_target_pairs={{0,1},{1,0},{2,3},{3,2},{4,5},{5,4},{6,7},{7,6},{8,9},{9,8},{10,11... | collective-permute-start | bytes 589832 | tf_op jit(solution)/shard_map/ppermute | solution.py:355
  9.6 2.5 %collective-permute-start.4 = (f32[64,768]{1,0:T(8,128)S(1)}, f32[64,768]{1,0:T(8,128)S(1)}, u32[]{:S(2)}, u32[]{:S(2)}) collective-permute-start(f32[64,768]{1,0:T(8,128)S(1)} %copy-done.2), channel_id=1, source_target_pairs={{0,1},{1,0},{2,3},{3,2},{4,5},{5,4},{6,7},{7,6},{8,9},{9,8},{10,11... | collective-permute-start | bytes 589832 | tf_op jit(solution)/shard_map/ppermute | solution.py:355
  9.8 2.2 %collective-permute-start.1 = (f32[3,32,64]{2,1,0:T(8,128)S(1)}, f32[3,32,64]{2,1,0:T(8,128)S(1)}, u32[]{:S(2)}, u32[]{:S(2)}) collective-permute-start(f32[3,32,64]{2,1,0:T(8,128)S(1)} %pad_maximum_fusion.table_ref), channel_id=1, source_target_pairs={{0,1},{1,0},{2,3},{3,2},{4,5},{5,4},{6,7},{7,6},{8,9},{9,8},{10,11... | collective-permute-start | bytes 73736 | tf_op jit(solution)/shard_map/ppermute | solution.py:355
  10.1 2.0 %collective-permute-start = (s32[3,64]{1,0:T(4,128)S(1)}, s32[3,64]{1,0:T(4,128)S(1)}, u32[]{:S(2)}, u32[]{:S(2)}) collective-permute-start(s32[3,64]{1,0:T(4,128)S(1)} %pad_add_fusion.facts_ref), channel_id=1, source_target_pairs={{0,1},{1,0},{2,3},{3,2},{4,5},{5,4},{6,7},{7,6},{8,9},{9,8},{10,11... | collective-permute-start | bytes 2312 | tf_op jit(solution)/shard_map/ppermute | solution.py:355

commit v7 on v6

--- a/solution.py
+++ b/solution.py
@@ -99,8 +99,9 @@
         jnp.concatenate([field[:half], field[half:]], axis=1).astype(BF16)
         for field in (first, first + table_ref[1])
     ]
-    for d in range(send_ref.shape[0] // half):
-        send_ref[pl.ds(d * half, half), :] = packed[d % NEWTON]
+    devices = send_ref.shape[0] // half
+    for d in range(devices):
+        send_ref[pl.ds(d * half, half), :] = packed[d * NEWTON // devices]
 
 
 def inner_images(volt_rows, update_rows, cap_rows, source_ref, target_ref, gain_ref):
@@ -205,6 +206,9 @@
 
     facts = jnp.concatenate([facts_ref[...], facts_other[...]], axis=1).astype(F32)
     block_row, owner_row, offset_row = facts[0:1], facts[1:2], facts[2:3]
+    chip_row = jnp.floor(owner_row * 0.5)
+    chips = row_hot_ref.shape[1] // (NEWTON * half)
+    owner_row = (owner_row - NEWTON * chip_row) * chips + chip_row
     mine = iota((1, stamp_count), 1) < own_count
     block = row_to_column(jnp.where(mine, block_row, block_row + block_count))
     owner = row_to_column(owner_row)
@@ -292,7 +296,7 @@
     received = images_ref[...]
     block_count = inner_ref.shape[1]
     parts = LANES // block_count
-    step = iota(received.shape, 0) // row_count % NEWTON
+    step = iota(received.shape, 0) // (received.shape[0] // NEWTON)
     totals = []
     for t in range(NEWTON):
         mine = jnp.where(step == t, received.astype(F32), 0.0).astype(BF16)
@@ -327,7 +331,7 @@
 
 def exchange(rows, devices):
     shaped = rows.reshape((devices, rows.shape[0] // devices, rows.shape[1]))
-    out = lax.all_to_all(shaped, AXES, split_axis=0, concat_axis=0, tiled=True)
+    out = lax.all_to_all(shaped, AXES[::-1], split_axis=0, concat_axis=0, tiled=True)
     return out.reshape(rows.shape)
 
 

time: 29 us -> 28.8 us (level)
  no operation moved by 1% of the time
where the time goes in v7:
time: 28.8 us; the launch traced here: 28.5 us
  blocking collectives  9.33 us (32%)
  starting transfers between devices  8.64 us (30%)
  Pallas kernels  5.66 us (20%)
  waiting for transfers between devices  3.85 us (13%)
  other arithmetic  0.78 us (3%)
    all_to_all x1, blocking collectives, exchange(): lax.all_to_all(shaped, AXES[::-1], split_axis=0, concat_axis=0, tiled=True)  9.33 us
    all_to_all x1, starting transfers between devices, exchange(): lax.all_to_all(shaped, AXES[::-1], split_axis=0, concat_axis=0, tiled=True)  7.3 us
    pallas_call x5, Pallas kernels, call(): pl.pallas_call(kernel, out_shape=out_shape, in_specs=[spec] * len(args),...  5.66 us
    all_to_all x1, waiting for transfers between devices, exchange(): lax.all_to_all(shaped, AXES[::-1], split_axis=0, concat_axis=0, tiled=True)  3.84 us
    ppermute x5, starting transfers between devices, per_device(): swap = lambda array: lax.ppermute(array, 'sub', [(0, 1), (1, 0)])  1.34 us
    concatenate x1, other arithmetic, per_device(): jnp.concatenate([voltages.T[None], newton_steps.transpose(0, 2, 1)], axis=0)  0.77 us
  transfers between devices with their start and end apart: 6, of which 1 were waited for; matrix products, arithmetic and copies ran while one was open for 0% of the time, Pallas kernels for 9%

profile of v7, /device:TPU:0, one launch (start us, length us, event | category | flops | bytes accessed | tf_op | source)
XLA Modules:
  0.0 28.5 jit_solution(1526379381965413990)
XLA Ops:
  0.0 0.8 %pad_maximum_fusion.table_ref = f32[3,32,64]{2,1,0:T(8,128)S(1)} fusion(f32[2,32,64]{2,1,0:T(8,128)} %bitcast.19, f32[1,32,64]{2,1,0:T(8,128)} %bitcast.20), kind=kLoop, calls=%fused_computation | loop fusion | flops 6144 | bytes 49152 | tf_op jit(solution)/shard_map/concatenate | solution.py:360
  0.8 0.0 copy-start.8
  0.8 0.0 copy-start.9
  0.8 0.0 copy-start.10
  0.8 0.0 copy-start.1
  0.8 0.0 copy-start.2
  0.8 0.0 copy-start.3
  0.8 0.0 copy-start.4
  0.8 0.0 copy-start.5
  0.9 0.0 copy-start.6
  0.9 0.7 %shard_map.127 = bf16[512,128]{1,0:T(8,128)(2,1)} custom-call(f32[3,32,64]{2,1,0:T(8,128)S(1)} %pad_maximum_fusion.table_ref), custom_call_target="tpu_custom_call" | custom-call | flops 20000000000 | bytes 1000000 | tf_op jit(solution)/shard_map/pallas_call | solution.py:321
  1.6 0.0 copy-start
  1.6 0.0 copy-done.8
  1.6 0.0 copy-done.9
  1.6 0.0 copy-done.10
  1.6 0.0 copy-start.7
  1.6 7.3 %all-to-all-start = ((bf16[32,16,128]{2,1,0:T(8,128)(2,1)}), bf16[32,16,128]{2,1,0:T(8,128)(2,1)S(1)}, u32[]{:S(2)}, u32[]{:S(2)}) async-start(bf16[32,16,128]{2,1,0:T(8,128)(2,1)} %bitcast.6), calls=%async_computation | async-start | bytes 262144 | tf_op jit(solution)/shard_map/all_to_all | solution.py:334
  9.0 0.0 copy-done
  9.0 0.3 %collective-permute-start.2 = (s32[64,768]{1,0:T(8,128)S(1)}, s32[64,768]{1,0:T(8,128)S(1)}, u32[]{:S(2)}, u32[]{:S(2)}) collective-permute-start(s32[64,768]{1,0:T(8,128)S(1)} %copy-done), channel_id=1, source_target_pairs={{0,1},{1,0},{2,3},{3,2},{4,5},{5,4},{6,7},{7,6},{8,9},{9,8},{10,11... | collective-permute-start | bytes 589832 | tf_op jit(solution)/shard_map/ppermute | solution.py:359
  9.3 0.0 copy-done.1
  9.3 0.3 collective-permute-start.3
  9.5 0.0 copy-done.2
  9.6 0.3 collective-permute-start.4
  9.8 0.3 collective-permute-start.1
  10.1 0.3 collective-permute-start
  10.3 0.0 copy-done.3
  10.3 0.0 copy-done.4
  10.3 0.0 copy-done.5
  10.3 0.0 copy-done.6
  10.3 0.0 copy-done.7
  10.3 1.7 %shard_map.128 = (f32[128,32]{1,0:T(8,128)S(1)}, f32[16,64,128]{2,1,0:T(8,128)S(1)}) custom-call(f32[3,32,64]{2,1,0:T(8,128)S(1)} %pad_maximum_fusion.table_ref, f32[32,64]{1,0:T(8,128)S(1)} %bitcast.18, s32[32,768]{1,0:T(8,128)S(1)} %copy-done.4, s32[32,768]{1,0:T(8,128)S(1)} %copy-done.5, f32[32,768]{1,0:T(8,128)S(1)} %copy-done.6, f32[64,32,64]{2,1,0:T(8,128)S(1)} %bitcast.17), custom_call_target="tpu_custom_call" | custom-call | flops 1000000000 | bytes 1000000 | tf_op jit(solution)/shard_map/pallas_call | solution.py:321
  12.0 0.0 collective-permute-done.facts_other
  12.0 0.0 collective-permute-done.1.table_other
  12.0 0.0 collective-permute-done.2.source_other
  12.1 0.0 collective-permute-done.3.target_other
  12.1 0.0 collective-permute-done.4.gain_other
  12.1 1.0 %shard_map.129 = (bf16[128,768]{1,0:T(8,128)(2,1)S(1)}, f32[128,768]{1,0:T(8,128)S(1)}, f32[128,768]{1,0:T(8,128)S(1)}, bf16[128,768]{1,0:T(8,128)(2,1)S(1)}, bf...) custom-call(s32[3,64]{1,0:T(4,128)S(1)} %pad_add_fusion.facts_ref, ...), custom_call_target="tpu_custom_call" | custom-call | flops 100000000 | bytes 1000000 | tf_op jit(solution)/shard_map/pallas_call | solution.py:321
  13.0 3.8 %all-to-all-done = bf16[32,16,128]{2,1,0:T(8,128)(2,1)S(1)} async-done(((bf16[32,16,128]{2,1,0:T(8,128)(2,1)}), bf16[32,16,128]{2,1,0:T(8,128)(2,1)S(1)}, u32[]{:S(2)}, u32[]{:S(2)}) %all-to-all-start) | async-done | bytes 131104 | tf_op jit(solution)/shard_map/all_to_all | solution.py:334
  16.9 1.1 %shard_map.130 = bf16[256,128]{1,0:T(8,128)(2,1)S(1)} custom-call(bf16[512,128]{1,0:T(8,128)(2,1)S(1)} %bitcast.15, bf16[128,768]{1,0:T(8,128)(2,1)S(1)} %get-tuple-element.24.target_ref, f32[128,768]{1,0:T(8,128)S(1)} %get-tuple-element.25.gain_ref, f32[128,768]{1,0:T(8,128)S(1)} %get-tuple-element.26.near_ref, ...), custom_call_target="tpu_custom_call" | custom-call | flops 4000000000 | bytes 1000000 | tf_op jit(solution)/shard_map/pallas_call | solution.py:321
  18.0 9.3 %all_to_all.10 = bf16[32,8,128]{2,1,0:T(8,128)(2,1)S(1)} all-to-all(bf16[32,8,128]{2,1,0:T(8,128)(2,1)S(1)} %bitcast.16), channel_id=1, replica_groups=mesh['dom'=16,'sub'=2] {'sub','dom'}, dimensions={0} | all-to-all | bytes 131072 | tf_op jit(solution)/shard_map/all_to_all | solution.py:334
  27.3 1.2 %shard_map.131 = f32[2,32,64]{2,1,0:T(8,128)} custom-call(bf16[256,128]{1,0:T(8,128)(2,1)S(1)} %bitcast.14, f32[128,32]{1,0:T(8,128)S(1)} %get-tuple-element.31.inner_ref, f32[16,64,128]{2,1,0:T(8,128)S(1)} %get-tuple-element.32.packed_ref), custom_call_target="tpu_custom_call" | custom-call | flops 100000000 | bytes 1000000 | tf_op jit(solution)/shard_map/pallas_call | solution.py:321
  (1 shorter events, 0.0 us)
Async XLA Ops:
  0.8 0.8 %copy-start.8 = (s32[64]{0:T(128)S(1)}, s32[64]{0:T(128)}, u32[]{:S(2)}) copy-start(s32[64]{0:T(128)} %param.19) | copy-start | bytes 772
  0.8 0.8 %copy-start.9 = (s32[64,1]{0,1:T(1,128)S(1)}, s32[64,1]{0,1:T(1,128)}, u32[]{:S(2)}) copy-start(s32[64,1]{0,1:T(1,128)} %param.18) | copy-start | bytes 772
  0.8 0.8 %copy-start.10 = (s32[64]{0:T(128)S(1)}, s32[64]{0:T(128)}, u32[]{:S(2)}) copy-start(s32[64]{0:T(128)} %param.17) | copy-start | bytes 772
  0.8 8.5 %copy-start.1 = (s32[64,768]{1,0:T(8,128)S(1)}, s32[64,768]{1,0:T(8,128)}, u32[]{:S(2)}) copy-start(s32[64,768]{1,0:T(8,128)} %target_ref.1) | copy-start | bytes 589828
  0.8 8.7 %copy-start.2 = (f32[64,768]{1,0:T(8,128)S(1)}, f32[64,768]{1,0:T(8,128)}, u32[]{:S(2)}) copy-start(f32[64,768]{1,0:T(8,128)} %gain_ref.1) | copy-start | bytes 589828
  0.8 9.5 %copy-start.3 = (f32[64,64,32]{1,2,0:T(8,128)S(1)}, f32[64,64,32]{1,2,0:T(8,128)}, u32[]{:S(2)}) copy-start(f32[64,64,32]{1,2,0:T(8,128)} %param.16) | copy-start | bytes 1572868
  0.8 9.5 %copy-start.4 = (s32[32,768]{1,0:T(8,128)S(1)}, s32[32,768]{1,0:T(8,128)}, u32[]{:S(2)}) copy-start(s32[32,768]{1,0:T(8,128)} %inner_source_ref.1) | copy-start | bytes 294916
  0.8 9.5 %copy-start.5 = (s32[32,768]{1,0:T(8,128)S(1)}, s32[32,768]{1,0:T(8,128)}, u32[]{:S(2)}) copy-start(s32[32,768]{1,0:T(8,128)} %inner_target_ref.1) | copy-start | bytes 294916
  0.9 9.5 %copy-start.6 = (f32[32,768]{1,0:T(8,128)S(1)}, f32[32,768]{1,0:T(8,128)}, u32[]{:S(2)}) copy-start(f32[32,768]{1,0:T(8,128)} %inner_gain_ref.1) | copy-start | bytes 294916
  1.6 7.4 %copy-start = (s32[64,768]{1,0:T(8,128)S(1)}, s32[64,768]{1,0:T(8,128)}, u32[]{:S(2)}) copy-start(s32[64,768]{1,0:T(8,128)} %source_ref.1) | copy-start | bytes 589828
  1.6 8.7 %copy-start.7 = (f32[64,32]{0,1:T(8,128)S(1)}, f32[64,32]{0,1:T(8,128)}, u32[]{:S(2)}) copy-start(f32[64,32]{0,1:T(8,128)} %param.15) | copy-start | bytes 24580
  1.6 15.2 %all-to-all-start = ((bf16[32,16,128]{2,1,0:T(8,128)(2,1)}), bf16[32,16,128]{2,1,0:T(8,128)(2,1)S(1)}, u32[]{:S(2)}, u32[]{:S(2)}) async-start(bf16[32,16,128]{2,1,0:T(8,128)(2,1)} %bitcast.6), calls=%async_computation | async-start | bytes 262144 | tf_op jit(solution)/shard_map/all_to_all | solution.py:334
  9.0 3.1 %collective-permute-start.2 = (s32[64,768]{1,0:T(8,128)S(1)}, s32[64,768]{1,0:T(8,128)S(1)}, u32[]{:S(2)}, u32[]{:S(2)}) collective-permute-start(s32[64,768]{1,0:T(8,128)S(1)} %copy-done), channel_id=1, source_target_pairs={{0,1},{1,0},{2,3},{3,2},{4,5},{5,4},{6,7},{7,6},{8,9},{9,8},{10,11... | collective-permute-start | bytes 589832 | tf_op jit(solution)/shard_map/ppermute | solution.py:359
  9.3 2.8 %collective-permute-start.3 = (s32[64,768]{1,0:T(8,128)S(1)}, s32[64,768]{1,0:T(8,128)S(1)}, u32[]{:S(2)}, u32[]{:S(2)}) collective-permute-start(s32[64,768]{1,0:T(8,128)S(1)} %copy-done.1), channel_id=1, source_target_pairs={{0,1},{1,0},{2,3},{3,2},{4,5},{5,4},{6,7},{7,6},{8,9},{9,8},{10,11... | collective-permute-start | bytes 589832 | tf_op jit(solution)/shard_map/ppermute | solution.py:359
  9.6 2.5 %collective-permute-start.4 = (f32[64,768]{1,0:T(8,128)S(1)}, f32[64,768]{1,0:T(8,128)S(1)}, u32[]{:S(2)}, u32[]{:S(2)}) collective-permute-start(f32[64,768]{1,0:T(8,128)S(1)} %copy-done.2), channel_id=1, source_target_pairs={{0,1},{1,0},{2,3},{3,2},{4,5},{5,4},{6,7},{7,6},{8,9},{9,8},{10,11... | collective-permute-start | bytes 589832 | tf_op jit(solution)/shard_map/ppermute | solution.py:359
  9.8 2.2 %collective-permute-start.1 = (f32[3,32,64]{2,1,0:T(8,128)S(1)}, f32[3,32,64]{2,1,0:T(8,128)S(1)}, u32[]{:S(2)}, u32[]{:S(2)}) collective-permute-start(f32[3,32,64]{2,1,0:T(8,128)S(1)} %pad_maximum_fusion.table_ref), channel_id=1, source_target_pairs={{0,1},{1,0},{2,3},{3,2},{4,5},{5,4},{6,7},{7,6},{8,9},{9,8},{10,11... | collective-permute-start | bytes 73736 | tf_op jit(solution)/shard_map/ppermute | solution.py:359
  10.1 2.0 %collective-permute-start = (s32[3,64]{1,0:T(4,128)S(1)}, s32[3,64]{1,0:T(4,128)S(1)}, u32[]{:S(2)}, u32[]{:S(2)}) collective-permute-start(s32[3,64]{1,0:T(4,128)S(1)} %pad_add_fusion.facts_ref), channel_id=1, source_target_pairs={{0,1},{1,0},{2,3},{3,2},{4,5},{5,4},{6,7},{7,6},{8,9},{9,8},{10,11... | collective-permute-start | bytes 2312 | tf_op jit(solution)/shard_map/ppermute | solution.py:359

commit v8 on v7

--- a/solution.py
+++ b/solution.py
@@ -91,13 +91,13 @@
     return jnp.concatenate([first, first + table_ref[1]], axis=1)
 
 
-def prepare_kernel(table_ref, send_ref):
-    block_count = table_ref.shape[1]
+def prepare_kernel(volt_ref, step_ref, send_ref):
+    block_count = volt_ref.shape[0]
     half = block_count // 2
-    first = table_ref[0]
+    first = volt_ref[...]
     packed = [
         jnp.concatenate([field[:half], field[half:]], axis=1).astype(BF16)
-        for field in (first, first + table_ref[1])
+        for field in (first, first + step_ref[...])
     ]
     devices = send_ref.shape[0] // half
     for d in range(devices):
@@ -234,12 +234,12 @@
         ((source_ref, target_ref, gain_ref), (source_other, target_other, gain_other))
     ):
         held = slice(n * own_count, (n + 1) * own_count)
-        gain_out[held, :] = -gains[...]
+        gain_out[held, :] = (-gains[...]).astype(BF16)
         near = local[held]
         for at in range(0, elements, LANES):
             lanes = slice(at, at + LANES)
             source = sources[:, lanes]
-            near_ref[held, lanes] = pick(near, source)
+            near_ref[held, lanes] = pick(near, source).astype(BF16)
             moved_ref[held, lanes] = pick(near, source + BS).astype(BF16)
             target = targets[:, lanes] + upper[held] * BS
             target_out[held, lanes] = target.astype(F32).astype(BF16)
@@ -270,7 +270,8 @@
             target = target_ref[rows, lanes].astype(F32).astype(jnp.int32)
             high, low = digits(target & (BS - 1))
             far = pick(remote[rows], target)
-            weight = conductance(gain_ref[rows, lanes], near_ref[rows, lanes], far)
+            gain, near = gain_ref[rows, lanes].astype(F32), near_ref[rows, lanes].astype(F32)
+            weight = conductance(gain, near, far)
             left.append(hot_rows(high, [weight.astype(BF16)]))
             right.append(hot_rows(low, [moved_ref[rows, lanes]]))
         product = dot(jnp.concatenate(left, axis=1), jnp.concatenate(right, axis=1), NT)
@@ -359,7 +360,7 @@
     swap = lambda array: lax.ppermute(array, "sub", [(0, 1), (1, 0)])
     table = jnp.concatenate([voltages.T[None], newton_steps.transpose(0, 2, 1)], axis=0)
     send = call(
-        prepare_kernel, like((devices * block_count // 2, LANES), BF16), (table,), (2 * 10**10, 10**6)
+        prepare_kernel, like((devices * block_count // 2, LANES), BF16), (voltages.T, newton_steps[0].T), (2 * 10**10, 10**6)
     )
     facts = [fact.reshape(1, stamp_count) for fact in (couple_block, couple_owner, couple_offset)]
     send, facts = lax.optimization_barrier((send, jnp.concatenate(facts, axis=0)))
@@ -387,8 +388,8 @@
         functools.partial(stamp_kernel, per_owner),
         [
             like((both, elements), BF16),
-            like((both, elements), F32),
-            like((both, elements), F32),
+            like((both, elements), BF16),
+            like((both, elements), BF16),
             like((both, elements), BF16),
             like((both, devices * block_count // 2), BF16),
             like((row_count, both), BF16),

time: 28.8 us -> 28.9 us (level)
  other arithmetic: 0.78 us -> 0.02 us
  local copies, waits for them, and re-layouts: 0.06 us -> 0.8 us
    concatenate x1, other arithmetic: 0.77 us -> 0.01 us  [per_device(): jnp.concatenate([voltages.T[None], newton_steps.transpose(0, 2, 1)], axis=0)]
    transpose x0 -> x1, local copies, waits for them, and re-layouts: none -> 0.73 us  [per_device(): newton_steps[0]]
where the time goes in v8:
time: 28.9 us; the launch traced here: 28.5 us
  blocking collectives  9.33 us (32%)
  starting transfers between devices  8.7 us (30%)
  Pallas kernels  5.69 us (20%)
  waiting for transfers between devices  3.76 us (13%)
  local copies, waits for them, and re-layouts  0.8 us (3%)
    all_to_all x1, blocking collectives, exchange(): lax.all_to_all(shaped, AXES[::-1], split_axis=0, concat_axis=0, tiled=True)  9.33 us
    all_to_all x1, starting transfers between devices, exchange(): lax.all_to_all(shaped, AXES[::-1], split_axis=0, concat_axis=0, tiled=True)  7.3 us
    pallas_call x5, Pallas kernels, call(): pl.pallas_call(kernel, out_shape=out_shape, in_specs=[spec] * len(args),...  5.69 us
    all_to_all x1, waiting for transfers between devices, exchange(): lax.all_to_all(shaped, AXES[::-1], split_axis=0, concat_axis=0, tiled=True)  3.75 us
    ppermute x5, starting transfers between devices, per_device(): swap = lambda array: lax.ppermute(array, 'sub', [(0, 1), (1, 0)])  1.4 us
    transpose x1, local copies, waits for them, and re-layouts, per_device(): newton_steps[0]  0.73 us
  transfers between devices with their start and end apart: 6, of which 1 were waited for; matrix products, arithmetic and copies ran while one was open for 0% of the time, Pallas kernels for 9%

profile of v8, /device:TPU:0, one launch (start us, length us, event | category | flops | bytes accessed | tf_op | source)
XLA Modules:
  0.0 28.5 jit_solution(2307285749286046890)
XLA Ops:
  0.0 0.0 copy-start.3
  0.0 0.7 %slice_bitcast_fusion.step_ref = f32[32,64]{1,0:T(8,128)S(1)} fusion(f32[2,64,32]{1,2,0:T(8,128)} %param.14), kind=kLoop, calls=%fused_computation.1 | loop fusion | bytes 16384 | tf_op jit(solution)/shard_map/transpose | solution.py:363
  0.7 0.0 copy-done.3
  0.7 0.0 copy-start.10
  0.7 0.0 copy-start.11
  0.7 0.0 copy-start.12
  0.7 0.0 copy-start.1
  0.8 0.0 copy-start.2
  0.8 0.0 copy-start.4
  0.8 0.0 copy-start.6
  0.8 0.0 copy-start.7
  0.8 0.0 copy-start.8
  0.8 0.7 %shard_map.127 = bf16[512,128]{1,0:T(8,128)(2,1)} custom-call(f32[32,64]{1,0:T(8,128)S(1)} %bitcast.21, f32[32,64]{1,0:T(8,128)S(1)} %slice_bitcast_fusion.step_ref), custom_call_target="tpu_custom_call" | custom-call | flops 20000000000 | bytes 1000000 | tf_op jit(solution)/shard_map/pallas_call | solution.py:322
  1.5 0.0 copy-start
  1.6 0.0 copy-done.10
  1.6 0.0 copy-done.11
  1.6 0.0 copy-done.12
  1.6 0.0 copy-start.9
  1.6 7.3 %all-to-all-start = ((bf16[32,16,128]{2,1,0:T(8,128)(2,1)}), bf16[32,16,128]{2,1,0:T(8,128)(2,1)S(1)}, u32[]{:S(2)}, u32[]{:S(2)}) async-start(bf16[32,16,128]{2,1,0:T(8,128)(2,1)} %bitcast.6), calls=%async_computation | async-start | bytes 262144 | tf_op jit(solution)/shard_map/all_to_all | solution.py:335
  8.9 0.0 copy-done
  8.9 0.0 copy-start.5
  8.9 0.3 %collective-permute-start.2 = (s32[64,768]{1,0:T(8,128)S(1)}, s32[64,768]{1,0:T(8,128)S(1)}, u32[]{:S(2)}, u32[]{:S(2)}) collective-permute-start(s32[64,768]{1,0:T(8,128)S(1)} %copy-done), channel_id=1, source_target_pairs={{0,1},{1,0},{2,3},{3,2},{4,5},{5,4},{6,7},{7,6},{8,9},{9,8},{10,11... | collective-permute-start | bytes 589832 | tf_op jit(solution)/shard_map/ppermute | solution.py:360
  9.2 0.0 copy-done.1
  9.2 0.3 collective-permute-start.3
  9.5 0.0 copy-done.2
  9.5 0.3 collective-permute-start.4
  9.8 0.0 copy-done.9
  9.8 0.3 %collective-permute-start.1 = (f32[3,32,64]{2,1,0:T(8,128)S(1)}, f32[3,32,64]{2,1,0:T(8,128)S(1)}, u32[]{:S(2)}, u32[]{:S(2)}) collective-permute-start(f32[3,32,64]{2,1,0:T(8,128)S(1)} %pad_maximum_fusion.table_ref), channel_id=1, source_target_pairs={{0,1},{1,0},{2,3},{3,2},{4,5},{5,4},{6,7},{7,6},{8,9},{9,8},{10,11... | collective-permute-start | bytes 73736 | tf_op jit(solution)/shard_map/ppermute | solution.py:360
  10.1 0.3 collective-permute-start
  10.3 0.0 copy-done.4
  10.3 0.0 copy-done.6
  10.3 0.0 copy-done.7
  10.4 0.0 copy-done.8
  10.4 0.0 copy-done.5
  10.4 1.7 %shard_map.128 = (f32[128,32]{1,0:T(8,128)S(1)}, f32[16,64,128]{2,1,0:T(8,128)S(1)}) custom-call(f32[3,32,64]{2,1,0:T(8,128)S(1)} %pad_maximum_fusion.table_ref, f32[32,64]{1,0:T(8,128)S(1)} %bitcast.24, s32[32,768]{1,0:T(8,128)S(1)} %copy-done.5, s32[32,768]{1,0:T(8,128)S(1)} %copy-done.6, f32[32,768]{1,0:T(8,128)S(1)} %copy-done.7, f32[64,32,64]{2,1,0:T(8,128)S(1)} %bitcast.23), custom_call_target="tpu_custom_call" | custom-call | flops 1000000000 | bytes 1000000 | tf_op jit(solution)/shard_map/pallas_call | solution.py:322
  12.1 0.0 collective-permute-done.facts_other
  12.1 0.0 collective-permute-done.1.table_other
  12.1 0.0 collective-permute-done.2.source_other
  12.1 0.0 collective-permute-done.3.target_other
  12.1 0.0 collective-permute-done.4.gain_other
  12.1 1.0 %shard_map.129 = (bf16[128,768]{1,0:T(8,128)(2,1)S(1)}, bf16[128,768]{1,0:T(8,128)(2,1)S(1)}, bf16[128,768]{1,0:T(8,128)(2,1)S(1)}, bf16[128,768]{1,0:T(8,128)(2...) custom-call(s32[3,64]{1,0:T(4,128)S(1)} %pad_add_fusion.facts_ref, ...), custom_call_target="tpu_custom_call" | custom-call | flops 100000000 | bytes 1000000 | tf_op jit(solution)/shard_map/pallas_call | solution.py:322
  13.1 3.7 %all-to-all-done = bf16[32,16,128]{2,1,0:T(8,128)(2,1)S(1)} async-done(((bf16[32,16,128]{2,1,0:T(8,128)(2,1)}), bf16[32,16,128]{2,1,0:T(8,128)(2,1)S(1)}, u32[]{:S(2)}, u32[]{:S(2)}) %all-to-all-start) | async-done | bytes 131104 | tf_op jit(solution)/shard_map/all_to_all | solution.py:335
  16.8 1.2 %shard_map.130 = bf16[256,128]{1,0:T(8,128)(2,1)S(1)} custom-call(bf16[512,128]{1,0:T(8,128)(2,1)S(1)} %bitcast.19, bf16[128,768]{1,0:T(8,128)(2,1)S(1)} %get-tuple-element.24.target_ref, bf16[128,768]{1,0:T(8,128)(2,1)S(1)} %get-tuple-element.25.gain_ref, bf16[128,768]{1,0:T(8,128)(2,1)S(1)} %get-tuple-element.26.near_ref, ...), custom_call_target="tpu_custom_call" | custom-call | flops 4000000000 | bytes 1000000 | tf_op jit(solution)/shard_map/pallas_call | solution.py:322
  18.0 9.3 %all_to_all.10 = bf16[32,8,128]{2,1,0:T(8,128)(2,1)S(1)} all-to-all(bf16[32,8,128]{2,1,0:T(8,128)(2,1)S(1)} %bitcast.20), channel_id=1, replica_groups=mesh['dom'=16,'sub'=2] {'sub','dom'}, dimensions={0} | all-to-all | bytes 131072 | tf_op jit(solution)/shard_map/all_to_all | solution.py:335
  27.3 1.2 %shard_map.131 = f32[2,32,64]{2,1,0:T(8,128)} custom-call(bf16[256,128]{1,0:T(8,128)(2,1)S(1)} %bitcast.18, f32[128,32]{1,0:T(8,128)S(1)} %get-tuple-element.31.inner_ref, f32[16,64,128]{2,1,0:T(8,128)S(1)} %get-tuple-element.32.packed_ref), custom_call_target="tpu_custom_call" | custom-call | flops 100000000 | bytes 1000000 | tf_op jit(solution)/shard_map/pallas_call | solution.py:322
  (2 shorter events, 0.0 us)
Async XLA Ops:
  0.0 0.7 %copy-start.3 = (f32[64,32]{0,1:T(8,128)S(1)}, f32[64,32]{0,1:T(8,128)}, u32[]{:S(2)}) copy-start(f32[64,32]{0,1:T(8,128)} %param.13) | copy-start | bytes 24580
  0.7 0.8 %copy-start.10 = (s32[64]{0:T(128)S(1)}, s32[64]{0:T(128)}, u32[]{:S(2)}) copy-start(s32[64]{0:T(128)} %param.19) | copy-start | bytes 772
  0.7 0.8 %copy-start.11 = (s32[64,1]{0,1:T(1,128)S(1)}, s32[64,1]{0,1:T(1,128)}, u32[]{:S(2)}) copy-start(s32[64,1]{0,1:T(1,128)} %param.18) | copy-start | bytes 772
  0.7 0.8 %copy-start.12 = (s32[64]{0:T(128)S(1)}, s32[64]{0:T(128)}, u32[]{:S(2)}) copy-start(s32[64]{0:T(128)} %param.17) | copy-start | bytes 772
  0.7 8.5 %copy-start.1 = (s32[64,768]{1,0:T(8,128)S(1)}, s32[64,768]{1,0:T(8,128)}, u32[]{:S(2)}) copy-start(s32[64,768]{1,0:T(8,128)} %target_ref.1) | copy-start | bytes 589828
  0.8 8.7 %copy-start.2 = (f32[64,768]{1,0:T(8,128)S(1)}, f32[64,768]{1,0:T(8,128)}, u32[]{:S(2)}) copy-start(f32[64,768]{1,0:T(8,128)} %gain_ref.1) | copy-start | bytes 589828
  0.8 9.6 %copy-start.4 = (f32[64,64,32]{1,2,0:T(8,128)S(1)}, f32[64,64,32]{1,2,0:T(8,128)}, u32[]{:S(2)}) copy-start(f32[64,64,32]{1,2,0:T(8,128)} %param.16) | copy-start | bytes 1572868
  0.8 9.6 %copy-start.6 = (s32[32,768]{1,0:T(8,128)S(1)}, s32[32,768]{1,0:T(8,128)}, u32[]{:S(2)}) copy-start(s32[32,768]{1,0:T(8,128)} %inner_target_ref.1) | copy-start | bytes 294916
  0.8 9.6 %copy-start.7 = (f32[32,768]{1,0:T(8,128)S(1)}, f32[32,768]{1,0:T(8,128)}, u32[]{:S(2)}) copy-start(f32[32,768]{1,0:T(8,128)} %inner_gain_ref.1) | copy-start | bytes 294916
  0.8 9.5 %copy-start.8 = (f32[64,32]{0,1:T(8,128)S(1)}, f32[64,32]{0,1:T(8,128)}, u32[]{:S(2)}) copy-start(f32[64,32]{0,1:T(8,128)} %param.15) | copy-start | bytes 24580
  1.5 7.4 %copy-start = (s32[64,768]{1,0:T(8,128)S(1)}, s32[64,768]{1,0:T(8,128)}, u32[]{:S(2)}) copy-start(s32[64,768]{1,0:T(8,128)} %source_ref.1) | copy-start | bytes 589828
  1.6 8.2 %copy-start.9 = (f32[2,64,32]{1,2,0:T(8,128)S(1)}, f32[2,64,32]{1,2,0:T(8,128)}, u32[]{:S(2)}) copy-start(f32[2,64,32]{1,2,0:T(8,128)} %param.14) | copy-start | bytes 49156
  1.6 15.2 %all-to-all-start = ((bf16[32,16,128]{2,1,0:T(8,128)(2,1)}), bf16[32,16,128]{2,1,0:T(8,128)(2,1)S(1)}, u32[]{:S(2)}, u32[]{:S(2)}) async-start(bf16[32,16,128]{2,1,0:T(8,128)(2,1)} %bitcast.6), calls=%async_computation | async-start | bytes 262144 | tf_op jit(solution)/shard_map/all_to_all | solution.py:335
  8.9 1.4 %copy-start.5 = (s32[32,768]{1,0:T(8,128)S(1)}, s32[32,768]{1,0:T(8,128)}, u32[]{:S(2)}) copy-start(s32[32,768]{1,0:T(8,128)} %inner_source_ref.1) | copy-start | bytes 294916
  8.9 3.2 %collective-permute-start.2 = (s32[64,768]{1,0:T(8,128)S(1)}, s32[64,768]{1,0:T(8,128)S(1)}, u32[]{:S(2)}, u32[]{:S(2)}) collective-permute-start(s32[64,768]{1,0:T(8,128)S(1)} %copy-done), channel_id=1, source_target_pairs={{0,1},{1,0},{2,3},{3,2},{4,5},{5,4},{6,7},{7,6},{8,9},{9,8},{10,11... | collective-permute-start | bytes 589832 | tf_op jit(solution)/shard_map/ppermute | solution.py:360
  9.2 2.8 %collective-permute-start.3 = (s32[64,768]{1,0:T(8,128)S(1)}, s32[64,768]{1,0:T(8,128)S(1)}, u32[]{:S(2)}, u32[]{:S(2)}) collective-permute-start(s32[64,768]{1,0:T(8,128)S(1)} %copy-done.1), channel_id=1, source_target_pairs={{0,1},{1,0},{2,3},{3,2},{4,5},{5,4},{6,7},{7,6},{8,9},{9,8},{10,11... | collective-permute-start | bytes 589832 | tf_op jit(solution)/shard_map/ppermute | solution.py:360
  9.5 2.6 %collective-permute-start.4 = (f32[64,768]{1,0:T(8,128)S(1)}, f32[64,768]{1,0:T(8,128)S(1)}, u32[]{:S(2)}, u32[]{:S(2)}) collective-permute-start(f32[64,768]{1,0:T(8,128)S(1)} %copy-done.2), channel_id=1, source_target_pairs={{0,1},{1,0},{2,3},{3,2},{4,5},{5,4},{6,7},{7,6},{8,9},{9,8},{10,11... | collective-permute-start | bytes 589832 | tf_op jit(solution)/shard_map/ppermute | solution.py:360
  9.8 2.3 %collective-permute-start.1 = (f32[3,32,64]{2,1,0:T(8,128)S(1)}, f32[3,32,64]{2,1,0:T(8,128)S(1)}, u32[]{:S(2)}, u32[]{:S(2)}) collective-permute-start(f32[3,32,64]{2,1,0:T(8,128)S(1)} %pad_maximum_fusion.table_ref), channel_id=1, source_target_pairs={{0,1},{1,0},{2,3},{3,2},{4,5},{5,4},{6,7},{7,6},{8,9},{9,8},{10,11... | collective-permute-start | bytes 73736 | tf_op jit(solution)/shard_map/ppermute | solution.py:360
  10.1 2.0 %collective-permute-start = (s32[3,64]{1,0:T(4,128)S(1)}, s32[3,64]{1,0:T(4,128)S(1)}, u32[]{:S(2)}, u32[]{:S(2)}) collective-permute-start(s32[3,64]{1,0:T(4,128)S(1)} %pad_add_fusion.facts_ref), channel_id=1, source_target_pairs={{0,1},{1,0},{2,3},{3,2},{4,5},{5,4},{6,7},{7,6},{8,9},{9,8},{10,11... | collective-permute-start | bytes 2312 | tf_op jit(solution)/shard_map/ppermute | solution.py:360

commit v9 on v7

--- a/solution.py
+++ b/solution.py
@@ -274,7 +274,7 @@
             left.append(hot_rows(high, [weight.astype(BF16)]))
             right.append(hot_rows(low, [moved_ref[rows, lanes]]))
         product = dot(jnp.concatenate(left, axis=1), jnp.concatenate(right, axis=1), NT)
-        product_ref[held, :] = jnp.where(same, product, 0.0).astype(BF16)
+        product_ref[held, :] = jnp.where(same, product.astype(BF16), jnp.zeros((), BF16))
     shape = (rows_of, LANES)
     node = iota(shape, 1) - BS
     nodes = (node >= 0) & (node % DIGIT == iota(shape, 0) // group)
@@ -299,7 +299,7 @@
     step = iota(received.shape, 0) // (received.shape[0] // NEWTON)
     totals = []
     for t in range(NEWTON):
-        mine = jnp.where(step == t, received.astype(F32), 0.0).astype(BF16)
+        mine = jnp.where(step == t, received, jnp.zeros((), BF16))
         couple = dot(received, mine, TN)[BS:, :block_count]
         total = inner_ref[t * BS : (t + 1) * BS, :] + couple
         totals.append(jnp.concatenate([total] * parts, axis=1))

time: 28.8 us -> 28.8 us (level)
  no operation moved by 1% of the time
where the time goes in v9:
time: 28.8 us; the launch traced here: 28.5 us
  blocking collectives  9.33 us (32%)
  starting transfers between devices  8.64 us (30%)
  Pallas kernels  5.66 us (20%)
  waiting for transfers between devices  3.85 us (13%)
  other arithmetic  0.78 us (3%)
    all_to_all x1, blocking collectives, exchange(): lax.all_to_all(shaped, AXES[::-1], split_axis=0, concat_axis=0, tiled=True)  9.33 us
    all_to_all x1, starting transfers between devices, exchange(): lax.all_to_all(shaped, AXES[::-1], split_axis=0, concat_axis=0, tiled=True)  7.3 us
    pallas_call x5, Pallas kernels, call(): pl.pallas_call(kernel, out_shape=out_shape, in_specs=[spec] * len(args),...  5.66 us
    all_to_all x1, waiting for transfers between devices, exchange(): lax.all_to_all(shaped, AXES[::-1], split_axis=0, concat_axis=0, tiled=True)  3.84 us
    ppermute x5, starting transfers between devices, per_device(): swap = lambda array: lax.ppermute(array, 'sub', [(0, 1), (1, 0)])  1.34 us
    concatenate x1, other arithmetic, per_device(): jnp.concatenate([voltages.T[None], newton_steps.transpose(0, 2, 1)], axis=0)  0.77 us
  transfers between devices with their start and end apart: 6, of which 1 were waited for; matrix products, arithmetic and copies ran while one was open for 0% of the time, Pallas kernels for 9%

profile of v9, /device:TPU:0, one launch (start us, length us, event | category | flops | bytes accessed | tf_op | source)
XLA Modules:
  0.0 28.5 jit_solution(8803390833767113867)
XLA Ops:
  0.0 0.8 %pad_maximum_fusion.table_ref = f32[3,32,64]{2,1,0:T(8,128)S(1)} fusion(f32[2,32,64]{2,1,0:T(8,128)} %bitcast.19, f32[1,32,64]{2,1,0:T(8,128)} %bitcast.20), kind=kLoop, calls=%fused_computation | loop fusion | flops 6144 | bytes 49152 | tf_op jit(solution)/shard_map/concatenate | solution.py:360
  0.8 0.0 copy-start.8
  0.8 0.0 copy-start.9
  0.8 0.0 copy-start.10
  0.8 0.0 copy-start.1
  0.8 0.0 copy-start.2
  0.8 0.0 copy-start.3
  0.8 0.0 copy-start.4
  0.8 0.0 copy-start.5
  0.9 0.0 copy-start.6
  0.9 0.7 %shard_map.127 = bf16[512,128]{1,0:T(8,128)(2,1)} custom-call(f32[3,32,64]{2,1,0:T(8,128)S(1)} %pad_maximum_fusion.table_ref), custom_call_target="tpu_custom_call" | custom-call | flops 20000000000 | bytes 1000000 | tf_op jit(solution)/shard_map/pallas_call | solution.py:321
  1.6 0.0 copy-start
  1.6 0.0 copy-done.8
  1.6 0.0 copy-done.9
  1.6 0.0 copy-done.10
  1.6 0.0 copy-start.7
  1.6 7.3 %all-to-all-start = ((bf16[32,16,128]{2,1,0:T(8,128)(2,1)}), bf16[32,16,128]{2,1,0:T(8,128)(2,1)S(1)}, u32[]{:S(2)}, u32[]{:S(2)}) async-start(bf16[32,16,128]{2,1,0:T(8,128)(2,1)} %bitcast.6), calls=%async_computation | async-start | bytes 262144 | tf_op jit(solution)/shard_map/all_to_all | solution.py:334
  9.0 0.0 copy-done
  9.0 0.3 %collective-permute-start.2 = (s32[64,768]{1,0:T(8,128)S(1)}, s32[64,768]{1,0:T(8,128)S(1)}, u32[]{:S(2)}, u32[]{:S(2)}) collective-permute-start(s32[64,768]{1,0:T(8,128)S(1)} %copy-done), channel_id=1, source_target_pairs={{0,1},{1,0},{2,3},{3,2},{4,5},{5,4},{6,7},{7,6},{8,9},{9,8},{10,11... | collective-permute-start | bytes 589832 | tf_op jit(solution)/shard_map/ppermute | solution.py:359
  9.3 0.0 copy-done.1
  9.3 0.3 collective-permute-start.3
  9.5 0.0 copy-done.2
  9.6 0.3 collective-permute-start.4
  9.8 0.3 collective-permute-start.1
  10.1 0.3 collective-permute-start
  10.3 0.0 copy-done.3
  10.3 0.0 copy-done.4
  10.3 0.0 copy-done.5
  10.3 0.0 copy-done.6
  10.3 0.0 copy-done.7
  10.3 1.7 %shard_map.128 = (f32[128,32]{1,0:T(8,128)S(1)}, f32[16,64,128]{2,1,0:T(8,128)S(1)}) custom-call(f32[3,32,64]{2,1,0:T(8,128)S(1)} %pad_maximum_fusion.table_ref, f32[32,64]{1,0:T(8,128)S(1)} %bitcast.18, s32[32,768]{1,0:T(8,128)S(1)} %copy-done.4, s32[32,768]{1,0:T(8,128)S(1)} %copy-done.5, f32[32,768]{1,0:T(8,128)S(1)} %copy-done.6, f32[64,32,64]{2,1,0:T(8,128)S(1)} %bitcast.17), custom_call_target="tpu_custom_call" | custom-call | flops 1000000000 | bytes 1000000 | tf_op jit(solution)/shard_map/pallas_call | solution.py:321
  12.0 0.0 collective-permute-done.facts_other
  12.0 0.0 collective-permute-done.1.table_other
  12.0 0.0 collective-permute-done.2.source_other
  12.1 0.0 collective-permute-done.3.target_other
  12.1 0.0 collective-permute-done.4.gain_other
  12.1 1.0 %shard_map.129 = (bf16[128,768]{1,0:T(8,128)(2,1)S(1)}, f32[128,768]{1,0:T(8,128)S(1)}, f32[128,768]{1,0:T(8,128)S(1)}, bf16[128,768]{1,0:T(8,128)(2,1)S(1)}, bf...) custom-call(s32[3,64]{1,0:T(4,128)S(1)} %pad_add_fusion.facts_ref, ...), custom_call_target="tpu_custom_call" | custom-call | flops 100000000 | bytes 1000000 | tf_op jit(solution)/shard_map/pallas_call | solution.py:321
  13.0 3.8 %all-to-all-done = bf16[32,16,128]{2,1,0:T(8,128)(2,1)S(1)} async-done(((bf16[32,16,128]{2,1,0:T(8,128)(2,1)}), bf16[32,16,128]{2,1,0:T(8,128)(2,1)S(1)}, u32[]{:S(2)}, u32[]{:S(2)}) %all-to-all-start) | async-done | bytes 131104 | tf_op jit(solution)/shard_map/all_to_all | solution.py:334
  16.9 1.1 %shard_map.130 = bf16[256,128]{1,0:T(8,128)(2,1)S(1)} custom-call(bf16[512,128]{1,0:T(8,128)(2,1)S(1)} %bitcast.15, bf16[128,768]{1,0:T(8,128)(2,1)S(1)} %get-tuple-element.24.target_ref, f32[128,768]{1,0:T(8,128)S(1)} %get-tuple-element.25.gain_ref, f32[128,768]{1,0:T(8,128)S(1)} %get-tuple-element.26.near_ref, ...), custom_call_target="tpu_custom_call" | custom-call | flops 4000000000 | bytes 1000000 | tf_op jit(solution)/shard_map/pallas_call | solution.py:321
  18.0 9.3 %all_to_all.10 = bf16[32,8,128]{2,1,0:T(8,128)(2,1)S(1)} all-to-all(bf16[32,8,128]{2,1,0:T(8,128)(2,1)S(1)} %bitcast.16), channel_id=1, replica_groups=mesh['dom'=16,'sub'=2] {'sub','dom'}, dimensions={0} | all-to-all | bytes 131072 | tf_op jit(solution)/shard_map/all_to_all | solution.py:334
  27.3 1.2 %shard_map.131 = f32[2,32,64]{2,1,0:T(8,128)} custom-call(bf16[256,128]{1,0:T(8,128)(2,1)S(1)} %bitcast.14, f32[128,32]{1,0:T(8,128)S(1)} %get-tuple-element.31.inner_ref, f32[16,64,128]{2,1,0:T(8,128)S(1)} %get-tuple-element.32.packed_ref), custom_call_target="tpu_custom_call" | custom-call | flops 100000000 | bytes 1000000 | tf_op jit(solution)/shard_map/pallas_call | solution.py:321
  (1 shorter events, 0.0 us)
Async XLA Ops:
  0.8 0.8 %copy-start.8 = (s32[64]{0:T(128)S(1)}, s32[64]{0:T(128)}, u32[]{:S(2)}) copy-start(s32[64]{0:T(128)} %param.19) | copy-start | bytes 772
  0.8 0.8 %copy-start.9 = (s32[64,1]{0,1:T(1,128)S(1)}, s32[64,1]{0,1:T(1,128)}, u32[]{:S(2)}) copy-start(s32[64,1]{0,1:T(1,128)} %param.18) | copy-start | bytes 772
  0.8 0.8 %copy-start.10 = (s32[64]{0:T(128)S(1)}, s32[64]{0:T(128)}, u32[]{:S(2)}) copy-start(s32[64]{0:T(128)} %param.17) | copy-start | bytes 772
  0.8 8.5 %copy-start.1 = (s32[64,768]{1,0:T(8,128)S(1)}, s32[64,768]{1,0:T(8,128)}, u32[]{:S(2)}) copy-start(s32[64,768]{1,0:T(8,128)} %target_ref.1) | copy-start | bytes 589828
  0.8 8.7 %copy-start.2 = (f32[64,768]{1,0:T(8,128)S(1)}, f32[64,768]{1,0:T(8,128)}, u32[]{:S(2)}) copy-start(f32[64,768]{1,0:T(8,128)} %gain_ref.1) | copy-start | bytes 589828
  0.8 9.5 %copy-start.3 = (f32[64,64,32]{1,2,0:T(8,128)S(1)}, f32[64,64,32]{1,2,0:T(8,128)}, u32[]{:S(2)}) copy-start(f32[64,64,32]{1,2,0:T(8,128)} %param.16) | copy-start | bytes 1572868
  0.8 9.5 %copy-start.4 = (s32[32,768]{1,0:T(8,128)S(1)}, s32[32,768]{1,0:T(8,128)}, u32[]{:S(2)}) copy-start(s32[32,768]{1,0:T(8,128)} %inner_source_ref.1) | copy-start | bytes 294916
  0.8 9.5 %copy-start.5 = (s32[32,768]{1,0:T(8,128)S(1)}, s32[32,768]{1,0:T(8,128)}, u32[]{:S(2)}) copy-start(s32[32,768]{1,0:T(8,128)} %inner_target_ref.1) | copy-start | bytes 294916
  0.9 9.5 %copy-start.6 = (f32[32,768]{1,0:T(8,128)S(1)}, f32[32,768]{1,0:T(8,128)}, u32[]{:S(2)}) copy-start(f32[32,768]{1,0:T(8,128)} %inner_gain_ref.1) | copy-start | bytes 294916
  1.6 7.4 %copy-start = (s32[64,768]{1,0:T(8,128)S(1)}, s32[64,768]{1,0:T(8,128)}, u32[]{:S(2)}) copy-start(s32[64,768]{1,0:T(8,128)} %source_ref.1) | copy-start | bytes 589828
  1.6 8.7 %copy-start.7 = (f32[64,32]{0,1:T(8,128)S(1)}, f32[64,32]{0,1:T(8,128)}, u32[]{:S(2)}) copy-start(f32[64,32]{0,1:T(8,128)} %param.15) | copy-start | bytes 24580
  1.6 15.2 %all-to-all-start = ((bf16[32,16,128]{2,1,0:T(8,128)(2,1)}), bf16[32,16,128]{2,1,0:T(8,128)(2,1)S(1)}, u32[]{:S(2)}, u32[]{:S(2)}) async-start(bf16[32,16,128]{2,1,0:T(8,128)(2,1)} %bitcast.6), calls=%async_computation | async-start | bytes 262144 | tf_op jit(solution)/shard_map/all_to_all | solution.py:334
  9.0 3.1 %collective-permute-start.2 = (s32[64,768]{1,0:T(8,128)S(1)}, s32[64,768]{1,0:T(8,128)S(1)}, u32[]{:S(2)}, u32[]{:S(2)}) collective-permute-start(s32[64,768]{1,0:T(8,128)S(1)} %copy-done), channel_id=1, source_target_pairs={{0,1},{1,0},{2,3},{3,2},{4,5},{5,4},{6,7},{7,6},{8,9},{9,8},{10,11... | collective-permute-start | bytes 589832 | tf_op jit(solution)/shard_map/ppermute | solution.py:359
  9.3 2.8 %collective-permute-start.3 = (s32[64,768]{1,0:T(8,128)S(1)}, s32[64,768]{1,0:T(8,128)S(1)}, u32[]{:S(2)}, u32[]{:S(2)}) collective-permute-start(s32[64,768]{1,0:T(8,128)S(1)} %copy-done.1), channel_id=1, source_target_pairs={{0,1},{1,0},{2,3},{3,2},{4,5},{5,4},{6,7},{7,6},{8,9},{9,8},{10,11... | collective-permute-start | bytes 589832 | tf_op jit(solution)/shard_map/ppermute | solution.py:359
  9.6 2.5 %collective-permute-start.4 = (f32[64,768]{1,0:T(8,128)S(1)}, f32[64,768]{1,0:T(8,128)S(1)}, u32[]{:S(2)}, u32[]{:S(2)}) collective-permute-start(f32[64,768]{1,0:T(8,128)S(1)} %copy-done.2), channel_id=1, source_target_pairs={{0,1},{1,0},{2,3},{3,2},{4,5},{5,4},{6,7},{7,6},{8,9},{9,8},{10,11... | collective-permute-start | bytes 589832 | tf_op jit(solution)/shard_map/ppermute | solution.py:359
  9.8 2.2 %collective-permute-start.1 = (f32[3,32,64]{2,1,0:T(8,128)S(1)}, f32[3,32,64]{2,1,0:T(8,128)S(1)}, u32[]{:S(2)}, u32[]{:S(2)}) collective-permute-start(f32[3,32,64]{2,1,0:T(8,128)S(1)} %pad_maximum_fusion.table_ref), channel_id=1, source_target_pairs={{0,1},{1,0},{2,3},{3,2},{4,5},{5,4},{6,7},{7,6},{8,9},{9,8},{10,11... | collective-permute-start | bytes 73736 | tf_op jit(solution)/shard_map/ppermute | solution.py:359
  10.1 2.0 %collective-permute-start = (s32[3,64]{1,0:T(4,128)S(1)}, s32[3,64]{1,0:T(4,128)S(1)}, u32[]{:S(2)}, u32[]{:S(2)}) collective-permute-start(s32[3,64]{1,0:T(4,128)S(1)} %pad_add_fusion.facts_ref), channel_id=1, source_target_pairs={{0,1},{1,0},{2,3},{3,2},{4,5},{5,4},{6,7},{7,6},{8,9},{9,8},{10,11... | collective-permute-start | bytes 2312 | tf_op jit(solution)/shard_map/ppermute | solution.py:359
